TPU v7x, 256 devices: a whole 4x4x8 slice. The times are simulated.
256 devices in a mesh: lon: 64 (over z, x, core), lat: 4 (over y).
Axes of the slice: x: 4, y: 4, z: 8, core: 2. Of those that a mesh axis runs over, the one named last changes fastest.
Arguments:
- piece_height: float32 [4096, 128, 128], P('lon', 'lat')
- piece_weight: float32 [4096, 128, 128], P('lon', 'lat'), may hold values from 0.05 to 2
- piece_column: int32 [4096], P('lon'), may hold values from 0 to 262016, as said below
- piece_width: int32 [4096], P('lon'), may hold values from 64 to 128
Outputs:
- solution_field: float32 [128, 262144], P('lat', 'lon')
- residual: float32 [128, 262144], P('lat', 'lon')
Inputs may be any that keep to these rules, and one draw needn't show every extreme that they name: Every value is a multiple of 128 and a piece lies inside one tile of 4096 columns, tile piece_column // 4096. The pieces of one device name each tile at most 2 times; one tile is named exactly 2 times by the pieces of every device.
All inputs are finite; a program needn't handle non-finite values.
Results may differ from a plain program's by a relative error of at most 0.0007.
Values sent between devices are 32-bit elements; how exact they have to be, the bound alone decides.
No kernel may reach another device: no remote copies, remote signals or barrier semaphores. Data moves between devices by JAX's collectives and lax.ppermute only.
A program may use at most 128 MiB of HBM per device.

v0:
```python
import jax
import jax.numpy as jnp
from jax import lax
from jax.sharding import PartitionSpec as P

ROWS = 128
COLS_DEV = 4096
CAPACITY = 2
ITERS = 4


MU_DATA = 0.5
DAMPING = 0.5
RIDGE = 0.05
HIGHEST = lax.Precision.HIGHEST


def padded_2(block, sides, width):
    for axis, dim in sides:
        count = lax.axis_size(axis)
        forward = [(i, i + 1) for i in range(count - 1)]
        forward.append((count - 1, 0))
        backward = [(target, source) for source, target in forward]
        low = lax.ppermute(
            lax.slice_in_dim(block, block.shape[dim] - width, None, axis=dim), axis, forward
        )
        high = lax.ppermute(lax.slice_in_dim(block, 0, width, axis=dim), axis, backward)
        block = jnp.concatenate([low, block, high], axis=dim)
    return block


def passed_along(block, axis, distance):
    devices = range(lax.axis_size(axis))
    route = [(i - distance, i) for i in devices if i - distance in devices]
    return lax.ppermute(block, axis, route)


def piece_terms(height, weight, width, north_step, row_global):
    column = jnp.arange(height.shape[2], dtype=jnp.int32)
    valid_cell = column[None, None, :] < width[:, None, None]
    east_edge = column[None, None, :] + 1 < width[:, None, None]
    north_edge = valid_cell & (row_global[None, :, None] < ROWS - 1)
    east_step = jnp.concatenate(
        [height[:, :, 1:] - height[:, :, :-1], jnp.zeros_like(height[:, :, :1])], axis=2
    )
    cell_weight = jnp.where(valid_cell, weight, jnp.float32(0.0))
    east_weight = jnp.where(east_edge, weight, jnp.float32(0.0))
    north_weight = jnp.where(north_edge, weight, jnp.float32(0.0))
    return (
        cell_weight,
        cell_weight * height,
        east_weight,
        east_weight * east_step,
        north_weight,
        north_weight * north_step,
    )


def north_steps(height, next_first):
    inner = height[:, 1:, :] - height[:, :-1, :]
    return jnp.concatenate([inner, next_first - height[:, -1:, :]], axis=1)


def operate(field, diagonal, has_upper, has_lower):
    padded = padded_2(field, (("lon", 1), ("lat", 0)), 1)
    coupling = 2.0 * field - padded[1:-1, :-2] - padded[1:-1, 2:]
    coupling = coupling + jnp.where(has_upper, field - padded[2:, 1:-1], jnp.float32(0.0))
    coupling = coupling + jnp.where(has_lower, field - padded[:-2, 1:-1], jnp.float32(0.0))
    return diagonal * field + coupling


def squares(residual):
    return lax.psum(jnp.sum(residual * residual), ("lon", "lat"))


def body(piece_height, piece_weight, piece_column, piece_width):
    pieces, rows_dev, block_width = piece_height.shape
    lon_count = lax.axis_size("lon")
    slot_count = lon_count * CAPACITY
    tile_blocks = COLS_DEV // block_width
    flat_size = rows_dev * block_width
    row_global = lax.axis_index("lat") * rows_dev + jnp.arange(rows_dev, dtype=jnp.int32)
    target_tile = piece_column // COLS_DEV
    tile_block = piece_column % COLS_DEV // block_width
    order_ids = jnp.arange(pieces, dtype=jnp.int32)
    same_tile = target_tile[:, None] == target_tile[None, :]
    earlier = order_ids[None, :] < order_ids[:, None]
    rank_in_tile = jnp.sum((same_tile & earlier).astype(jnp.int32), axis=1)
    slot_of_piece = target_tile * CAPACITY + rank_in_tile
    placing = jnp.arange(slot_count, dtype=jnp.int32)[:, None] == slot_of_piece[None, :]
    place_float = placing.astype(jnp.float32)
    place_int = placing.astype(jnp.int32)

    def place(values):
        moved = jnp.dot(place_float, values.reshape(pieces, flat_size), precision=HIGHEST)
        return moved.reshape(slot_count, rows_dev, block_width)

    sent_height = place(piece_height)
    sent_weight = place(piece_weight)
    sent_block = jnp.sum(place_int * tile_block[None, :], axis=1).astype(jnp.float32)
    sent_width = jnp.sum(place_int * piece_width[None, :], axis=1).astype(jnp.float32)
    next_first = passed_along(piece_height[:, :1, :], "lat", -1)
    sent_north = place(north_steps(piece_height, next_first))
    got_height, got_weight, got_north, got_block_f, got_width_f = (
        lax.all_to_all(sent_height, "lon", split_axis=0, concat_axis=0, tiled=True),
        lax.all_to_all(sent_weight, "lon", split_axis=0, concat_axis=0, tiled=True),
        lax.all_to_all(sent_north, "lon", split_axis=0, concat_axis=0, tiled=True),
        lax.all_to_all(sent_block, "lon", split_axis=0, concat_axis=0, tiled=True),
        lax.all_to_all(sent_width, "lon", split_axis=0, concat_axis=0, tiled=True),
    )
    got_block = got_block_f.astype(jnp.int32)
    got_width = got_width_f.astype(jnp.int32)
    terms = piece_terms(got_height, got_weight, got_width, got_north, row_global)
    stacked = jnp.stack(terms, axis=1)
    block_hot = (got_block[:, None] == jnp.arange(tile_blocks, dtype=jnp.int32)[None, :]).astype(
        jnp.float32
    )
    fields = jnp.einsum("sb,sqrj->qrbj", block_hot, stacked, precision=HIGHEST).reshape(
        6, rows_dev, COLS_DEV
    )
    weight_sum, height_sum, east_weight_sum, east_sum, north_weight_sum, north_sum = (
        fields[0],
        fields[1],
        fields[2],
        fields[3],
        fields[4],
        fields[5],
    )
    target_east = east_sum / (east_weight_sum + DAMPING)
    target_north = north_sum / (north_weight_sum + DAMPING)
    south_row = passed_along(target_north[-1:, :], "lat", 1)
    west_east = jnp.concatenate([jnp.zeros_like(target_east[:, :1]), target_east[:, :-1]], axis=1)
    south_target = jnp.concatenate([south_row, target_north[:-1]], axis=0)
    right_side = MU_DATA * height_sum - (target_east - west_east) - (target_north - south_target)
    diagonal = MU_DATA * weight_sum + RIDGE
    has_upper = (row_global < ROWS - 1)[:, None]
    has_lower = (row_global > 0)[:, None]
    solution_field = jnp.zeros_like(right_side)
    residual = right_side
    direction = right_side
    norm_now = squares(residual)
    for iteration in range(ITERS):
        image = operate(direction, diagonal, has_upper, has_lower)
        curvature = lax.psum(jnp.sum(direction * image), ("lon", "lat"))
        alpha = norm_now / curvature
        solution_field = solution_field + alpha * direction
        residual = residual - alpha * image
        norm_next = squares(residual)
        direction = residual + norm_next / norm_now * direction
        norm_now = norm_next
    return (solution_field, residual)


def solution(mesh):
    return jax.shard_map(
        body,
        mesh=mesh,
        in_specs=(P("lon", "lat", None), P("lon", "lat", None), P("lon"), P("lon")),
        out_specs=(P("lat", "lon"), P("lat", "lon")),
        check_vma=False,
    )
```

profile of v0, /device:TPU:1, one launch (start us, length us, event | category | flops | bytes accessed | tf_op | source)
XLA Modules:
  0.0 841.2 jit_solution(11415089841136239433)
XLA Ops:
  3.0 13.0 %all-to-all-start = ((f32[64,2,1]{1,2,0:T(1,128)}), f32[64,2,1]{1,2,0:T(1,128)S(1)}, u32[]{:S(2)}, u32[]{:S(2)}) async-start(f32[64,2,1]{1,2,0:T(1,128)} %bitcast), calls=%async_computation | async-start | bytes 65536 | tf_op jit(solution)/shard_map/all_to_all | solution.py:109
  16.8 8.5 %all-to-all-done = f32[64,2,1]{1,2,0:T(1,128)S(1)} async-done(((f32[64,2,1]{1,2,0:T(1,128)}), f32[64,2,1]{1,2,0:T(1,128)S(1)}, u32[]{:S(2)}, u32[]{:S(2)}) %all-to-all-start) | async-done | bytes 544 | tf_op jit(solution)/shard_map/all_to_all | solution.py:109
  25.3 4.7 all-to-all-start.4
  30.0 2.9 fusion.6
  35.4 4.0 all-to-all-done.4
  39.4 6.5 all-to-all-start.1
  50.3 45.4 %all-to-all-done.1 = f32[128,32,128]{2,1,0:T(8,128)S(1)} async-done(((f32[128,32,128]{2,1,0:T(8,128)}), f32[128,32,128]{2,1,0:T(8,128)S(1)}, u32[]{:S(2)}, u32[]{:S(2)}) %all-to-all-start.1) | async-done | bytes 2097184 | tf_op jit(solution)/shard_map/all_to_all | solution.py:106
  95.7 7.2 all-to-all-start.2
  104.6 3.3 collective-permute-done
  112.4 40.0 %all-to-all-done.2 = f32[128,32,128]{2,1,0:T(8,128)} async-done(((f32[128,32,128]{2,1,0:T(8,128)}), f32[128,32,128]{2,1,0:T(8,128)}, u32[]{:S(2)}, u32[]{:S(2)}) %all-to-all-start.2) | async-done | bytes 2097184 | tf_op jit(solution)/shard_map/all_to_all | solution.py:105
  152.5 7.2 all-to-all-start.3
  160.3 2.8 copy.30
  163.7 2.7 bitcast_dynamic-update-slice_fusion.5
  166.4 5.3 bitcast_dynamic-update-slice_fusion.4
  174.4 2.8 bitcast_dynamic-update-slice_fusion.2
  177.2 2.7 bitcast_dynamic-update-slice_fusion.1
  180.0 29.3 %all-to-all-done.3 = f32[128,32,128]{2,1,0:T(8,128)} async-done(((f32[128,32,128]{2,1,0:T(8,128)}), f32[128,32,128]{2,1,0:T(8,128)}, u32[]{:S(2)}, u32[]{:S(2)}) %all-to-all-start.3) | async-done | bytes 2097184 | tf_op jit(solution)/shard_map/all_to_all | solution.py:107
  209.3 14.2 %bitcast_dynamic-update-slice_fusion = f32[128,6,32,128]{3,0,2,1:T(8,128)} fusion(f32[128,6,32,128]{3,0,2,1:T(8,128)} %bitcast_dynamic-update-slice_fusion.1, f32[128,32,128]{2,1,0:T(8,128)} %all-to-all-done.3, f32[128,32,128]{2,1,0:T(8,128)S(1)} %all-to-all-done.1, pred[128,128]{1,0:T(8,128)(4,1)S(1)} %get-tuple-element.40, pred[32]{0:T(512)(128)(4,1)S(1)} %fusion.61), kind=kLoop, calls=%fused_computation.1 | loop fusion | flops 1572864 | bytes 6307872 | tf_op jit(solution)/shard_map/stack | solution.py:114
  223.4 7.6 convolution_bitcast_fusion
  231.4 3.2 collective-permute-start.1
  236.9 4.1 collective-permute-start.2
  244.8 3.5 collective-permute-start.4
  249.2 2.9 collective-permute-done.5
  253.4 77.0 %all-reduce.2 = (f32[]{:T(128)}, f32[]{:T(128)}) all-reduce(f32[]{:T(128)} %get-tuple-element.3, f32[]{:T(128)} %get-tuple-element.2), channel_id=1, replica_groups=mesh['lon'=64,'lat'=4] {'lon','lat'}, use_global_device_ids=true, to_apply=%region_4.5 | all-reduce | flops 2 | bytes 16 | tf_op jit(solution)/shard_map/psum | solution.py:73
  332.5 73.5 %psum.58 = f32[]{:T(128)} all-reduce(f32[]{:T(128)} %multiply_reduce_fusion.5), channel_id=1, replica_groups=mesh['lon'=64,'lat'=4] {'lon','lat'}, use_global_device_ids=true, to_apply=%region_8.9 | all-reduce | flops 1 | bytes 8 | tf_op jit(solution)/shard_map/psum | solution.py:73
  418.7 78.9 %psum.59 = f32[]{:T(128)} all-reduce(f32[]{:T(128)} %get-tuple-element.16), channel_id=1, replica_groups=mesh['lon'=64,'lat'=4] {'lon','lat'}, use_global_device_ids=true, to_apply=%region_10.11 | all-reduce | flops 1 | bytes 8 | tf_op jit(solution)/shard_map/psum | solution.py:144
  499.7 73.5 %psum.60 = f32[]{:T(128)} all-reduce(f32[]{:T(128)} %get-tuple-element.14), channel_id=1, replica_groups=mesh['lon'=64,'lat'=4] {'lon','lat'}, use_global_device_ids=true, to_apply=%region_12.13 | all-reduce | flops 1 | bytes 8 | tf_op jit(solution)/shard_map/psum | solution.py:73
  586.6 78.9 %psum.61 = f32[]{:T(128)} all-reduce(f32[]{:T(128)} %get-tuple-element.12), channel_id=1, replica_groups=mesh['lon'=64,'lat'=4] {'lon','lat'}, use_global_device_ids=true, to_apply=%region_14.15 | all-reduce | flops 1 | bytes 8 | tf_op jit(solution)/shard_map/psum | solution.py:144
  668.6 73.5 %psum.62 = f32[]{:T(128)} all-reduce(f32[]{:T(128)} %get-tuple-element.10), channel_id=1, replica_groups=mesh['lon'=64,'lat'=4] {'lon','lat'}, use_global_device_ids=true, to_apply=%region_16.17 | all-reduce | flops 1 | bytes 8 | tf_op jit(solution)/shard_map/psum | solution.py:73
  746.0 2.8 collective-permute-done.15
  755.1 3.3 multiply_reduce_fusion
  758.4 78.9 %psum.63 = f32[]{:T(128)} all-reduce(f32[]{:T(128)} %get-tuple-element.8), channel_id=1, replica_groups=mesh['lon'=64,'lat'=4] {'lon','lat'}, use_global_device_ids=true, to_apply=%region_18.19 | all-reduce | flops 1 | bytes 8 | tf_op jit(solution)/shard_map/psum | solution.py:144
  (88 shorter events, 66.4 us)
Async XLA Ops:
  3.0 22.3 %all-to-all-start = ((f32[64,2,1]{1,2,0:T(1,128)}), f32[64,2,1]{1,2,0:T(1,128)S(1)}, u32[]{:S(2)}, u32[]{:S(2)}) async-start(f32[64,2,1]{1,2,0:T(1,128)} %bitcast), calls=%async_computation | async-start | bytes 65536 | tf_op jit(solution)/shard_map/all_to_all | solution.py:109
  25.3 14.1 %all-to-all-start.4 = ((f32[64,2,1]{1,2,0:T(1,128)}), f32[64,2,1]{1,2,0:T(1,128)S(1)}, u32[]{:S(2)}, u32[]{:S(2)}) async-start(f32[64,2,1]{1,2,0:T(1,128)} %bitcast.11), calls=%async_computation.4 | async-start | bytes 65536 | tf_op jit(solution)/shard_map/all_to_all | solution.py:108
  35.4 10.6 %copy-start = (f32[64,32,128]{2,1,0:T(8,128)S(1)}, f32[64,32,128]{2,1,0:T(8,128)}, u32[]{:S(2)}) copy-start(f32[64,32,128]{2,1,0:T(8,128)} %param.4) | copy-start | bytes 3145732
  39.4 56.2 %all-to-all-start.1 = ((f32[128,32,128]{2,1,0:T(8,128)}), f32[128,32,128]{2,1,0:T(8,128)S(1)}, u32[]{:S(2)}, u32[]{:S(2)}) async-start(f32[128,32,128]{2,1,0:T(8,128)} %copy.26), calls=%async_computation.1 | async-start | bytes 4194304 | tf_op jit(solution)/shard_map/all_to_all | solution.py:106
  95.7 56.8 %all-to-all-start.2 = ((f32[128,32,128]{2,1,0:T(8,128)}), f32[128,32,128]{2,1,0:T(8,128)}, u32[]{:S(2)}, u32[]{:S(2)}) async-start(f32[128,32,128]{2,1,0:T(8,128)} %copy.29), calls=%async_computation.2 | async-start | bytes 4194304 | tf_op jit(solution)/shard_map/all_to_all | solution.py:105
  102.9 5.1 collective-permute-start
  152.5 56.8 %all-to-all-start.3 = ((f32[128,32,128]{2,1,0:T(8,128)}), f32[128,32,128]{2,1,0:T(8,128)}, u32[]{:S(2)}, u32[]{:S(2)}) async-start(f32[128,32,128]{2,1,0:T(8,128)} %copy.36), calls=%async_computation.3 | async-start | bytes 4194304 | tf_op jit(solution)/shard_map/all_to_all | solution.py:107
  231.4 4.1 collective-permute-start.1
  236.9 5.0 collective-permute-start.2
  241.0 3.5 collective-permute-start.3
  244.8 4.4 collective-permute-start.4
  248.3 3.8 collective-permute-start.5
  407.5 2.7 collective-permute-start.6
  409.3 3.2 collective-permute-start.7
  412.8 2.7 collective-permute-start.8
  413.6 3.8 collective-permute-start.9
  574.7 2.5 collective-permute-start.10
  576.3 3.2 collective-permute-start.11
  579.8 2.7 collective-permute-start.12
  580.6 3.8 collective-permute-start.13
  743.5 2.5 collective-permute-start.14
  745.1 3.7 collective-permute-start.15
  750.8 2.7 collective-permute-start.16
  751.3 3.8 collective-permute-start.17
where the time goes:
time: 850 us; the launch traced here: 841 us
  blocking collectives  534 us (63%)
  waiting for transfers between devices  157 us (18%)
  starting transfers between devices  61 us (7%)
  other arithmetic  48.7 us (6%)
  local copies, waits for them, and re-layouts  16.3 us (2%)
  matrix products  13.9 us (2%)
  between operations  10.6 us (1%)
    psum x4, blocking collectives, squares(): return lax.psum(jnp.sum(residual * residual), ('lon', 'lat'))  297 us
    psum x3, blocking collectives, body(): curvature = lax.psum(jnp.sum(direction * image), ('lon', 'lat'))  237 us
    all_to_all x1, waiting for transfers between devices, body(): lax.all_to_all(sent_weight, 'lon', split_axis=0, concat_axis=0, tiled=True)  45.4 us
    all_to_all x1, waiting for transfers between devices, body(): lax.all_to_all(sent_height, 'lon', split_axis=0, concat_axis=0, tiled=True)  40 us
    all_to_all x1, waiting for transfers between devices, body(): lax.all_to_all(sent_north, 'lon', split_axis=0, concat_axis=0, tiled=True)  29.3 us
  transfers between devices with their start and end apart: 23, of which 23 were waited for; matrix products, arithmetic and copies ran while one was open for 4% of the time, Pallas kernels for 0%

commit v1 on v0

v1 whole, which is shorter than its diff:
```python
import jax
import jax.numpy as jnp
from jax import lax
from jax.experimental import pallas as pl
from jax.experimental.pallas import tpu as pltpu
from jax.sharding import PartitionSpec as P

ROWS = 128
COLS_DEV = 4096
BW = 128
BLOCKS = COLS_DEV // BW
CAPACITY = 2

MU_DATA = 0.5
DAMPING = 0.5
RIDGE = 0.05
HIGHEST = lax.Precision.HIGHEST

MID = 5.5
HALF = 5.5
VMEM_BYTES = 40 * 1024 * 1024
F32 = jnp.float32


def passed_along(block, axis, distance):
    devices = range(lax.axis_size(axis))
    route = [(i, i + distance) for i in devices if i + distance in devices]
    return lax.ppermute(block, axis, route)


def passed_around(block, axis, distance):
    count = lax.axis_size(axis)
    return lax.ppermute(block, axis, [(i, (i + distance) % count) for i in range(count)])


def pack_kernel(column_ref, height_ref, weight_ref, out_ref, count_ref):
    tiles, pieces = out_ref.shape[0], height_ref.shape[0]

    @pl.loop(0, tiles)
    def _(t):
        count_ref[t] = 0

    @pl.loop(0, pieces, unroll=4)
    def _(p):
        tile = column_ref[p] // COLS_DEV
        slot = count_ref[tile]
        count_ref[tile] = slot + 1
        out_ref[tile, 2 * slot] = height_ref[p]
        out_ref[tile, 2 * slot + 1] = weight_ref[p]


def pack(piece_column, piece_height, piece_weight, tiles):
    rows = piece_height.shape[1]
    return pl.pallas_call(
        pack_kernel,
        out_shape=jax.ShapeDtypeStruct((tiles, 2 * CAPACITY, rows, BW), F32),
        in_specs=[
            pl.BlockSpec(memory_space=pltpu.SMEM),
            pl.BlockSpec(memory_space=pltpu.VMEM),
            pl.BlockSpec(memory_space=pltpu.VMEM),
        ],
        out_specs=pl.BlockSpec(memory_space=pltpu.VMEM),
        scratch_shapes=[pltpu.SMEM((tiles,), jnp.int32)],
        compiler_params=pltpu.CompilerParams(vmem_limit_bytes=VMEM_BYTES),
        name="pack",
    )(piece_column, piece_height, piece_weight)


def small_messages(piece_height, piece_column, piece_width, lon):
    pieces = piece_column.shape[0]
    lon_count = lax.axis_size("lon")
    tile = piece_column // COLS_DEV
    block = piece_column % COLS_DEV // BW
    ids = jnp.arange(pieces, dtype=jnp.int32)
    same = (tile[:, None] == tile[None, :]) & (ids[None, :] < ids[:, None])
    rank = jnp.sum(same.astype(jnp.int32), axis=1)
    place = (tile ^ lon) * CAPACITY + rank
    hot = jnp.arange(lon_count * CAPACITY, dtype=jnp.int32)[:, None] == place[None, :]
    hot_int = hot.astype(jnp.int32)
    block_of = jnp.sum(hot_int * (block + 1)[None, :], axis=1).reshape(lon_count, CAPACITY)
    width_of = jnp.sum(hot_int * piece_width[None, :], axis=1).reshape(lon_count, CAPACITY)
    next_first = passed_along(piece_height[:, 0, :], "lat", -1)
    first = jnp.dot(hot.astype(F32), next_first, precision=HIGHEST)
    facts = jnp.concatenate([block_of, width_of], axis=1).astype(F32)
    facts = jnp.pad(facts, ((0, 0), (0, BW - 2 * CAPACITY)))[:, None, :]
    first = first.reshape(lon_count, CAPACITY, BW)
    return jnp.concatenate([first, facts, jnp.zeros_like(facts)], axis=1)


def exchanged(message, lon_count):
    shape = message.shape
    bit = 1
    while bit < lon_count:
        split = message.reshape((lon_count // (2 * bit), 2, bit) + shape[1:])
        moved = lax.ppermute(split[:, 1], "lon", [(i, i ^ bit) for i in range(lon_count)])
        message = jnp.stack([split[:, 0], moved], axis=1).reshape(shape)
        bit *= 2
    return message


def sums_kernel(place_ref, facts_ref, got_ref, first_ref, rhs_ref, diag_ref, up_ref, down_ref,
                edge_ref, total_ref):
    step, steps = pl.program_id(0), pl.num_programs(0)
    sources, _, rows, _ = got_ref.shape
    lon, lat, lat_count = place_ref[0], place_ref[1], place_ref[2]
    lane = lax.broadcasted_iota(jnp.int32, (rows, BW), 1)
    row = lax.broadcasted_iota(jnp.int32, (rows, BW), 0)

    @pl.when(step == 0)
    def _():
        total_ref[...] = jnp.zeros_like(total_ref)

    for s in range(sources):
        entry = (step * sources + s) ^ lon
        for slot in range(CAPACITY):
            block = facts_ref[entry * 2 * CAPACITY + slot] - 1
            width = facts_ref[entry * 2 * CAPACITY + CAPACITY + slot]

            @pl.when(block >= 0)
            def _(s=s, slot=slot, block=block, width=width, entry=entry):
                height = got_ref[s, 2 * slot]
                weight = got_ref[s, 2 * slot + 1]
                above = first_ref[entry, pl.ds(slot, 1), :]
                cell = jnp.where(lane < width, weight, 0.0)
                east = jnp.where(lane + 1 < width, weight, 0.0)
                east_step = pltpu.roll(height, BW - 1, 1) - height
                raised = jnp.where(row == rows - 1, above, pltpu.roll(height, rows - 1, 0))
                total_ref[block, 0] += cell
                total_ref[block, 1] += cell * height
                total_ref[block, 2] += east
                total_ref[block, 3] += east * east_step
                total_ref[block, 4] += cell * (raised - height)

    @pl.when(step == steps - 1)
    def _():
        last = (row == rows - 1) & (lat == lat_count - 1)
        first = (row == 0) & (lat == 0)
        sides = 4.0 - last.astype(F32) - first.astype(F32) + RIDGE
        row8 = row[:8]

        @pl.loop(0, BLOCKS)
        def _(i):
            cell, height = total_ref[i, 0], total_ref[i, 1]
            east = total_ref[i, 3] / (total_ref[i, 2] + DAMPING)
            north = jnp.where(last, 0.0, total_ref[i, 4] / (cell + DAMPING))
            south = jnp.where(row == 0, 0.0, pltpu.roll(north, 1, 0))
            rhs = MU_DATA * height - (east - pltpu.roll(east, 1, 1)) - (north - south)
            diag = MU_DATA * cell + sides
            rhs_ref[i] = rhs
            diag_ref[i] = diag
            top = pltpu.roll(diag[rows - 8:], 4, 0)
            top = jnp.where(row8 == 0, pltpu.roll(north[rows - 8:], 1, 0), top)
            up_ref[i] = jnp.where(row8 >= 4, rhs[rows - 8:], top)
            down_ref[i] = jnp.where(row8 >= 4, pltpu.roll(diag[:8], 4, 0), rhs[:8])

        for side, block in ((0, 0), (1, BLOCKS - 1)):
            edge_ref[side, 0:rows] = rhs_ref[block]
            edge_ref[side, rows:2 * rows] = diag_ref[block]
            edge_ref[side, 2 * rows:2 * rows + 8] = up_ref[block]


def sums(place, facts, got, first, batch=8):
    tiles, arrays, rows, _ = got.shape
    whole = lambda *shape: pl.BlockSpec(shape, lambda i: (0,) * len(shape))
    field = (BLOCKS, rows, BW)
    strip = (BLOCKS, 8, BW)
    edge = (2, 2 * rows + 8, BW)
    return pl.pallas_call(
        sums_kernel,
        grid=(tiles // batch,),
        out_shape=[jax.ShapeDtypeStruct(s, F32) for s in (field, field, strip, strip, edge)],
        in_specs=[
            pl.BlockSpec(memory_space=pltpu.SMEM),
            pl.BlockSpec(memory_space=pltpu.SMEM),
            pl.BlockSpec((batch, arrays, rows, BW), lambda i: (i, 0, 0, 0)),
            whole(*first.shape),
        ],
        out_specs=[whole(*s) for s in (field, field, strip, strip, edge)],
        scratch_shapes=[pltpu.VMEM((BLOCKS, 5, rows, BW), F32)],
        compiler_params=pltpu.CompilerParams(vmem_limit_bytes=VMEM_BYTES),
        name="sums",
    )(place, facts, got, first)


PAIRS = [(i, j) for j in range(5) for i in range(min(j, 3) + 1)]


def basis_kernel(place_ref, rhs_ref, diag_ref, up_ref, south_ref, north_ref, west_ref, east_ref,
                 q_ref, gram_ref, scale_ref, v_ref):
    rows = rhs_ref.shape[1]
    tall = rows + 16
    lat, lat_count = place_ref[1], place_ref[2]
    row = lax.broadcasted_iota(jnp.int32, (rows, BW), 0)
    row8 = row[:8]
    row_all = lax.broadcasted_iota(jnp.int32, (tall, BW), 0)
    lane = lax.broadcasted_iota(jnp.int32, (tall, BW), 1)
    inside = ((row_all >= 8) | (lat > 0)) & ((row_all < rows + 8) | (lat < lat_count - 1))

    def assemble(i, rhs, diag, up, south, north):
        first = jnp.where(row == 0, south[0:1], 0.0) + rhs
        below = jnp.where(row8 >= 4, south, 0.0)
        above = jnp.where(row8 == 0, north + up, jnp.where(row8 < 4, north, 0.0))
        v_ref[0, i] = jnp.concatenate([below, first, above], axis=0)
        diag = jnp.concatenate([pltpu.roll(south, 4, 0), diag, pltpu.roll(north, 4, 0)], axis=0)
        scale_ref[i] = (diag - MID) * (2.0 / HALF)

    for i, ref in ((0, west_ref), (BLOCKS + 1, east_ref)):
        two = 2 * rows
        assemble(i, ref[0:rows], ref[rows:two], ref[two:two + 8], ref[two + 8:two + 16],
                 ref[two + 16:two + 24])

    @pl.loop(0, BLOCKS)
    def _(i):
        assemble(i + 1, rhs_ref[i], diag_ref[i], up_ref[i], south_ref[i], north_ref[i])

    def applied(k, i):
        v = v_ref[k, i]
        left = v_ref[k, jnp.maximum(i - 1, 0)]
        right = v_ref[k, jnp.minimum(i + 1, BLOCKS + 1)]
        west = pltpu.roll(jnp.where(lane == BW - 1, left, v), 1, 1)
        east = pltpu.roll(jnp.where(lane == 0, right, v), BW - 1, 1)
        south = pltpu.roll(v, 1, 0)
        north = pltpu.roll(v, tall - 1, 0)
        image = scale_ref[i] * v - (2.0 / HALF) * ((west + east) + (south + north))
        if k == 0:
            image = 0.5 * image
        else:
            image = image - v_ref[k - 1, i]
        return jnp.where(inside, image, 0.0)

    for k in range(3):
        @pl.loop(0, BLOCKS + 2)
        def _(i, k=k):
            v_ref[k + 1, i] = applied(k, i)

    def products(i, carry):
        last = applied(3, i + 1)[8:8 + rows]
        q = [v_ref[k, i + 1, 8:8 + rows] for k in range(4)] + [last]
        for k in range(5):
            q_ref[k, i] = q[k]
        out = []
        for total, (a, b) in zip(carry, PAIRS):
            term = q[a] * q[b]
            out.append(total + sum(term[8 * n:8 * n + 8] for n in range(rows // 8)))
        return tuple(out)

    zero = tuple(jnp.zeros((8, BW), F32) for _ in PAIRS)
    totals = lax.fori_loop(0, BLOCKS, products, zero)
    lane1 = lax.broadcasted_iota(jnp.int32, (1, BW), 1)
    gram = jnp.zeros((1, BW), F32)
    for n, total in enumerate(totals):
        value = jnp.sum(jnp.sum(total, axis=0, keepdims=True), axis=1, keepdims=True)
        gram = jnp.where(lane1 == n, value, gram)
    gram_ref[...] = gram


def basis(place, rhs, diag, up, south, north, west, east):
    rows = rhs.shape[1]
    vmem = pl.BlockSpec(memory_space=pltpu.VMEM)
    return pl.pallas_call(
        basis_kernel,
        out_shape=[
            jax.ShapeDtypeStruct((5, BLOCKS, rows, BW), F32),
            jax.ShapeDtypeStruct((1, BW), F32),
        ],
        in_specs=[pl.BlockSpec(memory_space=pltpu.SMEM)] + [vmem] * 7,
        out_specs=[vmem, vmem],
        scratch_shapes=[
            pltpu.VMEM((BLOCKS + 2, rows + 16, BW), F32),
            pltpu.VMEM((4, BLOCKS + 2, rows + 16, BW), F32),
        ],
        compiler_params=pltpu.CompilerParams(vmem_limit_bytes=VMEM_BYTES),
        name="basis",
    )(place, rhs, diag, up, south, north, west, east)


def solved(gram):
    g = {}
    for n, (a, b) in enumerate(PAIRS):
        g[a, b] = g[b, a] = gram[n]
    m = [[None] * 4 for _ in range(4)]
    for j in range(4):
        for i in range(j + 1):
            if j == 0:
                value = MID * g[i, 0] + HALF * g[i, 1]
            else:
                value = MID * g[i, j] + (0.5 * HALF) * (g[i, j + 1] + g[i, j - 1])
            m[i][j] = m[j][i] = value
    y = [g[0, i] for i in range(4)]
    inverse = []
    factor = [[None] * 4 for _ in range(4)]
    for k in range(4):
        pivot = m[k][k]
        inverse.append(jnp.where(pivot > 0.0, 1.0 / jnp.where(pivot > 0.0, pivot, 1.0), 0.0))
        for i in range(k + 1, 4):
            factor[i][k] = m[k][i] * inverse[k]
        for i in range(k + 1, 4):
            for j in range(i, 4):
                m[i][j] = m[i][j] - factor[i][k] * m[k][j]
            y[i] = y[i] - factor[i][k] * y[k]
    c = [y[k] * inverse[k] for k in range(4)]
    for k in range(3, -1, -1):
        for i in range(k):
            c[i] = c[i] - factor[k][i] * c[k]
    half = 0.5 * HALF
    r = [
        1.0 - (MID * c[0] + half * c[1]),
        -(HALF * c[0] + MID * c[1] + half * c[2]),
        -(half * c[1] + MID * c[2] + half * c[3]),
        -(half * c[2] + MID * c[3]),
        -(half * c[3]),
    ]
    return c, r


def combine_kernel(gram_ref, q_ref, x_ref, r_ref, c_ref):
    @pl.when(pl.program_id(0) == 0)
    def _():
        gram = jnp.sum(gram_ref[...], axis=0, keepdims=True)
        lane = lax.broadcasted_iota(jnp.int32, (1, BW), 1)
        pick = lambda n: jnp.sum(jnp.where(lane == n, gram, 0.0), axis=1, keepdims=True)
        c, r = solved([pick(n) for n in range(len(PAIRS))])
        for n, value in enumerate(c + r):
            c_ref[n] = jnp.broadcast_to(value, (8, BW))

    rows = q_ref.shape[2]
    factors = [jnp.concatenate([c_ref[n]] * (rows // 8), axis=0) for n in range(9)]
    for i in range(q_ref.shape[1]):
        q = [q_ref[k, i] for k in range(5)]
        columns = slice(i * BW, (i + 1) * BW)
        x_ref[:, columns] = sum(factors[k] * q[k] for k in range(4))
        r_ref[:, columns] = sum(factors[4 + k] * q[k] for k in range(5))


def combine(gram, q, batch=8):
    _, blocks, rows, _ = q.shape
    out = jax.ShapeDtypeStruct((rows, blocks * BW), F32)
    spec = pl.BlockSpec((rows, batch * BW), lambda i: (0, i))
    return pl.pallas_call(
        combine_kernel,
        grid=(blocks // batch,),
        out_shape=[out, out],
        in_specs=[
            pl.BlockSpec(gram.shape, lambda i: (0, 0)),
            pl.BlockSpec((5, batch, rows, BW), lambda i: (0, i, 0, 0)),
        ],
        out_specs=[spec, spec],
        scratch_shapes=[pltpu.VMEM((9, 8, BW), F32)],
        compiler_params=pltpu.CompilerParams(vmem_limit_bytes=VMEM_BYTES),
        name="combine",
    )(gram, q)


def body(piece_height, piece_weight, piece_column, piece_width):
    lon_count, lat_count = lax.axis_size("lon"), lax.axis_size("lat")
    lon, lat = lax.axis_index("lon"), lax.axis_index("lat")
    place = jnp.stack([lon, lat, jnp.int32(lat_count)]).astype(jnp.int32)

    packed = pack(piece_column, piece_height, piece_weight, lon_count)
    got = lax.all_to_all(packed, "lon", split_axis=0, concat_axis=0, tiled=True)

    small = exchanged(small_messages(piece_height, piece_column, piece_width, lon), lon_count)
    facts = small[:, CAPACITY, :2 * CAPACITY].astype(jnp.int32).reshape(-1)

    rhs, diag, up, down, edge = sums(place, facts, got, small)
    south = passed_along(up, "lat", 1)
    north = passed_along(down, "lat", -1)
    to_west = jnp.concatenate([edge[0], south[0], north[0]], axis=0)
    to_east = jnp.concatenate([edge[1], south[-1], north[-1]], axis=0)
    west = passed_around(to_east, "lon", 1)
    east = passed_around(to_west, "lon", -1)
    q, gram = basis(place, rhs, diag, up, south, north, west, east)
    spread = jnp.broadcast_to(gram[None], (lon_count * lat_count, 1, BW))
    grams = lax.all_to_all(spread, ("lon", "lat"), split_axis=0, concat_axis=0, tiled=True)
    return tuple(combine(grams.reshape(lon_count * lat_count, BW), q))


def solution(mesh):
    return jax.shard_map(
        body,
        mesh=mesh,
        in_specs=(P("lon", "lat", None), P("lon", "lat", None), P("lon"), P("lon")),
        out_specs=(P("lat", "lon"), P("lat", "lon")),
        check_vma=False,
    )
```

time: 850 us -> 195 us (0.23)
  blocking collectives: 534 us -> 27 us
  waiting for transfers between devices: 157 us -> 97.4 us
  other arithmetic: 48.7 us -> 0.82 us
  starting transfers between devices: 61 us -> 34 us
  Pallas kernels: 0 us -> 26.9 us
  matrix products: 13.9 us -> 0.32 us
  between operations: 10.6 us -> 0.93 us
  local copies, waits for them, and re-layouts: 16.3 us -> 6.93 us
    psum x7 -> x0, blocking collectives: 534 us -> none  [the longest x4 297 us: squares(): return lax.psum(jnp.sum(residual * residual), ('lon', 'lat'))]
    all_to_all x5 -> x1, waiting for transfers between devices: 127 us -> 0.01 us  [body(): got = lax.all_to_all(packed, 'lon', split_axis=0, concat_axis=0, tiled=True)]
    ppermute x16 -> x8, waiting for transfers between devices: 26 us -> 92.5 us  [the longest x6 89.1 us: exchanged(): lax.ppermute(split[:, 1], 'lon', [(i, i ^ bit) for i in range(lon_count)])]
    all_to_all x0 -> x1, blocking collectives: none -> 27 us  [body(): lax.all_to_all(spread, ('lon', 'lat'), split_axis=0, concat_axis=0, tiled...]
    pallas_call x0 -> x4, Pallas kernels: none -> 26.9 us  [the longest x1 12.7 us: basis(): pl.pallas_call(basis_kernel, out_shape=[jax.ShapeDtypeStruct((5, BLOCKS,...]
    all_to_all x5 -> x1, starting transfers between devices: 38.6 us -> 13.3 us  [body(): got = lax.all_to_all(packed, 'lon', split_axis=0, concat_axis=0, tiled=True)]
    unnamed x5 -> x0, other arithmetic: 16.2 us -> none
    another operation x1 -> x7, other arithmetic: 14.2 us -> 0.23 us  [the longest x6 0.15 us: exchanged(): message = jnp.stack([split[:, 0], moved], axis=1).reshape(shape)]
  transfers between devices with their start and end apart: 23 -> 12, of which waited for: 23 -> 11; matrix products, arithmetic and copies ran while one was open for 4% -> 2% of each run, Pallas kernels for 0% -> 0%
where the time goes in v1:
time: 195 us; the launch traced here: 194 us
  waiting for transfers between devices  97.4 us (50%)
  starting transfers between devices  34 us (17%)
  blocking collectives  27 us (14%)
  Pallas kernels  26.9 us (14%)
  local copies, waits for them, and re-layouts  6.93 us (4%)
    ppermute x6, waiting for transfers between devices, exchanged(): lax.ppermute(split[:, 1], 'lon', [(i, i ^ bit) for i in range(lon_count)])  89.1 us
    all_to_all x1, blocking collectives, body(): lax.all_to_all(spread, ('lon', 'lat'), split_axis=0, concat_axis=0, tiled...  27 us
    all_to_all x1, starting transfers between devices, body(): got = lax.all_to_all(packed, 'lon', split_axis=0, concat_axis=0, tiled=True)  13.3 us
    pallas_call x1, Pallas kernels, basis(): pl.pallas_call(basis_kernel, out_shape=[jax.ShapeDtypeStruct((5, BLOCKS,...  12.7 us
    pallas_call x1, Pallas kernels, sums(): pl.pallas_call(sums_kernel, grid=(tiles // batch,), out_shape=[jax.ShapeD...  10.8 us
    ppermute x6, starting transfers between devices, exchanged(): lax.ppermute(split[:, 1], 'lon', [(i, i ^ bit) for i in range(lon_count)])  10.4 us
    ppermute x3, starting transfers between devices, passed_along(): return lax.ppermute(block, axis, route)  6.58 us
    unnamed x14, local copies, waits for them, and re-layouts  5.1 us
  transfers between devices with their start and end apart: 12, of which 11 were waited for; matrix products, arithmetic and copies ran while one was open for 2% of the time, Pallas kernels for 0%

profile of v1, /device:TPU:1, one launch (start us, length us, event | category | flops | bytes accessed | tf_op | source)
XLA Modules:
  0.0 194.3 jit_solution(14041588674068631522)
XLA Ops:
  0.6 1.2 copy-done.1
  1.9 1.2 copy-done.2
  3.1 0.7 copy-done.3
  3.7 1.5 pack.1
  5.3 2.0 %copy-done = f32[64,4,32,128]{3,2,1,0:T(8,128)} copy-done((f32[64,4,32,128]{3,2,1,0:T(8,128)}, f32[64,4,32,128]{3,2,1,0:T(8,128)S(1)}, u32[]{:S(2)}) %copy-start) | copy-done | bytes 4194328
  7.2 13.3 %all-to-all-start = ((f32[64,4,32,128]{3,2,1,0:T(8,128)}), f32[64,4,32,128]{3,2,1,0:T(8,128)}, u32[]{:S(2)}, u32[]{:S(2)}) async-start(f32[64,4,32,128]{3,2,1,0:T(8,128)} %copy-done), calls=%async_computation | async-start | bytes 8388608 | tf_op jit(solution)/shard_map/all_to_all | solution.py:360
  20.6 1.0 slice.60
  21.5 1.3 collective-permute-start
  23.6 2.9 %collective-permute-done = f32[64,128]{1,0:T(8,128)S(1)} collective-permute-done((f32[64,128]{1,0:T(8,128)S(1)}, f32[64,128]{1,0:T(8,128)S(1)}, u32[]{:S(2)}, u32[]{:S(2)}) %collective-permute-start) | collective-permute-done | bytes 32800 | tf_op jit(solution)/shard_map/ppermute | solution.py:28
  27.0 1.4 collective-permute-start.1
  28.4 0.9 collective-permute-done.1
  29.4 1.3 collective-permute-start.2
  30.7 4.6 %collective-permute-done.2 = f32[16,2,4,128]{3,0,2,1:T(8,128)S(1)} collective-permute-done((f32[16,2,4,128]{3,0,2,1:T(8,128)S(1)}, f32[16,2,4,128]{3,0,2,1:T(8,128)S(1)}, u32[]{:S(2)}, u32[]{:S(2)}) %collective-permute-start.2) | collective-permute-done | bytes 65568 | tf_op jit(solution)/shard_map/ppermute | solution.py:95
  35.5 2.1 %collective-permute-start.3 = (f32[8,4,4,128]{3,0,2,1:T(8,128)S(1)}, f32[8,4,4,128]{3,0,2,1:T(8,128)S(1)}, u32[]{:S(2)}, u32[]{:S(2)}) collective-permute-start(f32[8,4,4,128]{3,0,2,1:T(8,128)S(1)} %bitcast.67), channel_id=1, source_target_pairs={{0,16},{4,20},{8,24},{12,28},{16,0},{20,4},{24,8},{28,12},{32,48},... | collective-permute-start | bytes 196616 | tf_op jit(solution)/shard_map/ppermute | solution.py:95
  37.5 3.7 %collective-permute-done.3 = f32[8,4,4,128]{3,0,2,1:T(8,128)S(1)} collective-permute-done((f32[8,4,4,128]{3,0,2,1:T(8,128)S(1)}, f32[8,4,4,128]{3,0,2,1:T(8,128)S(1)}, u32[]{:S(2)}, u32[]{:S(2)}) %collective-permute-start.3) | collective-permute-done | bytes 65568 | tf_op jit(solution)/shard_map/ppermute | solution.py:95
  41.4 2.2 %collective-permute-start.4 = (f32[4,8,4,128]{3,1,2,0:T(8,128)S(1)}, f32[4,8,4,128]{3,1,2,0:T(8,128)S(1)}, u32[]{:S(2)}, u32[]{:S(2)}) collective-permute-start(f32[4,8,4,128]{3,1,2,0:T(8,128)S(1)} %get-tuple-element.27), channel_id=1, source_target_pairs={{0,32},{4,36},{8,40},{12,44},{16,48},{20,52},{24,56},{28,60},{32,0... | collective-permute-start | bytes 196616 | tf_op jit(solution)/shard_map/ppermute | solution.py:95
  43.6 70.2 %collective-permute-done.4 = f32[4,8,4,128]{3,1,2,0:T(8,128)S(1)} collective-permute-done((f32[4,8,4,128]{3,1,2,0:T(8,128)S(1)}, f32[4,8,4,128]{3,1,2,0:T(8,128)S(1)}, u32[]{:S(2)}, u32[]{:S(2)}) %collective-permute-start.4) | collective-permute-done | bytes 65568 | tf_op jit(solution)/shard_map/ppermute | solution.py:95
  113.8 1.0 collective-permute-start.5
  114.8 5.0 %collective-permute-done.5 = f32[2,16,4,128]{3,1,2,0:T(8,128)S(1)} collective-permute-done((f32[2,16,4,128]{3,1,2,0:T(8,128)S(1)}, f32[2,16,4,128]{3,1,2,0:T(8,128)S(1)}, u32[]{:S(2)}, u32[]{:S(2)}) %collective-permute-start.5) | collective-permute-done | bytes 65568 | tf_op jit(solution)/shard_map/ppermute | solution.py:95
  119.8 2.5 %collective-permute-start.6 = (f32[1,32,4,128]{3,1,2,0:T(8,128)S(1)}, f32[1,32,4,128]{3,1,2,0:T(8,128)S(1)}, u32[]{:S(2)}, u32[]{:S(2)}) collective-permute-start(f32[1,32,4,128]{3,1,2,0:T(8,128)S(1)} %get-tuple-element.23), channel_id=1, source_target_pairs={{0,128},{4,132},{8,136},{12,140},{16,144},{20,148},{24,152},{28,15... | collective-permute-start | bytes 196616 | tf_op jit(solution)/shard_map/ppermute | solution.py:95
  122.4 4.6 %collective-permute-done.6 = f32[1,32,4,128]{3,1,2,0:T(8,128)S(1)} collective-permute-done((f32[1,32,4,128]{3,1,2,0:T(8,128)S(1)}, f32[1,32,4,128]{3,1,2,0:T(8,128)S(1)}, u32[]{:S(2)}, u32[]{:S(2)}) %collective-permute-start.6) | collective-permute-done | bytes 65568 | tf_op jit(solution)/shard_map/ppermute | solution.py:95
  127.4 10.8 %sums.1 = (f32[32,32,128]{2,1,0:T(8,128)S(1)}, f32[32,32,128]{2,1,0:T(8,128)S(1)}, f32[32,8,128]{2,1,0:T(8,128)S(1)}, f32[32,8,128]{2,1,0:T(8,128)S(1)}, f32[2,72,128]{2,1,0:T(8,128)S(1)}) custom-call(s32[3]{0:T(128)S(1)} %pad_add_fusion.place_ref, s32[256]{0:T(256)S(1)} %convert_element_type.20.facts_ref, f32[64,4,32,128]{3,2,1,0:T(8,128)} %all-to-all-done.got_ref, ...), custom_call_target="tpu_custom_call" | custom-call | tf_op jit(solution)/shard_map/sums/pallas_call | solution.py:168
  138.2 1.3 collective-permute-start.8
  139.5 4.0 %collective-permute-start.7 = (f32[32,8,128]{2,1,0:T(8,128)S(1)}, f32[32,8,128]{2,1,0:T(8,128)S(1)}, u32[]{:S(2)}, u32[]{:S(2)}) collective-permute-start(f32[32,8,128]{2,1,0:T(8,128)S(1)} %get-tuple-element.11.up_ref), channel_id=1, source_target_pairs={{0,1},{1,2},{2,3},{4,5},{5,6},{6,7},{8,9},{9,10},{10,11},{12,13},{... | collective-permute-start | bytes 393224 | tf_op jit(solution)/shard_map/ppermute | solution.py:28
  143.5 0.4 collective-permute-done.8.north_ref
  143.9 1.5 collective-permute-done.7.south_ref
  145.4 3.7 %collective-permute-start.9 = (f32[88,128]{1,0:T(8,128)S(1)}, f32[88,128]{1,0:T(8,128)S(1)}, u32[]{:S(2)}, u32[]{:S(2)}) collective-permute-start(f32[88,128]{1,0:T(8,128)S(1)} %pad_maximum_fusion.6), channel_id=1, source_target_pairs={{0,4},{4,8},{8,12},{12,16},{16,20},{20,24},{24,28},{28,32},{32,36}... | collective-permute-start | bytes 135176 | tf_op jit(solution)/shard_map/ppermute | solution.py:33
  149.1 1.1 collective-permute-done.9.west_ref
  150.3 2.3 %collective-permute-done.10.east_ref = f32[88,128]{1,0:T(8,128)S(1)} collective-permute-done((f32[88,128]{1,0:T(8,128)S(1)}, f32[88,128]{1,0:T(8,128)S(1)}, u32[]{:S(2)}, u32[]{:S(2)}) %collective-permute-start.10) | collective-permute-done | bytes 45088 | tf_op jit(solution)/shard_map/ppermute | solution.py:33
  152.6 12.7 %basis.1 = (f32[5,32,32,128]{3,2,1,0:T(8,128)S(1)}, f32[1,128]{1,0:T(1,128)S(1)}) custom-call(s32[3]{0:T(128)S(1)} %pad_add_fusion.place_ref, f32[32,32,128]{2,1,0:T(8,128)S(1)} %get-tuple-element.9.rhs_ref, f32[32,32,128]{2,1,0:T(8,128)S(1)} %get-tuple-element.10.diag_ref, f32[32,8,128]{2,1,0:T(8,128)S(1)} %get-tuple-element.11.up_ref, ...), custom_call_target="tpu_custom_call" | custom-call | tf_op jit(solution)/shard_map/basis/pallas_call | solution.py:260
  165.4 27.0 %all_to_all.10 = f32[256,1,128]{2,1,0:T(1,128)S(1)} all-to-all(f32[256,1,128]{2,1,0:T(1,128)S(1)} %broadcast_in_dim.8), channel_id=1, replica_groups=mesh['lon'=64,'lat'=4] {'lon','lat'}, dimensions={0} | all-to-all | bytes 262144 | tf_op jit(solution)/shard_map/all_to_all | solution.py:374
  192.4 2.0 %combine.1 = (f32[32,4096]{1,0:T(8,128)}, f32[32,4096]{1,0:T(8,128)}) custom-call(f32[256,128]{1,0:T(8,128)S(1)} %bitcast.51, f32[5,32,32,128]{3,2,1,0:T(8,128)S(1)} %get-tuple-element.15.q_ref), custom_call_target="tpu_custom_call" | custom-call | tf_op jit(solution)/shard_map/combine/pallas_call | solution.py:339
  (47 shorter events, 2.0 us)
Async XLA Ops:
  0.6 1.2 copy-start.1
  1.9 1.2 copy-start.2
  3.1 0.7 copy-start.3
  5.3 2.0 %copy-start = (f32[64,4,32,128]{3,2,1,0:T(8,128)}, f32[64,4,32,128]{3,2,1,0:T(8,128)S(1)}, u32[]{:S(2)}) copy-start(f32[64,4,32,128]{3,2,1,0:T(8,128)S(1)} %pack.1) | copy-start | bytes 12582916
  7.2 15.6 %copy-start.4 = (s32[64]{0:T(128)S(1)}, s32[64]{0:T(128)}, u32[]{:S(2)}) copy-start(s32[64]{0:T(128)} %column_ref.1) | copy-start | bytes 772
  7.2 15.8 %copy-start.5 = (s32[64]{0:T(128)S(1)}, s32[64]{0:T(128)}, u32[]{:S(2)}) copy-start(s32[64]{0:T(128)} %param.7) | copy-start | bytes 772
  7.2 120.2 %all-to-all-start = ((f32[64,4,32,128]{3,2,1,0:T(8,128)}), f32[64,4,32,128]{3,2,1,0:T(8,128)}, u32[]{:S(2)}, u32[]{:S(2)}) async-start(f32[64,4,32,128]{3,2,1,0:T(8,128)} %copy-done), calls=%async_computation | async-start | bytes 8388608 | tf_op jit(solution)/shard_map/all_to_all | solution.py:360
  21.5 5.1 %collective-permute-start = (f32[64,128]{1,0:T(8,128)S(1)}, f32[64,128]{1,0:T(8,128)S(1)}, u32[]{:S(2)}, u32[]{:S(2)}) collective-permute-start(f32[64,128]{1,0:T(8,128)S(1)} %bitcast.70), channel_id=1, source_target_pairs={{1,0},{2,1},{3,2},{5,4},{6,5},{7,6},{9,8},{10,9},{11,10},{13,12},{... | collective-permute-start | bytes 98312 | tf_op jit(solution)/shard_map/ppermute | solution.py:28
  27.0 2.3 %collective-permute-start.1 = (f32[32,1,4,128]{3,0,2,1:T(8,128)S(1)}, f32[32,1,4,128]{3,0,2,1:T(8,128)S(1)}, u32[]{:S(2)}, u32[]{:S(2)}) collective-permute-start(f32[32,1,4,128]{3,0,2,1:T(8,128)S(1)} %get-tuple-element.33), channel_id=1, source_target_pairs={{0,4},{4,0},{8,12},{12,8},{16,20},{20,16},{24,28},{28,24},{32,36},... | collective-permute-start | bytes 196616 | tf_op jit(solution)/shard_map/ppermute | solution.py:95
  29.4 5.9 %collective-permute-start.2 = (f32[16,2,4,128]{3,0,2,1:T(8,128)S(1)}, f32[16,2,4,128]{3,0,2,1:T(8,128)S(1)}, u32[]{:S(2)}, u32[]{:S(2)}) collective-permute-start(f32[16,2,4,128]{3,0,2,1:T(8,128)S(1)} %bitcast.65), channel_id=1, source_target_pairs={{0,8},{4,12},{8,0},{12,4},{16,24},{20,28},{24,16},{28,20},{32,40},... | collective-permute-start | bytes 196616 | tf_op jit(solution)/shard_map/ppermute | solution.py:95
  35.5 5.8 %collective-permute-start.3 = (f32[8,4,4,128]{3,0,2,1:T(8,128)S(1)}, f32[8,4,4,128]{3,0,2,1:T(8,128)S(1)}, u32[]{:S(2)}, u32[]{:S(2)}) collective-permute-start(f32[8,4,4,128]{3,0,2,1:T(8,128)S(1)} %bitcast.67), channel_id=1, source_target_pairs={{0,16},{4,20},{8,24},{12,28},{16,0},{20,4},{24,8},{28,12},{32,48},... | collective-permute-start | bytes 196616 | tf_op jit(solution)/shard_map/ppermute | solution.py:95
  41.4 72.4 %collective-permute-start.4 = (f32[4,8,4,128]{3,1,2,0:T(8,128)S(1)}, f32[4,8,4,128]{3,1,2,0:T(8,128)S(1)}, u32[]{:S(2)}, u32[]{:S(2)}) collective-permute-start(f32[4,8,4,128]{3,1,2,0:T(8,128)S(1)} %get-tuple-element.27), channel_id=1, source_target_pairs={{0,32},{4,36},{8,40},{12,44},{16,48},{20,52},{24,56},{28,60},{32,0... | collective-permute-start | bytes 196616 | tf_op jit(solution)/shard_map/ppermute | solution.py:95
  113.8 6.0 %collective-permute-start.5 = (f32[2,16,4,128]{3,1,2,0:T(8,128)S(1)}, f32[2,16,4,128]{3,1,2,0:T(8,128)S(1)}, u32[]{:S(2)}, u32[]{:S(2)}) collective-permute-start(f32[2,16,4,128]{3,1,2,0:T(8,128)S(1)} %get-tuple-element.25), channel_id=1, source_target_pairs={{0,64},{4,68},{8,72},{12,76},{16,80},{20,84},{24,88},{28,92},{32,9... | collective-permute-start | bytes 196616 | tf_op jit(solution)/shard_map/ppermute | solution.py:95
  119.8 7.2 %collective-permute-start.6 = (f32[1,32,4,128]{3,1,2,0:T(8,128)S(1)}, f32[1,32,4,128]{3,1,2,0:T(8,128)S(1)}, u32[]{:S(2)}, u32[]{:S(2)}) collective-permute-start(f32[1,32,4,128]{3,1,2,0:T(8,128)S(1)} %get-tuple-element.23), channel_id=1, source_target_pairs={{0,128},{4,132},{8,136},{12,140},{16,144},{20,148},{24,152},{28,15... | collective-permute-start | bytes 196616 | tf_op jit(solution)/shard_map/ppermute | solution.py:95
  138.2 5.7 %collective-permute-start.8 = (f32[32,8,128]{2,1,0:T(8,128)S(1)}, f32[32,8,128]{2,1,0:T(8,128)S(1)}, u32[]{:S(2)}, u32[]{:S(2)}) collective-permute-start(f32[32,8,128]{2,1,0:T(8,128)S(1)} %get-tuple-element.12), channel_id=1, source_target_pairs={{1,0},{2,1},{3,2},{5,4},{6,5},{7,6},{9,8},{10,9},{11,10},{13,12},{... | collective-permute-start | bytes 393224 | tf_op jit(solution)/shard_map/ppermute | solution.py:28
  139.5 5.9 %collective-permute-start.7 = (f32[32,8,128]{2,1,0:T(8,128)S(1)}, f32[32,8,128]{2,1,0:T(8,128)S(1)}, u32[]{:S(2)}, u32[]{:S(2)}) collective-permute-start(f32[32,8,128]{2,1,0:T(8,128)S(1)} %get-tuple-element.11.up_ref), channel_id=1, source_target_pairs={{0,1},{1,2},{2,3},{4,5},{5,6},{6,7},{8,9},{9,10},{10,11},{12,13},{... | collective-permute-start | bytes 393224 | tf_op jit(solution)/shard_map/ppermute | solution.py:28
  145.4 4.8 %collective-permute-start.9 = (f32[88,128]{1,0:T(8,128)S(1)}, f32[88,128]{1,0:T(8,128)S(1)}, u32[]{:S(2)}, u32[]{:S(2)}) collective-permute-start(f32[88,128]{1,0:T(8,128)S(1)} %pad_maximum_fusion.6), channel_id=1, source_target_pairs={{0,4},{4,8},{8,12},{12,16},{16,20},{20,24},{24,28},{28,32},{32,36}... | collective-permute-start | bytes 135176 | tf_op jit(solution)/shard_map/ppermute | solution.py:33
  149.1 3.5 %collective-permute-start.10 = (f32[88,128]{1,0:T(8,128)S(1)}, f32[88,128]{1,0:T(8,128)S(1)}, u32[]{:S(2)}, u32[]{:S(2)}) collective-permute-start(f32[88,128]{1,0:T(8,128)S(1)} %pad_maximum_fusion.7), channel_id=1, source_target_pairs={{0,252},{4,0},{8,4},{12,8},{16,12},{20,16},{24,20},{28,24},{32,28}... | collective-permute-start | bytes 135176 | tf_op jit(solution)/shard_map/ppermute | solution.py:33

commit v2 on v1

--- a/solution.py
+++ b/solution.py
@@ -10,6 +10,7 @@
 BW = 128
 BLOCKS = COLS_DEV // BW
 CAPACITY = 2
+NEAR = 8
 
 MU_DATA = 0.5
 DAMPING = 0.5
@@ -19,6 +20,7 @@
 MID = 5.5
 HALF = 5.5
 VMEM_BYTES = 40 * 1024 * 1024
+PACK_VMEM_BYTES = 60 * 1024 * 1024
 F32 = jnp.float32
 
 
@@ -33,10 +35,10 @@
     return lax.ppermute(block, axis, [(i, (i + distance) % count) for i in range(count)])
 
 
-def pack_kernel(column_ref, height_ref, weight_ref, out_ref, count_ref):
+def pack_kernel(column_ref, height_ref, weight_ref, out_ref, count_ref, sem):
     tiles, pieces = out_ref.shape[0], height_ref.shape[0]
 
-    @pl.loop(0, tiles)
+    @pl.loop(0, tiles, unroll=8)
     def _(t):
         count_ref[t] = 0
 
@@ -45,8 +47,12 @@
         tile = column_ref[p] // COLS_DEV
         slot = count_ref[tile]
         count_ref[tile] = slot + 1
-        out_ref[tile, 2 * slot] = height_ref[p]
-        out_ref[tile, 2 * slot + 1] = weight_ref[p]
+        pltpu.make_async_copy(height_ref.at[p], out_ref.at[tile, 2 * slot], sem.at[0]).start()
+        pltpu.make_async_copy(weight_ref.at[p], out_ref.at[tile, 2 * slot + 1], sem.at[1]).start()
+
+    half = out_ref.at[pl.ds(0, pieces), 0]
+    pltpu.make_async_copy(height_ref, half, sem.at[0]).wait()
+    pltpu.make_async_copy(weight_ref, half, sem.at[1]).wait()
 
 
 def pack(piece_column, piece_height, piece_weight, tiles):
@@ -56,12 +62,12 @@
         out_shape=jax.ShapeDtypeStruct((tiles, 2 * CAPACITY, rows, BW), F32),
         in_specs=[
             pl.BlockSpec(memory_space=pltpu.SMEM),
-            pl.BlockSpec(memory_space=pltpu.VMEM),
-            pl.BlockSpec(memory_space=pltpu.VMEM),
+            pl.BlockSpec(memory_space=pl.ANY),
+            pl.BlockSpec(memory_space=pl.ANY),
         ],
-        out_specs=pl.BlockSpec(memory_space=pltpu.VMEM),
-        scratch_shapes=[pltpu.SMEM((tiles,), jnp.int32)],
-        compiler_params=pltpu.CompilerParams(vmem_limit_bytes=VMEM_BYTES),
+        out_specs=pl.BlockSpec(memory_space=pl.ANY),
+        scratch_shapes=[pltpu.SMEM((tiles,), jnp.int32), pltpu.SemaphoreType.DMA((2,))],
+        compiler_params=pltpu.CompilerParams(vmem_limit_bytes=PACK_VMEM_BYTES),
         name="pack",
     )(piece_column, piece_height, piece_weight)
 
@@ -90,12 +96,16 @@
 def exchanged(message, lon_count):
     shape = message.shape
     bit = 1
-    while bit < lon_count:
+    while bit < NEAR:
         split = message.reshape((lon_count // (2 * bit), 2, bit) + shape[1:])
         moved = lax.ppermute(split[:, 1], "lon", [(i, i ^ bit) for i in range(lon_count)])
         message = jnp.stack([split[:, 0], moved], axis=1).reshape(shape)
         bit *= 2
-    return message
+    parts = [message[:NEAR]]
+    for far in range(NEAR, lon_count, NEAR):
+        route = [(i, i ^ far) for i in range(lon_count)]
+        parts.append(lax.ppermute(message[far:far + NEAR], "lon", route))
+    return jnp.concatenate(parts, axis=0)
 
 
 def sums_kernel(place_ref, facts_ref, got_ref, first_ref, rhs_ref, diag_ref, up_ref, down_ref,
@@ -114,22 +124,18 @@
         entry = (step * sources + s) ^ lon
         for slot in range(CAPACITY):
             block = facts_ref[entry * 2 * CAPACITY + slot] - 1
+            block = jnp.where(block < 0, BLOCKS, block)
             width = facts_ref[entry * 2 * CAPACITY + CAPACITY + slot]
-
-            @pl.when(block >= 0)
-            def _(s=s, slot=slot, block=block, width=width, entry=entry):
-                height = got_ref[s, 2 * slot]
-                weight = got_ref[s, 2 * slot + 1]
-                above = first_ref[entry, pl.ds(slot, 1), :]
-                cell = jnp.where(lane < width, weight, 0.0)
-                east = jnp.where(lane + 1 < width, weight, 0.0)
-                east_step = pltpu.roll(height, BW - 1, 1) - height
-                raised = jnp.where(row == rows - 1, above, pltpu.roll(height, rows - 1, 0))
-                total_ref[block, 0] += cell
-                total_ref[block, 1] += cell * height
-                total_ref[block, 2] += east
-                total_ref[block, 3] += east * east_step
-                total_ref[block, 4] += cell * (raised - height)
+            height = got_ref[s, 2 * slot]
+            weight = got_ref[s, 2 * slot + 1]
+            above = first_ref[entry, pl.ds(slot, 1), :]
+            cell = jnp.where(lane < width, weight, 0.0)
+            east = jnp.where(lane < width - 1, weight, 0.0)
+            east_step = pltpu.roll(height, BW - 1, 1) - height
+            raised = jnp.where(row == rows - 1, above, pltpu.roll(height, rows - 1, 0))
+            terms = (cell, cell * height, east, east * east_step, cell * (raised - height))
+            for n, term in enumerate(terms):
+                total_ref[block, n] += term
 
     @pl.when(step == steps - 1)
     def _():
@@ -138,7 +144,7 @@
         sides = 4.0 - last.astype(F32) - first.astype(F32) + RIDGE
         row8 = row[:8]
 
-        @pl.loop(0, BLOCKS)
+        @pl.loop(0, BLOCKS, unroll=4)
         def _(i):
             cell, height = total_ref[i, 0], total_ref[i, 1]
             east = total_ref[i, 3] / (total_ref[i, 2] + DAMPING)
@@ -176,7 +182,7 @@
             whole(*first.shape),
         ],
         out_specs=[whole(*s) for s in (field, field, strip, strip, edge)],
-        scratch_shapes=[pltpu.VMEM((BLOCKS, 5, rows, BW), F32)],
+        scratch_shapes=[pltpu.VMEM((BLOCKS + 1, 5, rows, BW), F32)],
         compiler_params=pltpu.CompilerParams(vmem_limit_bytes=VMEM_BYTES),
         name="sums",
     )(place, facts, got, first)
@@ -186,21 +192,19 @@
 
 
 def basis_kernel(place_ref, rhs_ref, diag_ref, up_ref, south_ref, north_ref, west_ref, east_ref,
-                 q_ref, gram_ref, scale_ref, v_ref):
+                 q_ref, gram_ref, scale_ref, *v_refs):
     rows = rhs_ref.shape[1]
     tall = rows + 16
     lat, lat_count = place_ref[1], place_ref[2]
     row = lax.broadcasted_iota(jnp.int32, (rows, BW), 0)
     row8 = row[:8]
-    row_all = lax.broadcasted_iota(jnp.int32, (tall, BW), 0)
     lane = lax.broadcasted_iota(jnp.int32, (tall, BW), 1)
-    inside = ((row_all >= 8) | (lat > 0)) & ((row_all < rows + 8) | (lat < lat_count - 1))
 
     def assemble(i, rhs, diag, up, south, north):
         first = jnp.where(row == 0, south[0:1], 0.0) + rhs
         below = jnp.where(row8 >= 4, south, 0.0)
         above = jnp.where(row8 == 0, north + up, jnp.where(row8 < 4, north, 0.0))
-        v_ref[0, i] = jnp.concatenate([below, first, above], axis=0)
+        v_refs[0][i, 8:8 + tall] = jnp.concatenate([below, first, above], axis=0)
         diag = jnp.concatenate([pltpu.roll(south, 4, 0), diag, pltpu.roll(north, 4, 0)], axis=0)
         scale_ref[i] = (diag - MID) * (2.0 / HALF)
 
@@ -209,33 +213,36 @@
         assemble(i, ref[0:rows], ref[rows:two], ref[two:two + 8], ref[two + 8:two + 16],
                  ref[two + 16:two + 24])
 
-    @pl.loop(0, BLOCKS)
+    @pl.loop(0, BLOCKS, unroll=4)
     def _(i):
         assemble(i + 1, rhs_ref[i], diag_ref[i], up_ref[i], south_ref[i], north_ref[i])
 
     def applied(k, i):
-        v = v_ref[k, i]
-        left = v_ref[k, jnp.maximum(i - 1, 0)]
-        right = v_ref[k, jnp.minimum(i + 1, BLOCKS + 1)]
+        body = slice(8, 8 + tall)
+        v = v_refs[k][i, body]
+        left = v_refs[k][jnp.maximum(i - 1, 0), body]
+        right = v_refs[k][jnp.minimum(i + 1, BLOCKS + 1), body]
         west = pltpu.roll(jnp.where(lane == BW - 1, left, v), 1, 1)
         east = pltpu.roll(jnp.where(lane == 0, right, v), BW - 1, 1)
-        south = pltpu.roll(v, 1, 0)
-        north = pltpu.roll(v, tall - 1, 0)
+        south = v_refs[k][i, 7:7 + tall]
+        north = v_refs[k][i, 9:9 + tall]
         image = scale_ref[i] * v - (2.0 / HALF) * ((west + east) + (south + north))
         if k == 0:
             image = 0.5 * image
         else:
-            image = image - v_ref[k - 1, i]
-        return jnp.where(inside, image, 0.0)
+            image = image - v_refs[k - 1][i, body]
+        ends = (jnp.where(lat > 0, image[:8], 0.0), image[8:rows + 8],
+                jnp.where(lat < lat_count - 1, image[rows + 8:], 0.0))
+        return jnp.concatenate(ends, axis=0)
 
     for k in range(3):
-        @pl.loop(0, BLOCKS + 2)
+        @pl.loop(0, BLOCKS + 2, unroll=17)
         def _(i, k=k):
-            v_ref[k + 1, i] = applied(k, i)
+            v_refs[k + 1][i, 8:8 + tall] = applied(k, i)
 
     def products(i, carry):
         last = applied(3, i + 1)[8:8 + rows]
-        q = [v_ref[k, i + 1, 8:8 + rows] for k in range(4)] + [last]
+        q = [v_refs[k][i + 1, 16:16 + rows] for k in range(4)] + [last]
         for k in range(5):
             q_ref[k, i] = q[k]
         out = []
@@ -245,7 +252,7 @@
         return tuple(out)
 
     zero = tuple(jnp.zeros((8, BW), F32) for _ in PAIRS)
-    totals = lax.fori_loop(0, BLOCKS, products, zero)
+    totals = lax.fori_loop(0, BLOCKS, products, zero, unroll=4)
     lane1 = lax.broadcasted_iota(jnp.int32, (1, BW), 1)
     gram = jnp.zeros((1, BW), F32)
     for n, total in enumerate(totals):
@@ -267,8 +274,7 @@
         out_specs=[vmem, vmem],
         scratch_shapes=[
             pltpu.VMEM((BLOCKS + 2, rows + 16, BW), F32),
-            pltpu.VMEM((4, BLOCKS + 2, rows + 16, BW), F32),
-        ],
+        ] + [pltpu.VMEM((BLOCKS + 2, rows + 32, BW), F32)] * 4,
         compiler_params=pltpu.CompilerParams(vmem_limit_bytes=VMEM_BYTES),
         name="basis",
     )(place, rhs, diag, up, south, north, west, east)

time: 195 us -> 234 us (1.20)
  Pallas kernels: 26.9 us -> 77.4 us
  waiting for transfers between devices: 97.4 us -> 79.9 us
  starting transfers between devices: 34 us -> 46.6 us
  local copies, waits for them, and re-layouts: 6.93 us -> 1.7 us
    ppermute x6 -> x3, waiting for transfers between devices: 89.1 us -> 9.2 us  [exchanged(): lax.ppermute(split[:, 1], 'lon', [(i, i ^ bit) for i in range(lon_count)])]
    pallas_call x1, Pallas kernels: 1.51 us -> 65.4 us  [pack(): pl.pallas_call(pack_kernel, out_shape=jax.ShapeDtypeStruct((tiles, 2 * CA...]
    ppermute x0 -> x7, waiting for transfers between devices: none -> 62.4 us  [exchanged(): parts.append(lax.ppermute(message[far:far + NEAR], 'lon', route))]
    ppermute x0 -> x7, starting transfers between devices: none -> 16.9 us  [exchanged(): parts.append(lax.ppermute(message[far:far + NEAR], 'lon', route))]
    pallas_call x1, Pallas kernels: 12.7 us -> 3.58 us  [basis(): pl.pallas_call(basis_kernel, out_shape=[jax.ShapeDtypeStruct((5, BLOCKS,...]
    ppermute x6 -> x3, starting transfers between devices: 10.4 us -> 4.73 us  [exchanged(): lax.ppermute(split[:, 1], 'lon', [(i, i ^ bit) for i in range(lon_count)])]
    unnamed x14 -> x11, local copies, waits for them, and re-layouts: 5.1 us -> 0.06 us
    pallas_call x1, Pallas kernels: 10.8 us -> 6.5 us  [sums(): pl.pallas_call(sums_kernel, grid=(tiles // batch,), out_shape=[jax.ShapeD...]
  transfers between devices with their start and end apart: 12 -> 16, of which waited for: 11 -> 11; matrix products, arithmetic and copies ran while one was open for 2% -> 1% of each run, Pallas kernels for 0% -> 0%
where the time goes in v2:
time: 234 us; the launch traced here: 233 us
  waiting for transfers between devices  79.9 us (34%)
  Pallas kernels  77.4 us (33%)
  starting transfers between devices  46.6 us (20%)
  blocking collectives  25.6 us (11%)
    pallas_call x1, Pallas kernels, pack(): pl.pallas_call(pack_kernel, out_shape=jax.ShapeDtypeStruct((tiles, 2 * CA...  65.4 us
    ppermute x7, waiting for transfers between devices, exchanged(): parts.append(lax.ppermute(message[far:far + NEAR], 'lon', route))  62.4 us
    all_to_all x1, blocking collectives, body(): lax.all_to_all(spread, ('lon', 'lat'), split_axis=0, concat_axis=0, tiled...  25.6 us
    ppermute x7, starting transfers between devices, exchanged(): parts.append(lax.ppermute(message[far:far + NEAR], 'lon', route))  16.9 us
    all_to_all x1, starting transfers between devices, body(): got = lax.all_to_all(packed, 'lon', split_axis=0, concat_axis=0, tiled=True)  13.2 us
    ppermute x3, waiting for transfers between devices, exchanged(): lax.ppermute(split[:, 1], 'lon', [(i, i ^ bit) for i in range(lon_count)])  9.2 us
    ppermute x3, starting transfers between devices, passed_along(): return lax.ppermute(block, axis, route)  6.58 us
    pallas_call x1, Pallas kernels, sums(): pl.pallas_call(sums_kernel, grid=(tiles // batch,), out_shape=[jax.ShapeD...  6.5 us
  transfers between devices with their start and end apart: 16, of which 11 were waited for; matrix products, arithmetic and copies ran while one was open for 1% of the time, Pallas kernels for 0%

profile of v2, /device:TPU:1, one launch (start us, length us, event | category | flops | bytes accessed | tf_op | source)
XLA Modules:
  0.0 233.3 jit_solution(3554824232064942711)
XLA Ops:
  0.6 65.4 %pack.1 = f32[64,4,32,128]{3,2,1,0:T(8,128)} custom-call(s32[64]{0:T(128)} %column_ref.1, f32[64,32,128]{2,1,0:T(8,128)} %height_ref.1, f32[64,32,128]{2,1,0:T(8,128)} %weight_ref.1), custom_call_target="tpu_custom_call" | custom-call | tf_op jit(solution)/shard_map/pack/pallas_call | solution.py:60
  66.1 13.2 %all-to-all-start = ((f32[64,4,32,128]{3,2,1,0:T(8,128)}), f32[64,4,32,128]{3,2,1,0:T(8,128)}, u32[]{:S(2)}, u32[]{:S(2)}) async-start(f32[64,4,32,128]{3,2,1,0:T(8,128)} %pack.1), calls=%async_computation | async-start | bytes 8388608 | tf_op jit(solution)/shard_map/all_to_all | solution.py:366
  79.3 1.0 slice.90
  80.2 1.3 collective-permute-start
  82.3 2.9 %collective-permute-done = f32[64,128]{1,0:T(8,128)S(1)} collective-permute-done((f32[64,128]{1,0:T(8,128)S(1)}, f32[64,128]{1,0:T(8,128)S(1)}, u32[]{:S(2)}, u32[]{:S(2)}) %collective-permute-start) | collective-permute-done | bytes 32800 | tf_op jit(solution)/shard_map/ppermute | solution.py:30
  85.3 0.3 fusion.2
  85.7 1.4 collective-permute-start.1
  87.1 0.9 collective-permute-done.1
  88.1 1.3 collective-permute-start.2
  89.4 4.6 %collective-permute-done.2 = f32[16,2,4,128]{3,0,2,1:T(8,128)S(1)} collective-permute-done((f32[16,2,4,128]{3,0,2,1:T(8,128)S(1)}, f32[16,2,4,128]{3,0,2,1:T(8,128)S(1)}, u32[]{:S(2)}, u32[]{:S(2)}) %collective-permute-start.2) | collective-permute-done | bytes 65568 | tf_op jit(solution)/shard_map/ppermute | solution.py:101
  94.2 2.1 collective-permute-start.3
  96.3 3.7 %collective-permute-done.3 = f32[8,4,4,128]{3,0,2,1:T(8,128)S(1)} collective-permute-done((f32[8,4,4,128]{3,0,2,1:T(8,128)S(1)}, f32[8,4,4,128]{3,0,2,1:T(8,128)S(1)}, u32[]{:S(2)}, u32[]{:S(2)}) %collective-permute-start.3) | collective-permute-done | bytes 65568 | tf_op jit(solution)/shard_map/ppermute | solution.py:101
  100.1 3.5 %collective-permute-start.10 = (f32[8,4,128]{2,1,0:T(4,128)S(1)}, f32[8,4,128]{2,1,0:T(4,128)S(1)}, u32[]{:S(2)}, u32[]{:S(2)}) collective-permute-start(f32[8,4,128]{2,1,0:T(4,128)S(1)} %bitcast.55), channel_id=1, source_target_pairs={{0,224},{4,228},{8,232},{12,236},{16,240},{20,244},{24,248},{28,25... | collective-permute-start | bytes 49160 | tf_op jit(solution)/shard_map/ppermute | solution.py:107
  103.6 4.9 %collective-permute-start.4 = (f32[8,4,128]{2,1,0:T(4,128)S(1)}, f32[8,4,128]{2,1,0:T(4,128)S(1)}, u32[]{:S(2)}, u32[]{:S(2)}) collective-permute-start(f32[8,4,128]{2,1,0:T(4,128)S(1)} %bitcast.61), channel_id=1, source_target_pairs={{0,32},{4,36},{8,40},{12,44},{16,48},{20,52},{24,56},{28,60},{32,0... | collective-permute-start | bytes 49160 | tf_op jit(solution)/shard_map/ppermute | solution.py:107
  108.5 2.1 collective-permute-start.6
  110.6 0.9 collective-permute-start.7
  111.5 60.3 %collective-permute-done.4 = f32[8,4,128]{2,1,0:T(4,128)S(1)} collective-permute-done((f32[8,4,128]{2,1,0:T(4,128)S(1)}, f32[8,4,128]{2,1,0:T(4,128)S(1)}, u32[]{:S(2)}, u32[]{:S(2)}) %collective-permute-start.4) | collective-permute-done | bytes 16416 | tf_op jit(solution)/shard_map/ppermute | solution.py:107
  171.8 2.6 %collective-permute-start.8 = (f32[8,4,128]{2,1,0:T(4,128)S(1)}, f32[8,4,128]{2,1,0:T(4,128)S(1)}, u32[]{:S(2)}, u32[]{:S(2)}) collective-permute-start(f32[8,4,128]{2,1,0:T(4,128)S(1)} %bitcast.57), channel_id=1, source_target_pairs={{0,160},{4,164},{8,168},{12,172},{16,176},{20,180},{24,184},{28,18... | collective-permute-start | bytes 49160 | tf_op jit(solution)/shard_map/ppermute | solution.py:107
  174.4 2.9 %collective-permute-start.9 = (f32[8,4,128]{2,1,0:T(4,128)S(1)}, f32[8,4,128]{2,1,0:T(4,128)S(1)}, u32[]{:S(2)}, u32[]{:S(2)}) collective-permute-start(f32[8,4,128]{2,1,0:T(4,128)S(1)} %bitcast.56), channel_id=1, source_target_pairs={{0,192},{4,196},{8,200},{12,204},{16,208},{20,212},{24,216},{28,22... | collective-permute-start | bytes 49160 | tf_op jit(solution)/shard_map/ppermute | solution.py:107
  177.3 0.3 collective-permute-done.8
  177.6 1.8 collective-permute-done.9
  179.7 6.5 %sums.1 = (f32[32,32,128]{2,1,0:T(8,128)S(1)}, f32[32,32,128]{2,1,0:T(8,128)S(1)}, f32[32,8,128]{2,1,0:T(8,128)S(1)}, f32[32,8,128]{2,1,0:T(8,128)S(1)}, f32[2,72,128]{2,1,0:T(8,128)S(1)}) custom-call(s32[3]{0:T(128)S(1)} %pad_add_fusion.place_ref, s32[256]{0:T(256)S(1)} %convert_element_type.20.facts_ref, f32[64,4,32,128]{3,2,1,0:T(8,128)} %all-to-all-done.got_ref, ...), custom_call_target="tpu_custom_call" | custom-call | tf_op jit(solution)/shard_map/sums/pallas_call | solution.py:174
  186.2 1.3 collective-permute-start.12
  187.5 4.0 %collective-permute-start.11 = (f32[32,8,128]{2,1,0:T(8,128)S(1)}, f32[32,8,128]{2,1,0:T(8,128)S(1)}, u32[]{:S(2)}, u32[]{:S(2)}) collective-permute-start(f32[32,8,128]{2,1,0:T(8,128)S(1)} %get-tuple-element.11.up_ref), channel_id=1, source_target_pairs={{0,1},{1,2},{2,3},{4,5},{5,6},{6,7},{8,9},{9,10},{10,11},{12,13},{... | collective-permute-start | bytes 393224 | tf_op jit(solution)/shard_map/ppermute | solution.py:30
  191.5 0.4 collective-permute-done.12.north_ref
  191.9 1.5 collective-permute-done.11.south_ref
  193.4 5.2 %collective-permute-start.13 = (f32[88,128]{1,0:T(8,128)S(1)}, f32[88,128]{1,0:T(8,128)S(1)}, u32[]{:S(2)}, u32[]{:S(2)}) collective-permute-start(f32[88,128]{1,0:T(8,128)S(1)} %pad_maximum_fusion.2), channel_id=1, source_target_pairs={{0,4},{4,8},{8,12},{12,16},{16,20},{20,24},{24,28},{28,32},{32,36}... | collective-permute-start | bytes 135176 | tf_op jit(solution)/shard_map/ppermute | solution.py:35
  198.6 1.1 collective-permute-done.13.west_ref
  199.7 2.3 %collective-permute-done.14.east_ref = f32[88,128]{1,0:T(8,128)S(1)} collective-permute-done((f32[88,128]{1,0:T(8,128)S(1)}, f32[88,128]{1,0:T(8,128)S(1)}, u32[]{:S(2)}, u32[]{:S(2)}) %collective-permute-start.14) | collective-permute-done | bytes 45088 | tf_op jit(solution)/shard_map/ppermute | solution.py:35
  202.1 3.6 %basis.1 = (f32[5,32,32,128]{3,2,1,0:T(8,128)S(1)}, f32[1,128]{1,0:T(1,128)S(1)}) custom-call(s32[3]{0:T(128)S(1)} %pad_add_fusion.place_ref, f32[32,32,128]{2,1,0:T(8,128)S(1)} %get-tuple-element.9.rhs_ref, f32[32,32,128]{2,1,0:T(8,128)S(1)} %get-tuple-element.10.diag_ref, f32[32,8,128]{2,1,0:T(8,128)S(1)} %get-tuple-element.11.up_ref, ...), custom_call_target="tpu_custom_call" | custom-call | tf_op jit(solution)/shard_map/basis/pallas_call | solution.py:267
  205.7 25.6 %all_to_all.10 = f32[256,1,128]{2,1,0:T(1,128)S(1)} all-to-all(f32[256,1,128]{2,1,0:T(1,128)S(1)} %broadcast_in_dim.8), channel_id=1, replica_groups=mesh['lon'=64,'lat'=4] {'lon','lat'}, dimensions={0} | all-to-all | bytes 262144 | tf_op jit(solution)/shard_map/all_to_all | solution.py:380
  231.4 2.0 combine.1
  (45 shorter events, 1.6 us)
Async XLA Ops:
  66.0 15.5 %copy-start = (s32[64]{0:T(128)S(1)}, s32[64]{0:T(128)}, u32[]{:S(2)}) copy-start(s32[64]{0:T(128)} %column_ref.1) | copy-start | bytes 772
  66.1 15.7 %copy-start.1 = (s32[64]{0:T(128)S(1)}, s32[64]{0:T(128)}, u32[]{:S(2)}) copy-start(s32[64]{0:T(128)} %param.7) | copy-start | bytes 772
  66.1 113.6 %all-to-all-start = ((f32[64,4,32,128]{3,2,1,0:T(8,128)}), f32[64,4,32,128]{3,2,1,0:T(8,128)}, u32[]{:S(2)}, u32[]{:S(2)}) async-start(f32[64,4,32,128]{3,2,1,0:T(8,128)} %pack.1), calls=%async_computation | async-start | bytes 8388608 | tf_op jit(solution)/shard_map/all_to_all | solution.py:366
  80.2 5.1 %collective-permute-start = (f32[64,128]{1,0:T(8,128)S(1)}, f32[64,128]{1,0:T(8,128)S(1)}, u32[]{:S(2)}, u32[]{:S(2)}) collective-permute-start(f32[64,128]{1,0:T(8,128)S(1)} %bitcast.54), channel_id=1, source_target_pairs={{1,0},{2,1},{3,2},{5,4},{6,5},{7,6},{9,8},{10,9},{11,10},{13,12},{... | collective-permute-start | bytes 98312 | tf_op jit(solution)/shard_map/ppermute | solution.py:30
  85.7 2.3 collective-permute-start.1
  88.1 5.9 %collective-permute-start.2 = (f32[16,2,4,128]{3,0,2,1:T(8,128)S(1)}, f32[16,2,4,128]{3,0,2,1:T(8,128)S(1)}, u32[]{:S(2)}, u32[]{:S(2)}) collective-permute-start(f32[16,2,4,128]{3,0,2,1:T(8,128)S(1)} %bitcast.50), channel_id=1, source_target_pairs={{0,8},{4,12},{8,0},{12,4},{16,24},{20,28},{24,16},{28,20},{32,40},... | collective-permute-start | bytes 196616 | tf_op jit(solution)/shard_map/ppermute | solution.py:101
  94.2 5.8 %collective-permute-start.3 = (f32[8,4,4,128]{3,0,2,1:T(8,128)S(1)}, f32[8,4,4,128]{3,0,2,1:T(8,128)S(1)}, u32[]{:S(2)}, u32[]{:S(2)}) collective-permute-start(f32[8,4,4,128]{3,0,2,1:T(8,128)S(1)} %bitcast.52), channel_id=1, source_target_pairs={{0,16},{4,20},{8,24},{12,28},{16,0},{20,4},{24,8},{28,12},{32,48},... | collective-permute-start | bytes 196616 | tf_op jit(solution)/shard_map/ppermute | solution.py:101
  100.1 79.4 %collective-permute-start.10 = (f32[8,4,128]{2,1,0:T(4,128)S(1)}, f32[8,4,128]{2,1,0:T(4,128)S(1)}, u32[]{:S(2)}, u32[]{:S(2)}) collective-permute-start(f32[8,4,128]{2,1,0:T(4,128)S(1)} %bitcast.55), channel_id=1, source_target_pairs={{0,224},{4,228},{8,232},{12,236},{16,240},{20,244},{24,248},{28,25... | collective-permute-start | bytes 49160 | tf_op jit(solution)/shard_map/ppermute | solution.py:107
  103.6 68.2 %collective-permute-start.4 = (f32[8,4,128]{2,1,0:T(4,128)S(1)}, f32[8,4,128]{2,1,0:T(4,128)S(1)}, u32[]{:S(2)}, u32[]{:S(2)}) collective-permute-start(f32[8,4,128]{2,1,0:T(4,128)S(1)} %bitcast.61), channel_id=1, source_target_pairs={{0,32},{4,36},{8,40},{12,44},{16,48},{20,52},{24,56},{28,60},{32,0... | collective-permute-start | bytes 49160 | tf_op jit(solution)/shard_map/ppermute | solution.py:107
  108.5 65.9 %collective-permute-start.5 = (f32[8,4,128]{2,1,0:T(4,128)S(1)}, f32[8,4,128]{2,1,0:T(4,128)S(1)}, u32[]{:S(2)}, u32[]{:S(2)}) collective-permute-start(f32[8,4,128]{2,1,0:T(4,128)S(1)} %bitcast.60), channel_id=1, source_target_pairs={{0,64},{4,68},{8,72},{12,76},{16,80},{20,84},{24,88},{28,92},{32,9... | collective-permute-start | bytes 49160 | tf_op jit(solution)/shard_map/ppermute | solution.py:107
  108.5 68.8 %collective-permute-start.6 = (f32[8,4,128]{2,1,0:T(4,128)S(1)}, f32[8,4,128]{2,1,0:T(4,128)S(1)}, u32[]{:S(2)}, u32[]{:S(2)}) collective-permute-start(f32[8,4,128]{2,1,0:T(4,128)S(1)} %bitcast.59), channel_id=1, source_target_pairs={{0,96},{4,100},{8,104},{12,108},{16,112},{20,116},{24,120},{28,124... | collective-permute-start | bytes 49160 | tf_op jit(solution)/shard_map/ppermute | solution.py:107
  110.6 66.7 %collective-permute-start.7 = (f32[8,4,128]{2,1,0:T(4,128)S(1)}, f32[8,4,128]{2,1,0:T(4,128)S(1)}, u32[]{:S(2)}, u32[]{:S(2)}) collective-permute-start(f32[8,4,128]{2,1,0:T(4,128)S(1)} %bitcast.58), channel_id=1, source_target_pairs={{0,128},{4,132},{8,136},{12,140},{16,144},{20,148},{24,152},{28,15... | collective-permute-start | bytes 49160 | tf_op jit(solution)/shard_map/ppermute | solution.py:107
  171.8 5.9 %collective-permute-start.8 = (f32[8,4,128]{2,1,0:T(4,128)S(1)}, f32[8,4,128]{2,1,0:T(4,128)S(1)}, u32[]{:S(2)}, u32[]{:S(2)}) collective-permute-start(f32[8,4,128]{2,1,0:T(4,128)S(1)} %bitcast.57), channel_id=1, source_target_pairs={{0,160},{4,164},{8,168},{12,172},{16,176},{20,180},{24,184},{28,18... | collective-permute-start | bytes 49160 | tf_op jit(solution)/shard_map/ppermute | solution.py:107
  174.4 5.0 %collective-permute-start.9 = (f32[8,4,128]{2,1,0:T(4,128)S(1)}, f32[8,4,128]{2,1,0:T(4,128)S(1)}, u32[]{:S(2)}, u32[]{:S(2)}) collective-permute-start(f32[8,4,128]{2,1,0:T(4,128)S(1)} %bitcast.56), channel_id=1, source_target_pairs={{0,192},{4,196},{8,200},{12,204},{16,208},{20,212},{24,216},{28,22... | collective-permute-start | bytes 49160 | tf_op jit(solution)/shard_map/ppermute | solution.py:107
  186.2 5.7 %collective-permute-start.12 = (f32[32,8,128]{2,1,0:T(8,128)S(1)}, f32[32,8,128]{2,1,0:T(8,128)S(1)}, u32[]{:S(2)}, u32[]{:S(2)}) collective-permute-start(f32[32,8,128]{2,1,0:T(8,128)S(1)} %get-tuple-element.12), channel_id=1, source_target_pairs={{1,0},{2,1},{3,2},{5,4},{6,5},{7,6},{9,8},{10,9},{11,10},{13,12},{... | collective-permute-start | bytes 393224 | tf_op jit(solution)/shard_map/ppermute | solution.py:30
  187.5 5.9 %collective-permute-start.11 = (f32[32,8,128]{2,1,0:T(8,128)S(1)}, f32[32,8,128]{2,1,0:T(8,128)S(1)}, u32[]{:S(2)}, u32[]{:S(2)}) collective-permute-start(f32[32,8,128]{2,1,0:T(8,128)S(1)} %get-tuple-element.11.up_ref), channel_id=1, source_target_pairs={{0,1},{1,2},{2,3},{4,5},{5,6},{6,7},{8,9},{9,10},{10,11},{12,13},{... | collective-permute-start | bytes 393224 | tf_op jit(solution)/shard_map/ppermute | solution.py:30
  193.4 6.3 %collective-permute-start.13 = (f32[88,128]{1,0:T(8,128)S(1)}, f32[88,128]{1,0:T(8,128)S(1)}, u32[]{:S(2)}, u32[]{:S(2)}) collective-permute-start(f32[88,128]{1,0:T(8,128)S(1)} %pad_maximum_fusion.2), channel_id=1, source_target_pairs={{0,4},{4,8},{8,12},{12,16},{16,20},{20,24},{24,28},{28,32},{32,36}... | collective-permute-start | bytes 135176 | tf_op jit(solution)/shard_map/ppermute | solution.py:35
  198.6 3.5 %collective-permute-start.14 = (f32[88,128]{1,0:T(8,128)S(1)}, f32[88,128]{1,0:T(8,128)S(1)}, u32[]{:S(2)}, u32[]{:S(2)}) collective-permute-start(f32[88,128]{1,0:T(8,128)S(1)} %pad_maximum_fusion.3), channel_id=1, source_target_pairs={{0,252},{4,0},{8,4},{12,8},{16,12},{20,16},{24,20},{28,24},{32,28}... | collective-permute-start | bytes 135176 | tf_op jit(solution)/shard_map/ppermute | solution.py:35

commit v3 on v2

--- a/solution.py
+++ b/solution.py
@@ -10,12 +10,10 @@
 BW = 128
 BLOCKS = COLS_DEV // BW
 CAPACITY = 2
-NEAR = 8
 
 MU_DATA = 0.5
 DAMPING = 0.5
 RIDGE = 0.05
-HIGHEST = lax.Precision.HIGHEST
 
 MID = 5.5
 HALF = 5.5
@@ -35,84 +33,125 @@
     return lax.ppermute(block, axis, [(i, (i + distance) % count) for i in range(count)])
 
 
-def pack_kernel(column_ref, height_ref, weight_ref, out_ref, count_ref, sem):
+def pack_kernel(column_ref, height_ref, weight_ref, out_ref, held_ref, count_ref, in_sem, out_sem):
     tiles, pieces = out_ref.shape[0], height_ref.shape[0]
+    rows = height_ref.shape[1]
+    batch = pieces // in_sem.shape[0]
+
+    def loads(g):
+        part = pl.ds(g * batch, batch)
+        sources = (height_ref, weight_ref)
+        return [pltpu.make_async_copy(source.at[part], held_ref.at[part, pl.ds(n * rows, rows)],
+                                      in_sem.at[g, n]) for n, source in enumerate(sources)]
+
+    for g in range(in_sem.shape[0]):
+        for load in loads(g):
+            load.start()
 
     @pl.loop(0, tiles, unroll=8)
     def _(t):
         count_ref[t] = 0
 
-    @pl.loop(0, pieces, unroll=4)
-    def _(p):
-        tile = column_ref[p] // COLS_DEV
-        slot = count_ref[tile]
-        count_ref[tile] = slot + 1
-        pltpu.make_async_copy(height_ref.at[p], out_ref.at[tile, 2 * slot], sem.at[0]).start()
-        pltpu.make_async_copy(weight_ref.at[p], out_ref.at[tile, 2 * slot + 1], sem.at[1]).start()
-
-    half = out_ref.at[pl.ds(0, pieces), 0]
-    pltpu.make_async_copy(height_ref, half, sem.at[0]).wait()
-    pltpu.make_async_copy(weight_ref, half, sem.at[1]).wait()
-
-
-def pack(piece_column, piece_height, piece_weight, tiles):
-    rows = piece_height.shape[1]
+    for g in range(in_sem.shape[0]):
+        for load in loads(g):
+            load.wait()
+
+        @pl.loop(g * batch, (g + 1) * batch, unroll=4)
+        def _(p):
+            tile = column_ref[p] // COLS_DEV
+            slot = count_ref[tile]
+            count_ref[tile] = slot + 1
+            pltpu.make_async_copy(held_ref.at[p], out_ref.at[tile, slot, pl.ds(0, 2 * rows)],
+                                  out_sem).start()
+
+    pltpu.make_async_copy(held_ref, out_ref.at[pl.ds(0, pieces), 0, pl.ds(0, 2 * rows)],
+                          out_sem).wait()
+
+
+def pack(piece_column, piece_height, piece_weight, tiles, batches=8):
+    pieces, rows, _ = piece_height.shape
+    tall = lambda array: array.reshape(pieces, rows, 1, BW)
     return pl.pallas_call(
         pack_kernel,
-        out_shape=jax.ShapeDtypeStruct((tiles, 2 * CAPACITY, rows, BW), F32),
+        out_shape=jax.ShapeDtypeStruct((tiles, CAPACITY, 2 * rows + 2, 1, BW), F32),
         in_specs=[
             pl.BlockSpec(memory_space=pltpu.SMEM),
             pl.BlockSpec(memory_space=pl.ANY),
             pl.BlockSpec(memory_space=pl.ANY),
         ],
         out_specs=pl.BlockSpec(memory_space=pl.ANY),
-        scratch_shapes=[pltpu.SMEM((tiles,), jnp.int32), pltpu.SemaphoreType.DMA((2,))],
+        scratch_shapes=[
+            pltpu.VMEM((pieces, 2 * rows, 1, BW), F32),
+            pltpu.SMEM((tiles,), jnp.int32),
+            pltpu.SemaphoreType.DMA((batches, 2)),
+            pltpu.SemaphoreType.DMA,
+        ],
         compiler_params=pltpu.CompilerParams(vmem_limit_bytes=PACK_VMEM_BYTES),
         name="pack",
-    )(piece_column, piece_height, piece_weight)
-
-
-def small_messages(piece_height, piece_column, piece_width, lon):
-    pieces = piece_column.shape[0]
-    lon_count = lax.axis_size("lon")
-    tile = piece_column // COLS_DEV
-    block = piece_column % COLS_DEV // BW
-    ids = jnp.arange(pieces, dtype=jnp.int32)
-    same = (tile[:, None] == tile[None, :]) & (ids[None, :] < ids[:, None])
-    rank = jnp.sum(same.astype(jnp.int32), axis=1)
-    place = (tile ^ lon) * CAPACITY + rank
-    hot = jnp.arange(lon_count * CAPACITY, dtype=jnp.int32)[:, None] == place[None, :]
-    hot_int = hot.astype(jnp.int32)
-    block_of = jnp.sum(hot_int * (block + 1)[None, :], axis=1).reshape(lon_count, CAPACITY)
-    width_of = jnp.sum(hot_int * piece_width[None, :], axis=1).reshape(lon_count, CAPACITY)
-    next_first = passed_along(piece_height[:, 0, :], "lat", -1)
-    first = jnp.dot(hot.astype(F32), next_first, precision=HIGHEST)
-    facts = jnp.concatenate([block_of, width_of], axis=1).astype(F32)
-    facts = jnp.pad(facts, ((0, 0), (0, BW - 2 * CAPACITY)))[:, None, :]
-    first = first.reshape(lon_count, CAPACITY, BW)
-    return jnp.concatenate([first, facts, jnp.zeros_like(facts)], axis=1)
-
-
-def exchanged(message, lon_count):
-    shape = message.shape
-    bit = 1
-    while bit < NEAR:
-        split = message.reshape((lon_count // (2 * bit), 2, bit) + shape[1:])
-        moved = lax.ppermute(split[:, 1], "lon", [(i, i ^ bit) for i in range(lon_count)])
-        message = jnp.stack([split[:, 0], moved], axis=1).reshape(shape)
-        bit *= 2
-    parts = [message[:NEAR]]
-    for far in range(NEAR, lon_count, NEAR):
-        route = [(i, i ^ far) for i in range(lon_count)]
-        parts.append(lax.ppermute(message[far:far + NEAR], "lon", route))
-    return jnp.concatenate(parts, axis=0)
-
-
-def sums_kernel(place_ref, facts_ref, got_ref, first_ref, rhs_ref, diag_ref, up_ref, down_ref,
-                edge_ref, total_ref):
+    )(piece_column, tall(piece_height), tall(piece_weight))
+
+
+def label_kernel(column_ref, width_ref, source_ref, packed_ref, out_ref, first_ref, held_ref,
+                 count_ref, sem):
+    tiles, pieces = out_ref.shape[0], first_ref.shape[0]
+    end = out_ref.shape[2]
+    load = pltpu.make_async_copy(source_ref, first_ref, sem.at[0])
+    load.start()
+    lane = lax.broadcasted_iota(jnp.int32, (1, BW), 1)
+    held_ref[...] = jnp.zeros_like(held_ref)
+
+    @pl.loop(0, tiles, unroll=8)
+    def _(t):
+        count_ref[t] = 0
+
+    load.wait()
+
+    @pl.loop(0, pieces, unroll=4)
+    def _(p):
+        tile = column_ref[p] // COLS_DEV
+        block = column_ref[p] % COLS_DEV // BW
+        slot = count_ref[tile]
+        count_ref[tile] = slot + 1
+        held_ref[tile, slot, 0] = first_ref[p]
+        facts = jnp.where(lane == 0, block + 1, jnp.where(lane == 1, width_ref[p], 0))
+        held_ref[tile, slot, 1] = facts.astype(F32)
+
+    copy = pltpu.make_async_copy(held_ref, out_ref.at[:, :, pl.ds(end - 2, 2)], sem.at[1])
+    copy.start()
+    copy.wait()
+
+
+def label(piece_column, piece_width, next_first, packed):
+    tiles = packed.shape[0]
+    return pl.pallas_call(
+        label_kernel,
+        out_shape=jax.ShapeDtypeStruct(packed.shape, F32),
+        in_specs=[
+            pl.BlockSpec(memory_space=pltpu.SMEM),
+            pl.BlockSpec(memory_space=pltpu.SMEM),
+            pl.BlockSpec(memory_space=pl.ANY),
+            pl.BlockSpec(memory_space=pl.ANY),
+        ],
+        out_specs=pl.BlockSpec(memory_space=pl.ANY),
+        scratch_shapes=[
+            pltpu.VMEM(next_first.shape, F32),
+            pltpu.VMEM((tiles, CAPACITY, 2, 1, BW), F32),
+            pltpu.SMEM((tiles,), jnp.int32),
+            pltpu.SemaphoreType.DMA((2,)),
+        ],
+        input_output_aliases={3: 0},
+        compiler_params=pltpu.CompilerParams(vmem_limit_bytes=PACK_VMEM_BYTES),
+        name="label",
+    )(piece_column, piece_width, next_first, packed)
+
+
+def sums_kernel(place_ref, facts_ref, got_ref, rhs_ref, diag_ref, up_ref, down_ref, edge_ref,
+                total_ref):
     step, steps = pl.program_id(0), pl.num_programs(0)
-    sources, _, rows, _ = got_ref.shape
-    lon, lat, lat_count = place_ref[0], place_ref[1], place_ref[2]
+    rows = rhs_ref.shape[1]
+    part = 2 * rows + 2
+    slots = got_ref.shape[0] // part
+    lat, lat_count = place_ref[0], place_ref[1]
     lane = lax.broadcasted_iota(jnp.int32, (rows, BW), 1)
     row = lax.broadcasted_iota(jnp.int32, (rows, BW), 0)
 
@@ -120,22 +159,20 @@
     def _():
         total_ref[...] = jnp.zeros_like(total_ref)
 
-    for s in range(sources):
-        entry = (step * sources + s) ^ lon
-        for slot in range(CAPACITY):
-            block = facts_ref[entry * 2 * CAPACITY + slot] - 1
-            block = jnp.where(block < 0, BLOCKS, block)
-            width = facts_ref[entry * 2 * CAPACITY + CAPACITY + slot]
-            height = got_ref[s, 2 * slot]
-            weight = got_ref[s, 2 * slot + 1]
-            above = first_ref[entry, pl.ds(slot, 1), :]
-            cell = jnp.where(lane < width, weight, 0.0)
-            east = jnp.where(lane < width - 1, weight, 0.0)
-            east_step = pltpu.roll(height, BW - 1, 1) - height
-            raised = jnp.where(row == rows - 1, above, pltpu.roll(height, rows - 1, 0))
-            terms = (cell, cell * height, east, east * east_step, cell * (raised - height))
-            for n, term in enumerate(terms):
-                total_ref[block, n] += term
+    for s in range(slots):
+        block = facts_ref[2 * (step * slots + s)] - 1
+        block = jnp.where(block < 0, BLOCKS, block)
+        width = facts_ref[2 * (step * slots + s) + 1]
+        height = got_ref[s * part:s * part + rows]
+        weight = got_ref[s * part + rows:s * part + 2 * rows]
+        above = got_ref[s * part + 2 * rows:s * part + 2 * rows + 1]
+        cell = jnp.where(lane < width, weight, 0.0)
+        east = jnp.where(lane < width - 1, weight, 0.0)
+        east_step = pltpu.roll(height, BW - 1, 1) - height
+        raised = jnp.where(row == rows - 1, above, pltpu.roll(height, rows - 1, 0))
+        terms = (cell, cell * height, east, east * east_step, cell * (raised - height))
+        for n, term in enumerate(terms):
+            total_ref[block, n] += term
 
     @pl.when(step == steps - 1)
     def _():
@@ -165,27 +202,27 @@
             edge_ref[side, 2 * rows:2 * rows + 8] = up_ref[block]
 
 
-def sums(place, facts, got, first, batch=8):
-    tiles, arrays, rows, _ = got.shape
+def sums(place, facts, got, rows, batch=8):
+    part = 2 * rows + 2
+    slots = got.shape[0] // part
     whole = lambda *shape: pl.BlockSpec(shape, lambda i: (0,) * len(shape))
     field = (BLOCKS, rows, BW)
     strip = (BLOCKS, 8, BW)
     edge = (2, 2 * rows + 8, BW)
     return pl.pallas_call(
         sums_kernel,
-        grid=(tiles // batch,),
+        grid=(slots // (2 * batch),),
         out_shape=[jax.ShapeDtypeStruct(s, F32) for s in (field, field, strip, strip, edge)],
         in_specs=[
             pl.BlockSpec(memory_space=pltpu.SMEM),
             pl.BlockSpec(memory_space=pltpu.SMEM),
-            pl.BlockSpec((batch, arrays, rows, BW), lambda i: (i, 0, 0, 0)),
-            whole(*first.shape),
+            pl.BlockSpec((2 * batch * part, BW), lambda i: (i, 0)),
         ],
         out_specs=[whole(*s) for s in (field, field, strip, strip, edge)],
         scratch_shapes=[pltpu.VMEM((BLOCKS + 1, 5, rows, BW), F32)],
         compiler_params=pltpu.CompilerParams(vmem_limit_bytes=VMEM_BYTES),
         name="sums",
-    )(place, facts, got, first)
+    )(place, facts, got)
 
 
 PAIRS = [(i, j) for j in range(5) for i in range(min(j, 3) + 1)]
@@ -195,7 +232,7 @@
                  q_ref, gram_ref, scale_ref, *v_refs):
     rows = rhs_ref.shape[1]
     tall = rows + 16
-    lat, lat_count = place_ref[1], place_ref[2]
+    lat, lat_count = place_ref[0], place_ref[1]
     row = lax.broadcasted_iota(jnp.int32, (rows, BW), 0)
     row8 = row[:8]
     lane = lax.broadcasted_iota(jnp.int32, (tall, BW), 1)
@@ -359,16 +396,16 @@
 
 def body(piece_height, piece_weight, piece_column, piece_width):
     lon_count, lat_count = lax.axis_size("lon"), lax.axis_size("lat")
-    lon, lat = lax.axis_index("lon"), lax.axis_index("lat")
-    place = jnp.stack([lon, lat, jnp.int32(lat_count)]).astype(jnp.int32)
-
+    rows = piece_height.shape[1]
+    place = jnp.stack([lax.axis_index("lat"), jnp.int32(lat_count)]).astype(jnp.int32)
+
+    next_first = passed_along(piece_height[:, :1, :], "lat", -1)
     packed = pack(piece_column, piece_height, piece_weight, lon_count)
-    got = lax.all_to_all(packed, "lon", split_axis=0, concat_axis=0, tiled=True)
-
-    small = exchanged(small_messages(piece_height, piece_column, piece_width, lon), lon_count)
-    facts = small[:, CAPACITY, :2 * CAPACITY].astype(jnp.int32).reshape(-1)
-
-    rhs, diag, up, down, edge = sums(place, facts, got, small)
+    labelled = label(piece_column, piece_width, next_first, packed)
+    got = lax.all_to_all(labelled, "lon", split_axis=0, concat_axis=0, tiled=True)
+    facts = got[:, :, -1, 0, :2].astype(jnp.int32).reshape(-1)
+    got = got.reshape(lon_count * CAPACITY * (2 * rows + 2), BW)
+    rhs, diag, up, down, edge = sums(place, facts, got, rows)
     south = passed_along(up, "lat", 1)
     north = passed_along(down, "lat", -1)
     to_west = jnp.concatenate([edge[0], south[0], north[0]], axis=0)

time: 234 us -> 175 us (0.75)
  Pallas kernels: 77.4 us -> 18.2 us
  waiting for transfers between devices: 79.9 us -> 104 us
  starting transfers between devices: 46.6 us -> 24.4 us
    all_to_all x1, waiting for transfers between devices: 0.01 us -> 97 us  [body(): lax.all_to_all(labelled, 'lon', split_axis=0, concat_axis=0, tiled=True)]
    ppermute x10 -> x0, waiting for transfers between devices: 71.6 us -> none  [the longest x7 62.4 us: exchanged(): parts.append(lax.ppermute(message[far:far + NEAR], 'lon', route))]
    pallas_call x2 -> x3, Pallas kernels: 71.9 us -> 12.7 us  [the longest x1 6.54 us: sums(): pl.pallas_call(sums_kernel, grid=(slots // (2 * batch),), out_shape=[jax....]
    ppermute x10 -> x0, starting transfers between devices: 21.6 us -> none  [the longest x7 16.9 us: exchanged(): parts.append(lax.ppermute(message[far:far + NEAR], 'lon', route))]
  transfers between devices with their start and end apart: 16 -> 6, of which waited for: 11 -> 5; matrix products, arithmetic and copies ran while one was open for 1% -> 0% of each run, Pallas kernels for 0% -> 2%
where the time goes in v3:
time: 175 us
  waiting for transfers between devices  104 us (59%)
  blocking collectives  24.7 us (14%)
  starting transfers between devices  24.4 us (14%)
  Pallas kernels  18.2 us (10%)
  local copies, waits for them, and re-layouts  1.81 us (1%)
    all_to_all x1, waiting for transfers between devices, body(): lax.all_to_all(labelled, 'lon', split_axis=0, concat_axis=0, tiled=True)  97 us
    all_to_all x1, blocking collectives, body(): lax.all_to_all(spread, ('lon', 'lat'), split_axis=0, concat_axis=0, tiled...  24.7 us
    all_to_all x1, starting transfers between devices, body(): lax.all_to_all(labelled, 'lon', split_axis=0, concat_axis=0, tiled=True)  13.6 us
    pallas_call x1, Pallas kernels, sums(): pl.pallas_call(sums_kernel, grid=(slots // (2 * batch),), out_shape=[jax....  6.54 us
    ppermute x3, starting transfers between devices, passed_along(): return lax.ppermute(block, axis, route)  5.79 us
    ppermute x3, waiting for transfers between devices, passed_along(): return lax.ppermute(block, axis, route)  5.22 us
    ppermute x2, starting transfers between devices, passed_around(): lax.ppermute(block, axis, [(i, (i + distance) % count) for i in range(cou...  5.01 us
    pallas_call x1, Pallas kernels, basis(): pl.pallas_call(basis_kernel, out_shape=[jax.ShapeDtypeStruct((5, BLOCKS,...  3.58 us
  transfers between devices with their start and end apart: 6, of which 5 were waited for; matrix products, arithmetic and copies ran while one was open for 0% of the time, Pallas kernels for 2%

profile of v3, /device:TPU:1, one launch (start us, length us, event | category | flops | bytes accessed | tf_op | source)
XLA Modules:
  0.0 174.9 jit_solution(9905457466363264158)
XLA Ops:
  0.6 1.0 slice.24
  1.6 1.3 collective-permute-start
  2.9 3.2 %pack.1.packed_ref = f32[64,2,66,1,128]{4,3,2,1,0:T(1,128)} custom-call(s32[64]{0:T(128)} %column_ref.3, f32[64,32,1,128]{3,2,1,0:T(1,128)} %bitcast.20, f32[64,32,1,128]{3,2,1,0:T(1,128)} %bitcast.21), custom_call_target="tpu_custom_call" | custom-call | tf_op jit(solution)/shard_map/pack/pallas_call | solution.py:74
  6.1 0.8 collective-permute-done.source_ref
  6.9 0.0 copy-start
  6.9 0.6 copy-done
  7.5 3.0 %label.1 = f32[64,2,66,1,128]{4,3,2,1,0:T(1,128)} custom-call(s32[64]{0:T(128)} %column_ref.3, s32[64]{0:T(128)} %width_ref.1, f32[64,1,128]{2,1,0:T(1,128)} %copy-done, f32[64,2,66,1,128]{4,3,2,1,0:T(1,128)} %pack.1.packed_ref), custom_call_target="tpu_custom_call", output_to_operand_aliasing={{}: (3, {})} | custom-call | tf_op jit(solution)/shard_map/label/pallas_call | solution.py:126
  10.5 13.6 %all-to-all-start = ((f32[64,2,66,1,128]{4,3,2,1,0:T(1,128)}), f32[64,2,66,1,128]{4,3,2,1,0:T(1,128)}, u32[]{:S(2)}, u32[]{:S(2)}) async-start(f32[64,2,66,1,128]{4,3,2,1,0:T(1,128)} %label.1), calls=%async_computation | async-start | bytes 8650752 | tf_op jit(solution)/shard_map/all_to_all | solution.py:405
  24.2 0.1 pad_add_fusion.place_ref
  24.2 97.0 %all-to-all-done = f32[64,2,66,1,128]{4,3,2,1,0:T(1,128)} async-done(((f32[64,2,66,1,128]{4,3,2,1,0:T(1,128)}), f32[64,2,66,1,128]{4,3,2,1,0:T(1,128)}, u32[]{:S(2)}, u32[]{:S(2)}) %all-to-all-start) | async-done | bytes 4325408 | tf_op jit(solution)/shard_map/all_to_all | solution.py:405
  121.3 1.1 fusion
  122.3 0.1 convert_element_type.8.facts_ref
  122.5 6.5 %sums.1 = (f32[32,32,128]{2,1,0:T(8,128)S(1)}, f32[32,32,128]{2,1,0:T(8,128)S(1)}, f32[32,8,128]{2,1,0:T(8,128)S(1)}, f32[32,8,128]{2,1,0:T(8,128)S(1)}, f32[2,72,128]{2,1,0:T(8,128)S(1)}) custom-call(s32[2]{0:T(128)S(1)} %pad_add_fusion.place_ref, s32[256]{0:T(256)S(1)} %convert_element_type.8.facts_ref, f32[8448,128]{1,0:T(8,128)} %bitcast.3.got_ref), custom_call_target="tpu_custom_call" | custom-call | tf_op jit(solution)/shard_map/sums/pallas_call | solution.py:212
  129.0 3.2 %collective-permute-start.1 = (f32[32,8,128]{2,1,0:T(8,128)S(1)}, f32[32,8,128]{2,1,0:T(8,128)S(1)}, u32[]{:S(2)}, u32[]{:S(2)}) collective-permute-start(f32[32,8,128]{2,1,0:T(8,128)S(1)} %get-tuple-element.11.up_ref), channel_id=1, source_target_pairs={{0,1},{1,2},{2,3},{4,5},{5,6},{6,7},{8,9},{9,10},{10,11},{12,13},{... | collective-permute-start | bytes 393224 | tf_op jit(solution)/shard_map/ppermute | solution.py:28
  132.2 1.3 collective-permute-start.2
  133.6 0.6 collective-permute-done.1.south_ref
  134.2 3.8 %collective-permute-done.2.north_ref = f32[32,8,128]{2,1,0:T(8,128)S(1)} collective-permute-done((f32[32,8,128]{2,1,0:T(8,128)S(1)}, f32[32,8,128]{2,1,0:T(8,128)S(1)}, u32[]{:S(2)}, u32[]{:S(2)}) %collective-permute-start.2) | collective-permute-done | bytes 131104 | tf_op jit(solution)/shard_map/ppermute | solution.py:28
  138.0 3.9 %collective-permute-start.4 = (f32[88,128]{1,0:T(8,128)S(1)}, f32[88,128]{1,0:T(8,128)S(1)}, u32[]{:S(2)}, u32[]{:S(2)}) collective-permute-start(f32[88,128]{1,0:T(8,128)S(1)} %pad_maximum_fusion.1), channel_id=1, source_target_pairs={{0,252},{4,0},{8,4},{12,8},{16,12},{20,16},{24,20},{28,24},{32,28}... | collective-permute-start | bytes 135176 | tf_op jit(solution)/shard_map/ppermute | solution.py:33
  141.9 1.1 collective-permute-start.3
  143.0 1.6 collective-permute-done.4.east_ref
  144.6 0.0 collective-permute-done.3.west_ref
  144.6 3.6 %basis.1 = (f32[5,32,32,128]{3,2,1,0:T(8,128)S(1)}, f32[1,128]{1,0:T(1,128)S(1)}) custom-call(s32[2]{0:T(128)S(1)} %pad_add_fusion.place_ref, f32[32,32,128]{2,1,0:T(8,128)S(1)} %get-tuple-element.9.rhs_ref, f32[32,32,128]{2,1,0:T(8,128)S(1)} %get-tuple-element.10.diag_ref, f32[32,8,128]{2,1,0:T(8,128)S(1)} %get-tuple-element.11.up_ref, ...), custom_call_target="tpu_custom_call" | custom-call | tf_op jit(solution)/shard_map/basis/pallas_call | solution.py:304
  148.2 0.1 broadcast_in_dim.9
  148.3 24.7 %all_to_all.10 = f32[256,1,128]{2,1,0:T(1,128)S(1)} all-to-all(f32[256,1,128]{2,1,0:T(1,128)S(1)} %broadcast_in_dim.9), channel_id=1, replica_groups=mesh['lon'=64,'lat'=4] {'lon','lat'}, dimensions={0} | all-to-all | bytes 262144 | tf_op jit(solution)/shard_map/all_to_all | solution.py:417
  173.0 2.0 %combine.1 = (f32[32,4096]{1,0:T(8,128)}, f32[32,4096]{1,0:T(8,128)}) custom-call(f32[256,128]{1,0:T(8,128)S(1)} %bitcast.18, f32[5,32,32,128]{3,2,1,0:T(8,128)S(1)} %get-tuple-element.15.q_ref), custom_call_target="tpu_custom_call" | custom-call | tf_op jit(solution)/shard_map/combine/pallas_call | solution.py:382
  (5 shorter events, 0.0 us)
Async XLA Ops:
  1.6 5.3 %collective-permute-start = (f32[64,1,128]{2,1,0:T(1,128)S(1)}, f32[64,1,128]{2,1,0:T(1,128)S(1)}, u32[]{:S(2)}, u32[]{:S(2)}) collective-permute-start(f32[64,1,128]{2,1,0:T(1,128)S(1)} %slice.24), channel_id=1, source_target_pairs={{1,0},{2,1},{3,2},{5,4},{6,5},{7,6},{9,8},{10,9},{11,10},{13,12},{... | collective-permute-start | bytes 98312 | tf_op jit(solution)/shard_map/ppermute | solution.py:28
  6.9 0.6 copy-start
  10.5 110.7 %all-to-all-start = ((f32[64,2,66,1,128]{4,3,2,1,0:T(1,128)}), f32[64,2,66,1,128]{4,3,2,1,0:T(1,128)}, u32[]{:S(2)}, u32[]{:S(2)}) async-start(f32[64,2,66,1,128]{4,3,2,1,0:T(1,128)} %label.1), calls=%async_computation | async-start | bytes 8650752 | tf_op jit(solution)/shard_map/all_to_all | solution.py:405
  129.0 5.1 %collective-permute-start.1 = (f32[32,8,128]{2,1,0:T(8,128)S(1)}, f32[32,8,128]{2,1,0:T(8,128)S(1)}, u32[]{:S(2)}, u32[]{:S(2)}) collective-permute-start(f32[32,8,128]{2,1,0:T(8,128)S(1)} %get-tuple-element.11.up_ref), channel_id=1, source_target_pairs={{0,1},{1,2},{2,3},{4,5},{5,6},{6,7},{8,9},{9,10},{10,11},{12,13},{... | collective-permute-start | bytes 393224 | tf_op jit(solution)/shard_map/ppermute | solution.py:28
  132.2 5.7 %collective-permute-start.2 = (f32[32,8,128]{2,1,0:T(8,128)S(1)}, f32[32,8,128]{2,1,0:T(8,128)S(1)}, u32[]{:S(2)}, u32[]{:S(2)}) collective-permute-start(f32[32,8,128]{2,1,0:T(8,128)S(1)} %get-tuple-element.12), channel_id=1, source_target_pairs={{1,0},{2,1},{3,2},{5,4},{6,5},{7,6},{9,8},{10,9},{11,10},{13,12},{... | collective-permute-start | bytes 393224 | tf_op jit(solution)/shard_map/ppermute | solution.py:28
  138.0 6.6 %collective-permute-start.4 = (f32[88,128]{1,0:T(8,128)S(1)}, f32[88,128]{1,0:T(8,128)S(1)}, u32[]{:S(2)}, u32[]{:S(2)}) collective-permute-start(f32[88,128]{1,0:T(8,128)S(1)} %pad_maximum_fusion.1), channel_id=1, source_target_pairs={{0,252},{4,0},{8,4},{12,8},{16,12},{20,16},{24,20},{28,24},{32,28}... | collective-permute-start | bytes 135176 | tf_op jit(solution)/shard_map/ppermute | solution.py:33
  141.9 2.7 %collective-permute-start.3 = (f32[88,128]{1,0:T(8,128)S(1)}, f32[88,128]{1,0:T(8,128)S(1)}, u32[]{:S(2)}, u32[]{:S(2)}) collective-permute-start(f32[88,128]{1,0:T(8,128)S(1)} %pad_maximum_fusion), channel_id=1, source_target_pairs={{0,4},{4,8},{8,12},{12,16},{16,20},{20,24},{24,28},{28,32},{32,36}... | collective-permute-start | bytes 135176 | tf_op jit(solution)/shard_map/ppermute | solution.py:33

commit v4 on v3

v4 whole, which is shorter than its diff:
```python
import jax
import jax.numpy as jnp
from jax import lax
from jax.experimental import pallas as pl
from jax.experimental.pallas import tpu as pltpu
from jax.sharding import PartitionSpec as P

ROWS = 128
COLS_DEV = 4096
BW = 128
BLOCKS = COLS_DEV // BW
CAPACITY = 2

MU_DATA = 0.5
DAMPING = 0.5
RIDGE = 0.05

MID = 5.5
HALF = 5.5
VMEM_BYTES = 40 * 1024 * 1024
PACK_VMEM_BYTES = 60 * 1024 * 1024
SOME_VMEM_BYTES = 50 * 1024 * 1024
F32 = jnp.float32


def passed_along(block, axis, distance):
    devices = range(lax.axis_size(axis))
    route = [(i, i + distance) for i in devices if i + distance in devices]
    return lax.ppermute(block, axis, route)


def swapped(block, axis, start, around):
    count = lax.axis_size(axis)
    lows = range(start, count if around else count - 1, 2)
    pairs = [(low, (low + 1) % count) for low in lows]
    return lax.ppermute(block, axis, pairs + [(b, a) for a, b in pairs])


def pack_kernel(column_ref, width_ref, height_ref, weight_ref, out_ref, held_ref, facts_ref,
                count_ref, in_sem, out_sem, facts_sem):
    tiles, pieces = out_ref.shape[0], height_ref.shape[0]
    rows = height_ref.shape[1]
    batch = pieces // in_sem.shape[0]
    lane = lax.broadcasted_iota(jnp.int32, (1, BW), 1)

    def loads(g):
        part = pl.ds(g * batch, batch)
        sources = (height_ref, weight_ref)
        return [pltpu.make_async_copy(source.at[part], held_ref.at[part, pl.ds(n * rows, rows)],
                                      in_sem.at[g, n]) for n, source in enumerate(sources)]

    for g in range(in_sem.shape[0]):
        for load in loads(g):
            load.start()

    facts_ref[...] = jnp.zeros_like(facts_ref)

    @pl.loop(0, tiles, unroll=8)
    def _(t):
        count_ref[t] = 0

    for g in range(in_sem.shape[0]):
        for load in loads(g):
            load.wait()

        @pl.loop(g * batch, (g + 1) * batch, unroll=4)
        def _(p):
            tile = column_ref[p] // COLS_DEV
            block = column_ref[p] % COLS_DEV // BW
            slot = count_ref[tile]
            count_ref[tile] = slot + 1
            facts = jnp.where(lane == 0, block + 1, jnp.where(lane == 1, width_ref[p], 0))
            facts_ref[tile, slot] = facts.astype(F32)
            pltpu.make_async_copy(held_ref.at[p], out_ref.at[tile, slot, pl.ds(0, 2 * rows)],
                                  out_sem).start()

    facts = pltpu.make_async_copy(facts_ref, out_ref.at[:, :, 2 * rows + 1], facts_sem)
    facts.start()
    pltpu.make_async_copy(held_ref, out_ref.at[pl.ds(0, pieces), 0, pl.ds(0, 2 * rows)],
                          out_sem).wait()
    facts.wait()


def pack(piece_column, piece_width, piece_height, piece_weight, tiles, batches=8):
    pieces, rows, _ = piece_height.shape
    tall = lambda array: array.reshape(pieces, rows, 1, BW)
    return pl.pallas_call(
        pack_kernel,
        out_shape=jax.ShapeDtypeStruct((tiles, CAPACITY, 2 * rows + 2, 1, BW), F32),
        in_specs=[
            pl.BlockSpec(memory_space=pltpu.SMEM),
            pl.BlockSpec(memory_space=pltpu.SMEM),
            pl.BlockSpec(memory_space=pl.ANY),
            pl.BlockSpec(memory_space=pl.ANY),
        ],
        out_specs=pl.BlockSpec(memory_space=pl.ANY),
        scratch_shapes=[
            pltpu.VMEM((pieces, 2 * rows, 1, BW), F32),
            pltpu.VMEM((tiles, CAPACITY, 1, BW), F32),
            pltpu.SMEM((tiles,), jnp.int32),
            pltpu.SemaphoreType.DMA((batches, 2)),
            pltpu.SemaphoreType.DMA,
            pltpu.SemaphoreType.DMA,
        ],
        compiler_params=pltpu.CompilerParams(vmem_limit_bytes=PACK_VMEM_BYTES),
        name="pack",
    )(piece_column, piece_width, tall(piece_height), tall(piece_weight))


def label_kernel(column_ref, first_ref, packed_ref, out_ref, count_ref, sem):
    tiles, pieces = out_ref.shape[0], first_ref.shape[0]
    end = out_ref.shape[2]

    @pl.loop(0, tiles, unroll=8)
    def _(t):
        count_ref[t] = 0

    @pl.loop(0, pieces, unroll=8)
    def _(p):
        tile = column_ref[p] // COLS_DEV
        slot = count_ref[tile]
        count_ref[tile] = slot + 1
        pltpu.make_async_copy(first_ref.at[p], out_ref.at[tile, slot, end - 2], sem).start()

    pltpu.make_async_copy(first_ref, out_ref.at[pl.ds(0, pieces), 0, end - 2], sem).wait()


def label(piece_column, next_first, packed):
    return pl.pallas_call(
        label_kernel,
        out_shape=jax.ShapeDtypeStruct(packed.shape, F32),
        in_specs=[
            pl.BlockSpec(memory_space=pltpu.SMEM),
            pl.BlockSpec(memory_space=pltpu.VMEM),
            pl.BlockSpec(memory_space=pl.ANY),
        ],
        out_specs=pl.BlockSpec(memory_space=pl.ANY),
        scratch_shapes=[
            pltpu.SMEM(packed.shape[:1], jnp.int32),
            pltpu.SemaphoreType.DMA,
        ],
        input_output_aliases={2: 0},
        compiler_params=pltpu.CompilerParams(vmem_limit_bytes=SOME_VMEM_BYTES),
        name="label",
    )(piece_column, next_first, packed)


def sums_kernel(place_ref, got_ref, rows_ref, rhs_ref, diag_ref, one_ref, two_ref, edge_ref,
                held_ref, facts_ref, total_ref, facts_sem, sem):
    rows = rhs_ref.shape[1]
    part = 2 * rows + 2
    chunks, height, _ = held_ref.shape
    slots = height // part
    lat, lat_count, lon = place_ref[0], place_ref[1], place_ref[2]
    lane = lax.broadcasted_iota(jnp.int32, (rows, BW), 1)
    row = lax.broadcasted_iota(jnp.int32, (rows, BW), 0)

    def load(n):
        rows_of = rows_ref.at[pl.ds(n * height, height)]
        return pltpu.make_async_copy(rows_of, held_ref.at[n], sem.at[n])

    facts = pltpu.make_async_copy(got_ref.at[:, :, part - 1], facts_ref, facts_sem)
    facts.start()
    for n in range(chunks):
        load(n).start()
    total_ref[...] = jnp.zeros_like(total_ref)
    facts.wait()

    @pl.loop(0, chunks)
    def _(n):
        load(n).wait()
        for s in range(slots):
            source, slot = n * (slots // CAPACITY) + s // CAPACITY, s % CAPACITY
            block = facts_ref[source, slot, 0, 0].astype(jnp.int32) - 1
            block = jnp.where(block < 0, BLOCKS, block)
            width = facts_ref[source, slot, 0, 1].astype(jnp.int32)
            height = held_ref[n, s * part:s * part + rows]
            weight = held_ref[n, s * part + rows:s * part + 2 * rows]
            above = held_ref[n, s * part + 2 * rows:s * part + 2 * rows + 1]
            cell = jnp.where(lane < width, weight, 0.0)
            east = jnp.where(lane < width - 1, weight, 0.0)
            east_step = pltpu.roll(height, BW - 1, 1) - height
            raised = jnp.where(row == rows - 1, above, pltpu.roll(height, rows - 1, 0))
            terms = (cell, cell * height, east, east * east_step, cell * (raised - height))
            for k, term in enumerate(terms):
                total_ref[block, k] += term

    last = (row == rows - 1) & (lat == lat_count - 1)
    first = (row == 0) & (lat == 0)
    sides = 4.0 - last.astype(F32) - first.astype(F32) + RIDGE
    row8 = row[:8]
    lat_even = lat % 2 == 0

    @pl.loop(0, BLOCKS, unroll=4)
    def _(i):
        cell, height = total_ref[i, 0], total_ref[i, 1]
        east = total_ref[i, 3] / (total_ref[i, 2] + DAMPING)
        north = jnp.where(last, 0.0, total_ref[i, 4] / (cell + DAMPING))
        south = jnp.where(row == 0, 0.0, pltpu.roll(north, 1, 0))
        rhs = MU_DATA * height - (east - pltpu.roll(east, 1, 1)) - (north - south)
        diag = MU_DATA * cell + sides
        rhs_ref[i] = rhs
        diag_ref[i] = diag
        top = pltpu.roll(diag[rows - 8:], 4, 0)
        top = jnp.where(row8 == 0, pltpu.roll(north[rows - 8:], 1, 0), top)
        up = jnp.where(row8 >= 4, rhs[rows - 8:], top)
        down = jnp.where(row8 >= 4, pltpu.roll(diag[:8], 4, 0), rhs[:8])
        one_ref[i] = jnp.where(lat_even, up, down)
        two_ref[i] = jnp.where(lat_even, down, up)

    first_edge = (BLOCKS - 1) * (1 - lon % 2)
    for side, block in ((0, first_edge), (1, BLOCKS - 1 - first_edge)):
        edge_ref[side, 0:rows] = rhs_ref[block]
        edge_ref[side, rows:2 * rows] = diag_ref[block]
        up = jnp.where(lat_even, one_ref[block], two_ref[block])
        edge_ref[side, 2 * rows:2 * rows + 8] = up


def sums(place, got, rows, chunks=4):
    tiles, _, part, _, _ = got.shape
    height = tiles * CAPACITY * part // chunks
    field = (BLOCKS, rows, BW)
    strip = (BLOCKS, 8, BW)
    edge = (2, 2 * rows + 8, BW)
    vmem = pl.BlockSpec(memory_space=pltpu.VMEM)
    return pl.pallas_call(
        sums_kernel,
        out_shape=[jax.ShapeDtypeStruct(s, F32) for s in (field, field, strip, strip, edge)],
        in_specs=[
            pl.BlockSpec(memory_space=pltpu.SMEM),
            pl.BlockSpec(memory_space=pl.ANY),
            pl.BlockSpec(memory_space=pl.ANY),
        ],
        out_specs=[vmem] * 5,
        scratch_shapes=[
            pltpu.VMEM((chunks, height, BW), F32),
            pltpu.SMEM((tiles, CAPACITY, 1, BW), F32),
            pltpu.VMEM((BLOCKS + 1, 5, rows, BW), F32),
            pltpu.SemaphoreType.DMA,
            pltpu.SemaphoreType.DMA((chunks,)),
        ],
        compiler_params=pltpu.CompilerParams(vmem_limit_bytes=VMEM_BYTES),
        name="sums",
    )(place, got, got.reshape(chunks * height, BW))


PAIRS = [(i, j) for j in range(5) for i in range(min(j, 3) + 1)]


def basis_kernel(place_ref, rhs_ref, diag_ref, own_one_ref, own_two_ref, one_ref, two_ref,
                 lon_one_ref, lon_two_ref, q_ref, gram_ref, scale_ref, *v_refs):
    rows = rhs_ref.shape[1]
    tall = rows + 16
    lat, lat_count, lon = place_ref[0], place_ref[1], place_ref[2]
    lat_even = lat % 2 == 0
    row = lax.broadcasted_iota(jnp.int32, (rows, BW), 0)
    row8 = row[:8]
    lane = lax.broadcasted_iota(jnp.int32, (tall, BW), 1)

    def assemble(i, rhs, diag, up, one, two):
        south = jnp.where(lat_even, two, one)
        north = jnp.where(lat_even, one, two)
        first = jnp.where(row == 0, south[0:1], 0.0) + rhs
        below = jnp.where(row8 >= 4, south, 0.0)
        above = jnp.where(row8 == 0, north + up, jnp.where(row8 < 4, north, 0.0))
        v_refs[0][i, 8:8 + tall] = jnp.concatenate([below, first, above], axis=0)
        diag = jnp.concatenate([pltpu.roll(south, 4, 0), diag, pltpu.roll(north, 4, 0)], axis=0)
        scale_ref[i] = (diag - MID) * (2.0 / HALF)

    side = (BLOCKS + 1) * (1 - lon % 2)
    for i, ref in ((side, lon_one_ref), (BLOCKS + 1 - side, lon_two_ref)):
        two = 2 * rows
        assemble(i, ref[0:rows], ref[rows:two], ref[two:two + 8], ref[two + 8:two + 16],
                 ref[two + 16:two + 24])

    @pl.loop(0, BLOCKS, unroll=4)
    def _(i):
        up = jnp.where(lat_even, own_one_ref[i], own_two_ref[i])
        assemble(i + 1, rhs_ref[i], diag_ref[i], up, one_ref[i], two_ref[i])

    def applied(k, i):
        body = slice(8, 8 + tall)
        v = v_refs[k][i, body]
        left = v_refs[k][jnp.maximum(i - 1, 0), body]
        right = v_refs[k][jnp.minimum(i + 1, BLOCKS + 1), body]
        west = pltpu.roll(jnp.where(lane == BW - 1, left, v), 1, 1)
        east = pltpu.roll(jnp.where(lane == 0, right, v), BW - 1, 1)
        south = v_refs[k][i, 7:7 + tall]
        north = v_refs[k][i, 9:9 + tall]
        image = scale_ref[i] * v - (2.0 / HALF) * ((west + east) + (south + north))
        if k == 0:
            image = 0.5 * image
        else:
            image = image - v_refs[k - 1][i, body]
        ends = (jnp.where(lat > 0, image[:8], 0.0), image[8:rows + 8],
                jnp.where(lat < lat_count - 1, image[rows + 8:], 0.0))
        return jnp.concatenate(ends, axis=0)

    for k in range(3):
        @pl.loop(0, BLOCKS + 2, unroll=17)
        def _(i, k=k):
            v_refs[k + 1][i, 8:8 + tall] = applied(k, i)

    def products(i, carry):
        last = applied(3, i + 1)[8:8 + rows]
        q = [v_refs[k][i + 1, 16:16 + rows] for k in range(4)] + [last]
        for k in range(5):
            q_ref[k, i] = q[k]
        out = []
        for total, (a, b) in zip(carry, PAIRS):
            term = q[a] * q[b]
            out.append(total + sum(term[8 * n:8 * n + 8] for n in range(rows // 8)))
        return tuple(out)

    zero = tuple(jnp.zeros((8, BW), F32) for _ in PAIRS)
    totals = lax.fori_loop(0, BLOCKS, products, zero, unroll=4)
    lane1 = lax.broadcasted_iota(jnp.int32, (1, BW), 1)
    gram = jnp.zeros((1, BW), F32)
    for n, total in enumerate(totals):
        value = jnp.sum(jnp.sum(total, axis=0, keepdims=True), axis=1, keepdims=True)
        gram = jnp.where(lane1 == n, value, gram)
    gram_ref[...] = gram


def basis(place, rhs, diag, *strips):
    rows = rhs.shape[1]
    vmem = pl.BlockSpec(memory_space=pltpu.VMEM)
    return pl.pallas_call(
        basis_kernel,
        out_shape=[
            jax.ShapeDtypeStruct((5, BLOCKS, rows, BW), F32),
            jax.ShapeDtypeStruct((1, BW), F32),
        ],
        in_specs=[pl.BlockSpec(memory_space=pltpu.SMEM)] + [vmem] * 8,
        out_specs=[vmem, vmem],
        scratch_shapes=[
            pltpu.VMEM((BLOCKS + 2, rows + 16, BW), F32),
        ] + [pltpu.VMEM((BLOCKS + 2, rows + 32, BW), F32)] * 4,
        compiler_params=pltpu.CompilerParams(vmem_limit_bytes=VMEM_BYTES),
        name="basis",
    )(place, rhs, diag, *strips)


def solved(gram):
    g = {}
    for n, (a, b) in enumerate(PAIRS):
        g[a, b] = g[b, a] = gram[n]
    m = [[None] * 4 for _ in range(4)]
    for j in range(4):
        for i in range(j + 1):
            if j == 0:
                value = MID * g[i, 0] + HALF * g[i, 1]
            else:
                value = MID * g[i, j] + (0.5 * HALF) * (g[i, j + 1] + g[i, j - 1])
            m[i][j] = m[j][i] = value
    y = [g[0, i] for i in range(4)]
    inverse = []
    factor = [[None] * 4 for _ in range(4)]
    for k in range(4):
        pivot = m[k][k]
        inverse.append(jnp.where(pivot > 0.0, 1.0 / jnp.where(pivot > 0.0, pivot, 1.0), 0.0))
        for i in range(k + 1, 4):
            factor[i][k] = m[k][i] * inverse[k]
        for i in range(k + 1, 4):
            for j in range(i, 4):
                m[i][j] = m[i][j] - factor[i][k] * m[k][j]
            y[i] = y[i] - factor[i][k] * y[k]
    c = [y[k] * inverse[k] for k in range(4)]
    for k in range(3, -1, -1):
        for i in range(k):
            c[i] = c[i] - factor[k][i] * c[k]
    half = 0.5 * HALF
    r = [
        1.0 - (MID * c[0] + half * c[1]),
        -(HALF * c[0] + MID * c[1] + half * c[2]),
        -(half * c[1] + MID * c[2] + half * c[3]),
        -(half * c[2] + MID * c[3]),
        -(half * c[3]),
    ]
    return c, r


def combine_kernel(gram_ref, q_ref, x_ref, r_ref, c_ref):
    @pl.when(pl.program_id(0) == 0)
    def _():
        gram = jnp.sum(gram_ref[...], axis=0, keepdims=True)
        lane = lax.broadcasted_iota(jnp.int32, (1, BW), 1)
        pick = lambda n: jnp.sum(jnp.where(lane == n, gram, 0.0), axis=1, keepdims=True)
        c, r = solved([pick(n) for n in range(len(PAIRS))])
        for n, value in enumerate(c + r):
            c_ref[n] = jnp.broadcast_to(value, (8, BW))

    rows = q_ref.shape[2]
    factors = [jnp.concatenate([c_ref[n]] * (rows // 8), axis=0) for n in range(9)]
    for i in range(q_ref.shape[1]):
        q = [q_ref[k, i] for k in range(5)]
        columns = slice(i * BW, (i + 1) * BW)
        x_ref[:, columns] = sum(factors[k] * q[k] for k in range(4))
        r_ref[:, columns] = sum(factors[4 + k] * q[k] for k in range(5))


def combine(gram, q, batch=8):
    _, blocks, rows, _ = q.shape
    out = jax.ShapeDtypeStruct((rows, blocks * BW), F32)
    spec = pl.BlockSpec((rows, batch * BW), lambda i: (0, i))
    return pl.pallas_call(
        combine_kernel,
        grid=(blocks // batch,),
        out_shape=[out, out],
        in_specs=[
            pl.BlockSpec(gram.shape, lambda i: (0, 0)),
            pl.BlockSpec((5, batch, rows, BW), lambda i: (0, i, 0, 0)),
        ],
        out_specs=[spec, spec],
        scratch_shapes=[pltpu.VMEM((9, 8, BW), F32)],
        compiler_params=pltpu.CompilerParams(vmem_limit_bytes=VMEM_BYTES),
        name="combine",
    )(gram, q)


def body(piece_height, piece_weight, piece_column, piece_width):
    lon_count, lat_count = lax.axis_size("lon"), lax.axis_size("lat")
    rows = piece_height.shape[1]
    lon, lat = lax.axis_index("lon"), lax.axis_index("lat")
    place = jnp.stack([lat, jnp.int32(lat_count), lon]).astype(jnp.int32)

    next_first = passed_along(piece_height[:, :1, :], "lat", -1)
    packed = pack(piece_column, piece_width, piece_height, piece_weight, lon_count)
    labelled = label(piece_column, next_first, packed)
    got = lax.all_to_all(labelled, "lon", split_axis=0, concat_axis=0, tiled=True)
    rhs, diag, own_one, own_two, edge = sums(place, got, rows)

    one = swapped(own_one, "lat", 0, False)
    two = swapped(own_two, "lat", 1, False)
    first_edge = (BLOCKS - 1) * (1 - lon % 2)
    strips = []
    for start, block in ((0, first_edge), (1, BLOCKS - 1 - first_edge)):
        pick = lambda strip: lax.dynamic_index_in_dim(strip, block, 0, keepdims=False)
        message = jnp.concatenate([edge[start], pick(one), pick(two)], axis=0)
        strips.append(swapped(message, "lon", start, True))
    q, gram = basis(place, rhs, diag, own_one, own_two, one, two, *strips)
    spread = jnp.broadcast_to(gram[None], (lon_count * lat_count, 1, BW))
    grams = lax.all_to_all(spread, ("lon", "lat"), split_axis=0, concat_axis=0, tiled=True)
    return tuple(combine(grams.reshape(lon_count * lat_count, BW), q))


def solution(mesh):
    return jax.shard_map(
        body,
        mesh=mesh,
        in_specs=(P("lon", "lat", None), P("lon", "lat", None), P("lon"), P("lon")),
        out_specs=(P("lat", "lon"), P("lat", "lon")),
        check_vma=False,
    )
```

time: 175 us -> 168 us (0.960)
  Pallas kernels: 18.2 us -> 15.6 us
  starting transfers between devices: 24.4 us -> 21.9 us
  blocking collectives: 24.7 us -> 26.7 us
  waiting for transfers between devices: 104 us -> 102 us
    ppermute x3 -> x1, waiting for transfers between devices: 5.22 us -> 0.54 us  [passed_along(): return lax.ppermute(block, axis, route)]
    ppermute x3 -> x1, starting transfers between devices: 5.79 us -> 1.29 us  [passed_along(): return lax.ppermute(block, axis, route)]
    ppermute x2 -> x4, waiting for transfers between devices: 1.63 us -> 4.12 us  [swapped(): return lax.ppermute(block, axis, pairs + [(b, a) for a, b in pairs])]
    all_to_all x1, blocking collectives: 24.7 us -> 26.7 us  [body(): lax.all_to_all(spread, ('lon', 'lat'), split_axis=0, concat_axis=0, tiled...]
    ppermute x2 -> x4, starting transfers between devices: 5.01 us -> 6.93 us  [swapped(): return lax.ppermute(block, axis, pairs + [(b, a) for a, b in pairs])]
  transfers between devices with their start and end apart: 6 -> 6, of which waited for: 5 -> 4; matrix products, arithmetic and copies ran while one was open for 0% -> 0% of each run, Pallas kernels for 2% -> 2%
where the time goes in v4:
time: 168 us
  waiting for transfers between devices  102 us (61%)
  blocking collectives  26.7 us (16%)
  starting transfers between devices  21.9 us (13%)
  Pallas kernels  15.6 us (9%)
    all_to_all x1, waiting for transfers between devices, body(): lax.all_to_all(labelled, 'lon', split_axis=0, concat_axis=0, tiled=True)  97 us
    all_to_all x1, blocking collectives, body(): lax.all_to_all(spread, ('lon', 'lat'), split_axis=0, concat_axis=0, tiled...  26.7 us
    all_to_all x1, starting transfers between devices, body(): lax.all_to_all(labelled, 'lon', split_axis=0, concat_axis=0, tiled=True)  13.6 us
    ppermute x4, starting transfers between devices, swapped(): return lax.ppermute(block, axis, pairs + [(b, a) for a, b in pairs])  6.93 us
    pallas_call x1, Pallas kernels, sums(): pl.pallas_call(sums_kernel, out_shape=[jax.ShapeDtypeStruct(s, F32) for s...  4.82 us
    ppermute x4, waiting for transfers between devices, swapped(): return lax.ppermute(block, axis, pairs + [(b, a) for a, b in pairs])  4.12 us
    pallas_call x1, Pallas kernels, basis(): pl.pallas_call(basis_kernel, out_shape=[jax.ShapeDtypeStruct((5, BLOCKS,...  3.58 us
    pallas_call x1, Pallas kernels, pack(): pl.pallas_call(pack_kernel, out_shape=jax.ShapeDtypeStruct((tiles, CAPACI...  3.49 us
  transfers between devices with their start and end apart: 6, of which 4 were waited for; matrix products, arithmetic and copies ran while one was open for 0% of the time, Pallas kernels for 2%

profile of v4, /device:TPU:1, one launch (start us, length us, event | category | flops | bytes accessed | tf_op | source)
XLA Modules:
  0.0 167.8 jit_solution(2677414841072246637)
XLA Ops:
  0.6 0.0 copy-start
  0.6 1.0 slice.9
  1.6 1.3 collective-permute-start
  2.9 3.5 %pack.1.packed_ref = f32[64,2,66,1,128]{4,3,2,1,0:T(1,128)} custom-call(s32[64]{0:T(128)} %column_ref.3, s32[64]{0:T(128)} %width_ref.1, f32[64,32,1,128]{3,2,1,0:T(1,128)} %bitcast.21, f32[64,32,1,128]{3,2,1,0:T(1,128)} %bitcast.22), custom_call_target="tpu_custom_call" | custom-call | tf_op jit(solution)/shard_map/pack/pallas_call | solution.py:87
  6.4 0.5 collective-permute-done.first_ref
  6.9 0.0 copy-done
  7.0 1.8 %label.1 = f32[64,2,66,1,128]{4,3,2,1,0:T(1,128)} custom-call(s32[64]{0:T(128)S(1)} %copy-done, f32[64,1,128]{2,1,0:T(1,128)S(1)} %collective-permute-done.first_ref, f32[64,2,66,1,128]{4,3,2,1,0:T(1,128)} %pack.1.packed_ref), custom_call_target="tpu_custom_call", output_to_operand_aliasing={{}: (2, {})} | custom-call | tf_op jit(solution)/shard_map/label/pallas_call | solution.py:129
  8.7 13.6 %all-to-all-start = ((f32[64,2,66,1,128]{4,3,2,1,0:T(1,128)}), f32[64,2,66,1,128]{4,3,2,1,0:T(1,128)}, u32[]{:S(2)}, u32[]{:S(2)}) async-start(f32[64,2,66,1,128]{4,3,2,1,0:T(1,128)} %label.1), calls=%async_computation | async-start | bytes 8650752 | tf_op jit(solution)/shard_map/all_to_all | solution.py:430
  22.4 0.1 pad_add_fusion.place_ref
  22.5 97.0 %all-to-all-done.got_ref = f32[64,2,66,1,128]{4,3,2,1,0:T(1,128)} async-done(((f32[64,2,66,1,128]{4,3,2,1,0:T(1,128)}), f32[64,2,66,1,128]{4,3,2,1,0:T(1,128)}, u32[]{:S(2)}, u32[]{:S(2)}) %all-to-all-start) | async-done | bytes 4325408 | tf_op jit(solution)/shard_map/all_to_all | solution.py:430
  119.5 4.8 %sums.1 = (f32[32,32,128]{2,1,0:T(8,128)S(1)}, f32[32,32,128]{2,1,0:T(8,128)S(1)}, f32[32,8,128]{2,1,0:T(8,128)S(1)}, f32[32,8,128]{2,1,0:T(8,128)S(1)}, f32[2,72,128]{2,1,0:T(8,128)S(1)}) custom-call(s32[3]{0:T(128)S(1)} %pad_add_fusion.place_ref, f32[64,2,66,1,128]{4,3,2,1,0:T(1,128)} %all-to-all-done.got_ref, f32[8448,128]{1,0:T(8,128)} %bitcast.4.rows_ref), custom_call_target="tpu_custom_call" | custom-call | tf_op jit(solution)/shard_map/sums/pallas_call | solution.py:226
  124.3 1.4 collective-permute-start.1
  125.8 0.7 collective-permute-start.2
  126.4 0.0 collective-permute-done.2.two_ref
  126.5 1.7 %collective-permute-done.1.one_ref = f32[32,8,128]{2,1,0:T(8,128)S(1)} collective-permute-done((f32[32,8,128]{2,1,0:T(8,128)S(1)}, f32[32,8,128]{2,1,0:T(8,128)S(1)}, u32[]{:S(2)}, u32[]{:S(2)}) %collective-permute-start.1) | collective-permute-done | bytes 131104 | tf_op jit(solution)/shard_map/ppermute | solution.py:36
  128.2 3.7 %collective-permute-start.3 = (f32[88,128]{1,0:T(8,128)S(1)}, f32[88,128]{1,0:T(8,128)S(1)}, u32[]{:S(2)}, u32[]{:S(2)}) collective-permute-start(f32[88,128]{1,0:T(8,128)S(1)} %pad_maximum_fusion), channel_id=1, source_target_pairs={{0,4},{8,12},{16,20},{24,28},{32,36},{40,44},{48,52},{56,60},{64,6... | collective-permute-start | bytes 135176 | tf_op jit(solution)/shard_map/ppermute | solution.py:36
  131.9 1.1 collective-permute-start.4
  133.1 0.0 collective-permute-done.3.lon_one_ref
  133.1 2.4 %collective-permute-done.4.lon_two_ref = f32[88,128]{1,0:T(8,128)S(1)} collective-permute-done((f32[88,128]{1,0:T(8,128)S(1)}, f32[88,128]{1,0:T(8,128)S(1)}, u32[]{:S(2)}, u32[]{:S(2)}) %collective-permute-start.4) | collective-permute-done | bytes 45088 | tf_op jit(solution)/shard_map/ppermute | solution.py:36
  135.4 3.6 %basis.1 = (f32[5,32,32,128]{3,2,1,0:T(8,128)S(1)}, f32[1,128]{1,0:T(1,128)S(1)}) custom-call(s32[3]{0:T(128)S(1)} %pad_add_fusion.place_ref, f32[32,32,128]{2,1,0:T(8,128)S(1)} %get-tuple-element.9.rhs_ref, f32[32,32,128]{2,1,0:T(8,128)S(1)} %get-tuple-element.10.diag_ref, f32[32,8,128]{2,1,0:T(8,128)S(1)} %get-tuple-element.11.own_one_ref, ...), custom_call_target="tpu_custom_call" | custom-call | tf_op jit(solution)/shard_map/basis/pallas_call | solution.py:328
  139.0 0.1 broadcast_in_dim.9
  139.1 26.7 %all_to_all.10 = f32[256,1,128]{2,1,0:T(1,128)S(1)} all-to-all(f32[256,1,128]{2,1,0:T(1,128)S(1)} %broadcast_in_dim.9), channel_id=1, replica_groups=mesh['lon'=64,'lat'=4] {'lon','lat'}, dimensions={0} | all-to-all | bytes 262144 | tf_op jit(solution)/shard_map/all_to_all | solution.py:443
  165.8 2.0 %combine.1 = (f32[32,4096]{1,0:T(8,128)}, f32[32,4096]{1,0:T(8,128)}) custom-call(f32[256,128]{1,0:T(8,128)S(1)} %bitcast.19, f32[5,32,32,128]{3,2,1,0:T(8,128)S(1)} %get-tuple-element.15.q_ref), custom_call_target="tpu_custom_call" | custom-call | tf_op jit(solution)/shard_map/combine/pallas_call | solution.py:406
  (5 shorter events, 0.0 us)
Async XLA Ops:
  0.6 6.3 %copy-start = (s32[64]{0:T(128)S(1)}, s32[64]{0:T(128)}, u32[]{:S(2)}) copy-start(s32[64]{0:T(128)} %column_ref.3) | copy-start | bytes 772
  1.6 5.3 %collective-permute-start = (f32[64,1,128]{2,1,0:T(1,128)S(1)}, f32[64,1,128]{2,1,0:T(1,128)S(1)}, u32[]{:S(2)}, u32[]{:S(2)}) collective-permute-start(f32[64,1,128]{2,1,0:T(1,128)S(1)} %slice.9), channel_id=1, source_target_pairs={{1,0},{2,1},{3,2},{5,4},{6,5},{7,6},{9,8},{10,9},{11,10},{13,12},{... | collective-permute-start | bytes 98312 | tf_op jit(solution)/shard_map/ppermute | solution.py:29
  8.7 110.7 %all-to-all-start = ((f32[64,2,66,1,128]{4,3,2,1,0:T(1,128)}), f32[64,2,66,1,128]{4,3,2,1,0:T(1,128)}, u32[]{:S(2)}, u32[]{:S(2)}) async-start(f32[64,2,66,1,128]{4,3,2,1,0:T(1,128)} %label.1), calls=%async_computation | async-start | bytes 8650752 | tf_op jit(solution)/shard_map/all_to_all | solution.py:430
  124.3 3.9 %collective-permute-start.1 = (f32[32,8,128]{2,1,0:T(8,128)S(1)}, f32[32,8,128]{2,1,0:T(8,128)S(1)}, u32[]{:S(2)}, u32[]{:S(2)}) collective-permute-start(f32[32,8,128]{2,1,0:T(8,128)S(1)} %get-tuple-element.11.own_one_ref), channel_id=1, source_target_pairs={{0,1},{2,3},{1,0},{3,2},{4,5},{6,7},{5,4},{7,6},{8,9},{10,11},{9,8... | collective-permute-start | bytes 393224 | tf_op jit(solution)/shard_map/ppermute | solution.py:36
  125.8 0.7 collective-permute-start.2
  128.2 4.8 %collective-permute-start.3 = (f32[88,128]{1,0:T(8,128)S(1)}, f32[88,128]{1,0:T(8,128)S(1)}, u32[]{:S(2)}, u32[]{:S(2)}) collective-permute-start(f32[88,128]{1,0:T(8,128)S(1)} %pad_maximum_fusion), channel_id=1, source_target_pairs={{0,4},{8,12},{16,20},{24,28},{32,36},{40,44},{48,52},{56,60},{64,6... | collective-permute-start | bytes 135176 | tf_op jit(solution)/shard_map/ppermute | solution.py:36
  131.9 3.5 %collective-permute-start.4 = (f32[88,128]{1,0:T(8,128)S(1)}, f32[88,128]{1,0:T(8,128)S(1)}, u32[]{:S(2)}, u32[]{:S(2)}) collective-permute-start(f32[88,128]{1,0:T(8,128)S(1)} %pad_maximum_fusion.1), channel_id=1, source_target_pairs={{4,8},{12,16},{20,24},{28,32},{36,40},{44,48},{52,56},{60,64},{68,... | collective-permute-start | bytes 135176 | tf_op jit(solution)/shard_map/ppermute | solution.py:36

commit v5 on v4

--- a/solution.py
+++ b/solution.py
@@ -15,8 +15,7 @@
 DAMPING = 0.5
 RIDGE = 0.05
 
-MID = 5.5
-HALF = 5.5
+MID = 4.0
 VMEM_BYTES = 40 * 1024 * 1024
 PACK_VMEM_BYTES = 60 * 1024 * 1024
 SOME_VMEM_BYTES = 50 * 1024 * 1024
@@ -40,6 +39,7 @@
                 count_ref, in_sem, out_sem, facts_sem):
     tiles, pieces = out_ref.shape[0], height_ref.shape[0]
     rows = height_ref.shape[1]
+    part = 2 * rows
     batch = pieces // in_sem.shape[0]
     lane = lax.broadcasted_iota(jnp.int32, (1, BW), 1)
 
@@ -69,15 +69,15 @@
             block = column_ref[p] % COLS_DEV // BW
             slot = count_ref[tile]
             count_ref[tile] = slot + 1
-            facts = jnp.where(lane == 0, block + 1, jnp.where(lane == 1, width_ref[p], 0))
-            facts_ref[tile, slot] = facts.astype(F32)
-            pltpu.make_async_copy(held_ref.at[p], out_ref.at[tile, slot, pl.ds(0, 2 * rows)],
+            at = 2 * slot
+            facts = jnp.where(lane == at, block + 1, jnp.where(lane == at + 1, width_ref[p], 0))
+            facts_ref[tile] += facts.astype(F32)
+            pltpu.make_async_copy(held_ref.at[p], out_ref.at[tile, pl.ds(slot * part, part)],
                                   out_sem).start()
 
-    facts = pltpu.make_async_copy(facts_ref, out_ref.at[:, :, 2 * rows + 1], facts_sem)
+    facts = pltpu.make_async_copy(facts_ref, out_ref.at[:, CAPACITY * (part + 1)], facts_sem)
     facts.start()
-    pltpu.make_async_copy(held_ref, out_ref.at[pl.ds(0, pieces), 0, pl.ds(0, 2 * rows)],
-                          out_sem).wait()
+    pltpu.make_async_copy(held_ref, out_ref.at[pl.ds(0, pieces), pl.ds(0, part)], out_sem).wait()
     facts.wait()
 
 
@@ -86,7 +86,7 @@
     tall = lambda array: array.reshape(pieces, rows, 1, BW)
     return pl.pallas_call(
         pack_kernel,
-        out_shape=jax.ShapeDtypeStruct((tiles, CAPACITY, 2 * rows + 2, 1, BW), F32),
+        out_shape=jax.ShapeDtypeStruct((tiles, CAPACITY * (2 * rows + 1) + 1, 1, BW), F32),
         in_specs=[
             pl.BlockSpec(memory_space=pltpu.SMEM),
             pl.BlockSpec(memory_space=pltpu.SMEM),
@@ -96,7 +96,7 @@
         out_specs=pl.BlockSpec(memory_space=pl.ANY),
         scratch_shapes=[
             pltpu.VMEM((pieces, 2 * rows, 1, BW), F32),
-            pltpu.VMEM((tiles, CAPACITY, 1, BW), F32),
+            pltpu.VMEM((tiles, 1, BW), F32),
             pltpu.SMEM((tiles,), jnp.int32),
             pltpu.SemaphoreType.DMA((batches, 2)),
             pltpu.SemaphoreType.DMA,
@@ -109,7 +109,7 @@
 
 def label_kernel(column_ref, first_ref, packed_ref, out_ref, count_ref, sem):
     tiles, pieces = out_ref.shape[0], first_ref.shape[0]
-    end = out_ref.shape[2]
+    first = out_ref.shape[1] - CAPACITY - 1
 
     @pl.loop(0, tiles, unroll=8)
     def _(t):
@@ -120,9 +120,9 @@
         tile = column_ref[p] // COLS_DEV
         slot = count_ref[tile]
         count_ref[tile] = slot + 1
-        pltpu.make_async_copy(first_ref.at[p], out_ref.at[tile, slot, end - 2], sem).start()
-
-    pltpu.make_async_copy(first_ref, out_ref.at[pl.ds(0, pieces), 0, end - 2], sem).wait()
+        pltpu.make_async_copy(first_ref.at[p], out_ref.at[tile, first + slot], sem).start()
+
+    pltpu.make_async_copy(first_ref, out_ref.at[pl.ds(0, pieces), first], sem).wait()
 
 
 def label(piece_column, next_first, packed):
@@ -148,9 +148,10 @@
 def sums_kernel(place_ref, got_ref, rows_ref, rhs_ref, diag_ref, one_ref, two_ref, edge_ref,
                 held_ref, facts_ref, total_ref, facts_sem, sem):
     rows = rhs_ref.shape[1]
-    part = 2 * rows + 2
+    part = 2 * rows
+    message = CAPACITY * (part + 1) + 1
     chunks, height, _ = held_ref.shape
-    slots = height // part
+    sources = height // message
     lat, lat_count, lon = place_ref[0], place_ref[1], place_ref[2]
     lane = lax.broadcasted_iota(jnp.int32, (rows, BW), 1)
     row = lax.broadcasted_iota(jnp.int32, (rows, BW), 0)
@@ -159,7 +160,7 @@
         rows_of = rows_ref.at[pl.ds(n * height, height)]
         return pltpu.make_async_copy(rows_of, held_ref.at[n], sem.at[n])
 
-    facts = pltpu.make_async_copy(got_ref.at[:, :, part - 1], facts_ref, facts_sem)
+    facts = pltpu.make_async_copy(got_ref.at[:, message - 1], facts_ref, facts_sem)
     facts.start()
     for n in range(chunks):
         load(n).start()
@@ -169,14 +170,16 @@
     @pl.loop(0, chunks)
     def _(n):
         load(n).wait()
-        for s in range(slots):
-            source, slot = n * (slots // CAPACITY) + s // CAPACITY, s % CAPACITY
-            block = facts_ref[source, slot, 0, 0].astype(jnp.int32) - 1
+        for s in range(sources * CAPACITY):
+            source, slot = s // CAPACITY, s % CAPACITY
+            block = facts_ref[n * sources + source, 0, 2 * slot].astype(jnp.int32) - 1
             block = jnp.where(block < 0, BLOCKS, block)
-            width = facts_ref[source, slot, 0, 1].astype(jnp.int32)
-            height = held_ref[n, s * part:s * part + rows]
-            weight = held_ref[n, s * part + rows:s * part + 2 * rows]
-            above = held_ref[n, s * part + 2 * rows:s * part + 2 * rows + 1]
+            width = facts_ref[n * sources + source, 0, 2 * slot + 1].astype(jnp.int32)
+            base = source * message
+            start, first = base + slot * part, base + CAPACITY * part + slot
+            height = held_ref[n, start:start + rows]
+            weight = held_ref[n, start + rows:start + part]
+            above = held_ref[n, first:first + 1]
             cell = jnp.where(lane < width, weight, 0.0)
             east = jnp.where(lane < width - 1, weight, 0.0)
             east_step = pltpu.roll(height, BW - 1, 1) - height
@@ -216,9 +219,9 @@
         edge_ref[side, 2 * rows:2 * rows + 8] = up
 
 
-def sums(place, got, rows, chunks=4):
-    tiles, _, part, _, _ = got.shape
-    height = tiles * CAPACITY * part // chunks
+def sums(place, got, rows, chunks=2):
+    tiles, message, _, _ = got.shape
+    height = tiles * message // chunks
     field = (BLOCKS, rows, BW)
     strip = (BLOCKS, 8, BW)
     edge = (2, 2 * rows + 8, BW)
@@ -234,7 +237,7 @@
         out_specs=[vmem] * 5,
         scratch_shapes=[
             pltpu.VMEM((chunks, height, BW), F32),
-            pltpu.SMEM((tiles, CAPACITY, 1, BW), F32),
+            pltpu.SMEM((tiles, 1, BW), F32),
             pltpu.VMEM((BLOCKS + 1, 5, rows, BW), F32),
             pltpu.SemaphoreType.DMA,
             pltpu.SemaphoreType.DMA((chunks,)),
@@ -244,7 +247,36 @@
     )(place, got, got.reshape(chunks * height, BW))
 
 
+def two_sum(a, b):
+    total = a + b
+    part = total - a
+    return total, (a - (total - part)) + (b - part)
+
+
+def pair_sum(high, low, other_high, other_low):
+    total, error = two_sum(high, other_high)
+    return total, low + other_low + error
+
+
+def two_product(a, b):
+    def split(x):
+        big = 4097.0 * x
+        top = big - (big - x)
+        return top, x - top
+
+    product = a * b
+    (a_top, a_end), (b_top, b_end) = split(a), split(b)
+    return product, ((a_top * b_top - product) + a_top * b_end + a_end * b_top) + a_end * b_end
+
+
+def all_rows(high, low):
+    for shift in (4, 2, 1):
+        high, low = pair_sum(high, low, pltpu.roll(high, shift, 0), pltpu.roll(low, shift, 0))
+    return high, low
+
+
 PAIRS = [(i, j) for j in range(5) for i in range(min(j, 3) + 1)]
+LOW = 16
 
 
 def basis_kernel(place_ref, rhs_ref, diag_ref, own_one_ref, own_two_ref, one_ref, two_ref,
@@ -265,7 +297,7 @@
         above = jnp.where(row8 == 0, north + up, jnp.where(row8 < 4, north, 0.0))
         v_refs[0][i, 8:8 + tall] = jnp.concatenate([below, first, above], axis=0)
         diag = jnp.concatenate([pltpu.roll(south, 4, 0), diag, pltpu.roll(north, 4, 0)], axis=0)
-        scale_ref[i] = (diag - MID) * (2.0 / HALF)
+        scale_ref[i] = (diag - MID) * 0.125
 
     side = (BLOCKS + 1) * (1 - lon % 2)
     for i, ref in ((side, lon_one_ref), (BLOCKS + 1 - side, lon_two_ref)):
@@ -287,17 +319,17 @@
         east = pltpu.roll(jnp.where(lane == 0, right, v), BW - 1, 1)
         south = v_refs[k][i, 7:7 + tall]
         north = v_refs[k][i, 9:9 + tall]
-        image = scale_ref[i] * v - (2.0 / HALF) * ((west + east) + (south + north))
+        image = scale_ref[i] * v - 0.125 * ((west + east) + (south + north))
         if k == 0:
             image = 0.5 * image
         else:
-            image = image - v_refs[k - 1][i, body]
+            image = image - 0.0625 * v_refs[k - 1][i, body]
         ends = (jnp.where(lat > 0, image[:8], 0.0), image[8:rows + 8],
                 jnp.where(lat < lat_count - 1, image[rows + 8:], 0.0))
         return jnp.concatenate(ends, axis=0)
 
     for k in range(3):
-        @pl.loop(0, BLOCKS + 2, unroll=17)
+        @pl.loop(0, BLOCKS + 2, unroll=34)
         def _(i, k=k):
             v_refs[k + 1][i, 8:8 + tall] = applied(k, i)
 
@@ -313,13 +345,24 @@
         return tuple(out)
 
     zero = tuple(jnp.zeros((8, BW), F32) for _ in PAIRS)
-    totals = lax.fori_loop(0, BLOCKS, products, zero, unroll=4)
-    lane1 = lax.broadcasted_iota(jnp.int32, (1, BW), 1)
-    gram = jnp.zeros((1, BW), F32)
-    for n, total in enumerate(totals):
-        value = jnp.sum(jnp.sum(total, axis=0, keepdims=True), axis=1, keepdims=True)
-        gram = jnp.where(lane1 == n, value, gram)
-    gram_ref[...] = gram
+    totals = lax.fori_loop(0, BLOCKS, products, zero, unroll=8)
+    row_of = lax.broadcasted_iota(jnp.int32, (8, BW), 0)
+    lane_of = lax.broadcasted_iota(jnp.int32, (8, BW), 1)
+    gram = jnp.zeros((8, BW), F32)
+    for start in range(0, len(PAIRS), 8):
+        high = jnp.zeros((8, BW), F32)
+        low = jnp.zeros((8, BW), F32)
+        for n, total in enumerate(totals[start:start + 8]):
+            pair = all_rows(total, jnp.zeros_like(total))
+            high = jnp.where(row_of == n, pair[0], high)
+            low = jnp.where(row_of == n, pair[1], low)
+        shift = BW // 2
+        while shift:
+            high, low = pair_sum(high, low, pltpu.roll(high, shift, 1), pltpu.roll(low, shift, 1))
+            shift //= 2
+        gram = jnp.where(lane_of == row_of + start, high, gram)
+        gram = jnp.where(lane_of == row_of + start + LOW, low, gram)
+    gram_ref[...] = jnp.sum(gram, axis=0, keepdims=True)
 
 
 def basis(place, rhs, diag, *strips):
@@ -341,78 +384,103 @@
     )(place, rhs, diag, *strips)
 
 
-def solved(gram):
+def solved(high, low):
     g = {}
     for n, (a, b) in enumerate(PAIRS):
-        g[a, b] = g[b, a] = gram[n]
+        g[a, b] = g[b, a] = (high[n], low[n])
+
+    def times(factor, pair):
+        return factor * pair[0], factor * pair[1]
+
     m = [[None] * 4 for _ in range(4)]
     for j in range(4):
         for i in range(j + 1):
-            if j == 0:
-                value = MID * g[i, 0] + HALF * g[i, 1]
-            else:
-                value = MID * g[i, j] + (0.5 * HALF) * (g[i, j + 1] + g[i, j - 1])
-            m[i][j] = m[j][i] = value
-    y = [g[0, i] for i in range(4)]
+            value = pair_sum(*times(MID, g[i, j]), *times(8.0 if j else 16.0, g[i, j + 1]))
+            if j:
+                value = pair_sum(*value, *times(0.5, g[i, j - 1]))
+            m[i][j] = m[j][i] = two_sum(*value)
+
+    work = [[m[i][j][0] for j in range(4)] for i in range(4)]
     inverse = []
     factor = [[None] * 4 for _ in range(4)]
     for k in range(4):
-        pivot = m[k][k]
+        pivot = work[k][k]
         inverse.append(jnp.where(pivot > 0.0, 1.0 / jnp.where(pivot > 0.0, pivot, 1.0), 0.0))
         for i in range(k + 1, 4):
-            factor[i][k] = m[k][i] * inverse[k]
+            factor[i][k] = work[k][i] * inverse[k]
         for i in range(k + 1, 4):
             for j in range(i, 4):
-                m[i][j] = m[i][j] - factor[i][k] * m[k][j]
-            y[i] = y[i] - factor[i][k] * y[k]
-    c = [y[k] * inverse[k] for k in range(4)]
-    for k in range(3, -1, -1):
-        for i in range(k):
-            c[i] = c[i] - factor[k][i] * c[k]
-    half = 0.5 * HALF
+                work[i][j] = work[i][j] - factor[i][k] * work[k][j]
+
+    def solve(y):
+        y = list(y)
+        for k in range(4):
+            for i in range(k + 1, 4):
+                y[i] = y[i] - factor[i][k] * y[k]
+        y = [y[k] * inverse[k] for k in range(4)]
+        for k in range(3, -1, -1):
+            for i in range(k):
+                y[i] = y[i] - factor[k][i] * y[k]
+        return y
+
+    rest = [g[0, i] for i in range(4)]
+    c = solve([pair[0] for pair in rest])
+    found = [c]
+    for _ in range(2):
+        for i in range(4):
+            for j in range(4):
+                product, error = two_product(m[i][j][0], c[j])
+                total, lost = two_sum(rest[i][0], -product)
+                rest[i] = total, rest[i][1] + (lost - error - m[i][j][1] * c[j])
+        rest = [two_sum(*pair) for pair in rest]
+        c = solve([pair[0] for pair in rest])
+        found.append(c)
+    c = [found[0][k] + (found[1][k] + found[2][k]) for k in range(4)]
     r = [
-        1.0 - (MID * c[0] + half * c[1]),
-        -(HALF * c[0] + MID * c[1] + half * c[2]),
-        -(half * c[1] + MID * c[2] + half * c[3]),
-        -(half * c[2] + MID * c[3]),
-        -(half * c[3]),
+        1.0 - (MID * c[0] + 0.5 * c[1]),
+        -(16.0 * c[0] + MID * c[1] + 0.5 * c[2]),
+        -(8.0 * c[1] + MID * c[2] + 0.5 * c[3]),
+        -(8.0 * c[2] + MID * c[3]),
+        -(8.0 * c[3]),
     ]
     return c, r
 
 
-def combine_kernel(gram_ref, q_ref, x_ref, r_ref, c_ref):
-    @pl.when(pl.program_id(0) == 0)
-    def _():
-        gram = jnp.sum(gram_ref[...], axis=0, keepdims=True)
-        lane = lax.broadcasted_iota(jnp.int32, (1, BW), 1)
-        pick = lambda n: jnp.sum(jnp.where(lane == n, gram, 0.0), axis=1, keepdims=True)
-        c, r = solved([pick(n) for n in range(len(PAIRS))])
-        for n, value in enumerate(c + r):
-            c_ref[n] = jnp.broadcast_to(value, (8, BW))
-
+def combine_kernel(gram_ref, q_ref, x_ref, r_ref):
     rows = q_ref.shape[2]
-    factors = [jnp.concatenate([c_ref[n]] * (rows // 8), axis=0) for n in range(9)]
+    terms = [(gram_ref[n:n + 8], jnp.zeros((8, BW), F32)) for n in range(0, gram_ref.shape[0], 8)]
+    while len(terms) > 1:
+        terms = [pair_sum(*terms[n], *terms[n + 1]) for n in range(0, len(terms), 2)]
+    high, low = all_rows(*terms[0])
+    high, low = two_sum(high, low + pltpu.roll(high, BW - LOW, 1))
+    first = high[0:1, 0:1]
+    scale = jnp.where(first > 1e25, 2.0 ** -60, jnp.where(first < 1e-15, 2.0 ** 60, 1.0))
+    lane = lax.broadcasted_iota(jnp.int32, (1, BW), 1)
+
+    def pick(values, n):
+        row = jnp.where(lane == n, values[0:1], 0.0)
+        return scale * jnp.sum(row, axis=1, keepdims=True)
+
+    count = range(len(PAIRS))
+    c, r = solved([pick(high, n) for n in count], [pick(low, n) for n in count])
+    c = [jnp.broadcast_to(value, (rows, BW)) for value in c]
+    r = [jnp.broadcast_to(value, (rows, BW)) for value in r]
     for i in range(q_ref.shape[1]):
         q = [q_ref[k, i] for k in range(5)]
         columns = slice(i * BW, (i + 1) * BW)
-        x_ref[:, columns] = sum(factors[k] * q[k] for k in range(4))
-        r_ref[:, columns] = sum(factors[4 + k] * q[k] for k in range(5))
-
-
-def combine(gram, q, batch=8):
+        x_ref[:, columns] = sum(c[k] * q[k] for k in range(4))
+        r_ref[:, columns] = sum(r[k] * q[k] for k in range(5))
+
+
+def combine(gram, q):
     _, blocks, rows, _ = q.shape
     out = jax.ShapeDtypeStruct((rows, blocks * BW), F32)
-    spec = pl.BlockSpec((rows, batch * BW), lambda i: (0, i))
+    vmem = pl.BlockSpec(memory_space=pltpu.VMEM)
     return pl.pallas_call(
         combine_kernel,
-        grid=(blocks // batch,),
         out_shape=[out, out],
-        in_specs=[
-            pl.BlockSpec(gram.shape, lambda i: (0, 0)),
-            pl.BlockSpec((5, batch, rows, BW), lambda i: (0, i, 0, 0)),
-        ],
-        out_specs=[spec, spec],
-        scratch_shapes=[pltpu.VMEM((9, 8, BW), F32)],
+        in_specs=[vmem, vmem],
+        out_specs=[vmem, vmem],
         compiler_params=pltpu.CompilerParams(vmem_limit_bytes=VMEM_BYTES),
         name="combine",
     )(gram, q)

time: 168 us -> 166 us (0.988)
  no operation moved by 1% of the time
where the time goes in v5:
time: 166 us
  waiting for transfers between devices  101 us (61%)
  blocking collectives  26.7 us (16%)
  starting transfers between devices  21.8 us (13%)
  Pallas kernels  14.8 us (9%)
    all_to_all x1, waiting for transfers between devices, body(): lax.all_to_all(labelled, 'lon', split_axis=0, concat_axis=0, tiled=True)  96.3 us
    all_to_all x1, blocking collectives, body(): lax.all_to_all(spread, ('lon', 'lat'), split_axis=0, concat_axis=0, tiled...  26.7 us
    all_to_all x1, starting transfers between devices, body(): lax.all_to_all(labelled, 'lon', split_axis=0, concat_axis=0, tiled=True)  13.6 us
    ppermute x4, starting transfers between devices, swapped(): return lax.ppermute(block, axis, pairs + [(b, a) for a, b in pairs])  6.87 us
    pallas_call x1, Pallas kernels, sums(): pl.pallas_call(sums_kernel, out_shape=[jax.ShapeDtypeStruct(s, F32) for s...  4.41 us
    ppermute x4, waiting for transfers between devices, swapped(): return lax.ppermute(block, axis, pairs + [(b, a) for a, b in pairs])  4.15 us
    pallas_call x1, Pallas kernels, basis(): pl.pallas_call(basis_kernel, out_shape=[jax.ShapeDtypeStruct((5, BLOCKS,...  3.47 us
    pallas_call x1, Pallas kernels, pack(): pl.pallas_call(pack_kernel, out_shape=jax.ShapeDtypeStruct((tiles, CAPACI...  3.47 us
  transfers between devices with their start and end apart: 6, of which 4 were waited for; matrix products, arithmetic and copies ran while one was open for 0% of the time, Pallas kernels for 2%

profile of v5, /device:TPU:1, one launch (start us, length us, event | category | flops | bytes accessed | tf_op | source)
XLA Modules:
  0.0 166.2 jit_solution(2314746013965502)
XLA Ops:
  0.6 0.0 copy-start
  0.6 1.0 slice.9
  1.6 1.3 collective-permute-start
  2.9 3.5 %pack.1.packed_ref = f32[64,131,1,128]{3,2,1,0:T(1,128)} custom-call(s32[64]{0:T(128)} %column_ref.3, s32[64]{0:T(128)} %width_ref.1, f32[64,32,1,128]{3,2,1,0:T(1,128)} %bitcast.21, f32[64,32,1,128]{3,2,1,0:T(1,128)} %bitcast.22), custom_call_target="tpu_custom_call" | custom-call | tf_op jit(solution)/shard_map/pack/pallas_call | solution.py:87
  6.4 0.6 collective-permute-done.first_ref
  6.9 0.0 copy-done
  7.0 1.8 %label.1 = f32[64,131,1,128]{3,2,1,0:T(1,128)} custom-call(s32[64]{0:T(128)S(1)} %copy-done, f32[64,1,128]{2,1,0:T(1,128)S(1)} %collective-permute-done.first_ref, f32[64,131,1,128]{3,2,1,0:T(1,128)} %pack.1.packed_ref), custom_call_target="tpu_custom_call", output_to_operand_aliasing={{}: (2, {})} | custom-call | tf_op jit(solution)/shard_map/label/pallas_call | solution.py:129
  8.7 13.6 %all-to-all-start = ((f32[64,131,1,128]{3,2,1,0:T(1,128)}), f32[64,131,1,128]{3,2,1,0:T(1,128)}, u32[]{:S(2)}, u32[]{:S(2)}) async-start(f32[64,131,1,128]{3,2,1,0:T(1,128)} %label.1), calls=%async_computation | async-start | bytes 8585216 | tf_op jit(solution)/shard_map/all_to_all | solution.py:498
  22.4 0.1 pad_add_fusion.place_ref
  22.5 96.3 %all-to-all-done.got_ref = f32[64,131,1,128]{3,2,1,0:T(1,128)} async-done(((f32[64,131,1,128]{3,2,1,0:T(1,128)}), f32[64,131,1,128]{3,2,1,0:T(1,128)}, u32[]{:S(2)}, u32[]{:S(2)}) %all-to-all-start) | async-done | bytes 4292640 | tf_op jit(solution)/shard_map/all_to_all | solution.py:498
  118.8 4.4 %sums.1 = (f32[32,32,128]{2,1,0:T(8,128)S(1)}, f32[32,32,128]{2,1,0:T(8,128)S(1)}, f32[32,8,128]{2,1,0:T(8,128)S(1)}, f32[32,8,128]{2,1,0:T(8,128)S(1)}, f32[2,72,128]{2,1,0:T(8,128)S(1)}) custom-call(s32[3]{0:T(128)S(1)} %pad_add_fusion.place_ref, f32[64,131,1,128]{3,2,1,0:T(1,128)} %all-to-all-done.got_ref, f32[8384,128]{1,0:T(8,128)} %bitcast.4.rows_ref), custom_call_target="tpu_custom_call" | custom-call | tf_op jit(solution)/shard_map/sums/pallas_call | solution.py:229
  123.2 1.4 collective-permute-start.1
  124.6 0.7 collective-permute-start.2
  125.3 0.0 collective-permute-done.2.two_ref
  125.3 1.8 %collective-permute-done.1.one_ref = f32[32,8,128]{2,1,0:T(8,128)S(1)} collective-permute-done((f32[32,8,128]{2,1,0:T(8,128)S(1)}, f32[32,8,128]{2,1,0:T(8,128)S(1)}, u32[]{:S(2)}, u32[]{:S(2)}) %collective-permute-start.1) | collective-permute-done | bytes 131104 | tf_op jit(solution)/shard_map/ppermute | solution.py:35
  127.1 3.7 %collective-permute-start.3 = (f32[88,128]{1,0:T(8,128)S(1)}, f32[88,128]{1,0:T(8,128)S(1)}, u32[]{:S(2)}, u32[]{:S(2)}) collective-permute-start(f32[88,128]{1,0:T(8,128)S(1)} %pad_maximum_fusion), channel_id=1, source_target_pairs={{0,4},{8,12},{16,20},{24,28},{32,36},{40,44},{48,52},{56,60},{64,6... | collective-permute-start | bytes 135176 | tf_op jit(solution)/shard_map/ppermute | solution.py:35
  130.8 1.1 collective-permute-start.4
  131.9 0.0 collective-permute-done.3.lon_one_ref
  131.9 2.4 %collective-permute-done.4.lon_two_ref = f32[88,128]{1,0:T(8,128)S(1)} collective-permute-done((f32[88,128]{1,0:T(8,128)S(1)}, f32[88,128]{1,0:T(8,128)S(1)}, u32[]{:S(2)}, u32[]{:S(2)}) %collective-permute-start.4) | collective-permute-done | bytes 45088 | tf_op jit(solution)/shard_map/ppermute | solution.py:35
  134.3 3.5 %basis.1 = (f32[5,32,32,128]{3,2,1,0:T(8,128)S(1)}, f32[1,128]{1,0:T(1,128)S(1)}) custom-call(s32[3]{0:T(128)S(1)} %pad_add_fusion.place_ref, f32[32,32,128]{2,1,0:T(8,128)S(1)} %get-tuple-element.9.rhs_ref, f32[32,32,128]{2,1,0:T(8,128)S(1)} %get-tuple-element.10.diag_ref, f32[32,8,128]{2,1,0:T(8,128)S(1)} %get-tuple-element.11.own_one_ref, ...), custom_call_target="tpu_custom_call" | custom-call | tf_op jit(solution)/shard_map/basis/pallas_call | solution.py:371
  137.8 0.1 broadcast_in_dim.9
  137.8 26.7 %all_to_all.10 = f32[256,1,128]{2,1,0:T(1,128)S(1)} all-to-all(f32[256,1,128]{2,1,0:T(1,128)S(1)} %broadcast_in_dim.9), channel_id=1, replica_groups=mesh['lon'=64,'lat'=4] {'lon','lat'}, dimensions={0} | all-to-all | bytes 262144 | tf_op jit(solution)/shard_map/all_to_all | solution.py:511
  164.5 1.6 combine.1
  (5 shorter events, 0.0 us)
Async XLA Ops:
  0.6 6.3 %copy-start = (s32[64]{0:T(128)S(1)}, s32[64]{0:T(128)}, u32[]{:S(2)}) copy-start(s32[64]{0:T(128)} %column_ref.3) | copy-start | bytes 772
  1.6 5.3 %collective-permute-start = (f32[64,1,128]{2,1,0:T(1,128)S(1)}, f32[64,1,128]{2,1,0:T(1,128)S(1)}, u32[]{:S(2)}, u32[]{:S(2)}) collective-permute-start(f32[64,1,128]{2,1,0:T(1,128)S(1)} %slice.9), channel_id=1, source_target_pairs={{1,0},{2,1},{3,2},{5,4},{6,5},{7,6},{9,8},{10,9},{11,10},{13,12},{... | collective-permute-start | bytes 98312 | tf_op jit(solution)/shard_map/ppermute | solution.py:28
  8.7 110.1 %all-to-all-start = ((f32[64,131,1,128]{3,2,1,0:T(1,128)}), f32[64,131,1,128]{3,2,1,0:T(1,128)}, u32[]{:S(2)}, u32[]{:S(2)}) async-start(f32[64,131,1,128]{3,2,1,0:T(1,128)} %label.1), calls=%async_computation | async-start | bytes 8585216 | tf_op jit(solution)/shard_map/all_to_all | solution.py:498
  123.2 3.9 %collective-permute-start.1 = (f32[32,8,128]{2,1,0:T(8,128)S(1)}, f32[32,8,128]{2,1,0:T(8,128)S(1)}, u32[]{:S(2)}, u32[]{:S(2)}) collective-permute-start(f32[32,8,128]{2,1,0:T(8,128)S(1)} %get-tuple-element.11.own_one_ref), channel_id=1, source_target_pairs={{0,1},{2,3},{1,0},{3,2},{4,5},{6,7},{5,4},{7,6},{8,9},{10,11},{9,8... | collective-permute-start | bytes 393224 | tf_op jit(solution)/shard_map/ppermute | solution.py:35
  124.6 0.7 collective-permute-start.2
  127.1 4.8 %collective-permute-start.3 = (f32[88,128]{1,0:T(8,128)S(1)}, f32[88,128]{1,0:T(8,128)S(1)}, u32[]{:S(2)}, u32[]{:S(2)}) collective-permute-start(f32[88,128]{1,0:T(8,128)S(1)} %pad_maximum_fusion), channel_id=1, source_target_pairs={{0,4},{8,12},{16,20},{24,28},{32,36},{40,44},{48,52},{56,60},{64,6... | collective-permute-start | bytes 135176 | tf_op jit(solution)/shard_map/ppermute | solution.py:35
  130.8 3.5 %collective-permute-start.4 = (f32[88,128]{1,0:T(8,128)S(1)}, f32[88,128]{1,0:T(8,128)S(1)}, u32[]{:S(2)}, u32[]{:S(2)}) collective-permute-start(f32[88,128]{1,0:T(8,128)S(1)} %pad_maximum_fusion.1), channel_id=1, source_target_pairs={{4,8},{12,16},{20,24},{28,32},{36,40},{44,48},{52,56},{60,64},{68,... | collective-permute-start | bytes 135176 | tf_op jit(solution)/shard_map/ppermute | solution.py:35

commit v6 on v5

--- a/solution.py
+++ b/solution.py
@@ -18,7 +18,6 @@
 MID = 4.0
 VMEM_BYTES = 40 * 1024 * 1024
 PACK_VMEM_BYTES = 60 * 1024 * 1024
-SOME_VMEM_BYTES = 50 * 1024 * 1024
 F32 = jnp.float32
 
 
@@ -75,7 +74,7 @@
             pltpu.make_async_copy(held_ref.at[p], out_ref.at[tile, pl.ds(slot * part, part)],
                                   out_sem).start()
 
-    facts = pltpu.make_async_copy(facts_ref, out_ref.at[:, CAPACITY * (part + 1)], facts_sem)
+    facts = pltpu.make_async_copy(facts_ref, out_ref.at[:, CAPACITY * part], facts_sem)
     facts.start()
     pltpu.make_async_copy(held_ref, out_ref.at[pl.ds(0, pieces), pl.ds(0, part)], out_sem).wait()
     facts.wait()
@@ -86,7 +85,7 @@
     tall = lambda array: array.reshape(pieces, rows, 1, BW)
     return pl.pallas_call(
         pack_kernel,
-        out_shape=jax.ShapeDtypeStruct((tiles, CAPACITY * (2 * rows + 1) + 1, 1, BW), F32),
+        out_shape=jax.ShapeDtypeStruct((tiles, CAPACITY * 2 * rows + 1, 1, BW), F32),
         in_specs=[
             pl.BlockSpec(memory_space=pltpu.SMEM),
             pl.BlockSpec(memory_space=pltpu.SMEM),
@@ -107,49 +106,11 @@
     )(piece_column, piece_width, tall(piece_height), tall(piece_weight))
 
 
-def label_kernel(column_ref, first_ref, packed_ref, out_ref, count_ref, sem):
-    tiles, pieces = out_ref.shape[0], first_ref.shape[0]
-    first = out_ref.shape[1] - CAPACITY - 1
-
-    @pl.loop(0, tiles, unroll=8)
-    def _(t):
-        count_ref[t] = 0
-
-    @pl.loop(0, pieces, unroll=8)
-    def _(p):
-        tile = column_ref[p] // COLS_DEV
-        slot = count_ref[tile]
-        count_ref[tile] = slot + 1
-        pltpu.make_async_copy(first_ref.at[p], out_ref.at[tile, first + slot], sem).start()
-
-    pltpu.make_async_copy(first_ref, out_ref.at[pl.ds(0, pieces), first], sem).wait()
-
-
-def label(piece_column, next_first, packed):
-    return pl.pallas_call(
-        label_kernel,
-        out_shape=jax.ShapeDtypeStruct(packed.shape, F32),
-        in_specs=[
-            pl.BlockSpec(memory_space=pltpu.SMEM),
-            pl.BlockSpec(memory_space=pltpu.VMEM),
-            pl.BlockSpec(memory_space=pl.ANY),
-        ],
-        out_specs=pl.BlockSpec(memory_space=pl.ANY),
-        scratch_shapes=[
-            pltpu.SMEM(packed.shape[:1], jnp.int32),
-            pltpu.SemaphoreType.DMA,
-        ],
-        input_output_aliases={2: 0},
-        compiler_params=pltpu.CompilerParams(vmem_limit_bytes=SOME_VMEM_BYTES),
-        name="label",
-    )(piece_column, next_first, packed)
-
-
-def sums_kernel(place_ref, got_ref, rows_ref, rhs_ref, diag_ref, one_ref, two_ref, edge_ref,
+def sums_kernel(place_ref, got_ref, rows_ref, above_ref, rhs_ref, diag_ref, one_ref, two_ref, edge_ref,
                 held_ref, facts_ref, total_ref, facts_sem, sem):
     rows = rhs_ref.shape[1]
     part = 2 * rows
-    message = CAPACITY * (part + 1) + 1
+    message = CAPACITY * part + 1
     chunks, height, _ = held_ref.shape
     sources = height // message
     lat, lat_count, lon = place_ref[0], place_ref[1], place_ref[2]
@@ -176,10 +137,10 @@
             block = jnp.where(block < 0, BLOCKS, block)
             width = facts_ref[n * sources + source, 0, 2 * slot + 1].astype(jnp.int32)
             base = source * message
-            start, first = base + slot * part, base + CAPACITY * part + slot
+            start = base + slot * part
             height = held_ref[n, start:start + rows]
             weight = held_ref[n, start + rows:start + part]
-            above = held_ref[n, first:first + 1]
+            above = above_ref[n * sources + source, slot]
             cell = jnp.where(lane < width, weight, 0.0)
             east = jnp.where(lane < width - 1, weight, 0.0)
             east_step = pltpu.roll(height, BW - 1, 1) - height
@@ -219,7 +180,7 @@
         edge_ref[side, 2 * rows:2 * rows + 8] = up
 
 
-def sums(place, got, rows, chunks=2):
+def sums(place, got, above, rows, chunks=2):
     tiles, message, _, _ = got.shape
     height = tiles * message // chunks
     field = (BLOCKS, rows, BW)
@@ -233,6 +194,7 @@
             pl.BlockSpec(memory_space=pltpu.SMEM),
             pl.BlockSpec(memory_space=pl.ANY),
             pl.BlockSpec(memory_space=pl.ANY),
+            vmem,
         ],
         out_specs=[vmem] * 5,
         scratch_shapes=[
@@ -244,7 +206,7 @@
         ],
         compiler_params=pltpu.CompilerParams(vmem_limit_bytes=VMEM_BYTES),
         name="sums",
-    )(place, got, got.reshape(chunks * height, BW))
+    )(place, got, got.reshape(chunks * height, BW), above)
 
 
 def two_sum(a, b):
@@ -492,11 +454,11 @@
     lon, lat = lax.axis_index("lon"), lax.axis_index("lat")
     place = jnp.stack([lat, jnp.int32(lat_count), lon]).astype(jnp.int32)
 
-    next_first = passed_along(piece_height[:, :1, :], "lat", -1)
     packed = pack(piece_column, piece_width, piece_height, piece_weight, lon_count)
-    labelled = label(piece_column, next_first, packed)
-    got = lax.all_to_all(labelled, "lon", split_axis=0, concat_axis=0, tiled=True)
-    rhs, diag, own_one, own_two, edge = sums(place, got, rows)
+    got = lax.all_to_all(packed, "lon", split_axis=0, concat_axis=0, tiled=True)
+    part = 2 * rows
+    above = passed_along(got[:, :CAPACITY * part:part], "lat", -1)
+    rhs, diag, own_one, own_two, edge = sums(place, got, above, rows)
 
     one = swapped(own_one, "lat", 0, False)
     two = swapped(own_two, "lat", 1, False)

time: 166 us -> 165 us (level)
  waiting for transfers between devices: 101 us -> 103 us
  Pallas kernels: 14.8 us -> 12.9 us
  blocking collectives: 26.7 us -> 25 us
    ppermute x1, waiting for transfers between devices: 0.55 us -> 3.63 us  [passed_along(): return lax.ppermute(block, axis, route)]
    pallas_call x1 -> x0, Pallas kernels: 1.77 us -> none  [label(): pl.pallas_call(label_kernel, out_shape=jax.ShapeDtypeStruct(packed.shape,...]
    all_to_all x1, blocking collectives: 26.7 us -> 25 us  [body(): lax.all_to_all(spread, ('lon', 'lat'), split_axis=0, concat_axis=0, tiled...]
  transfers between devices with their start and end apart: 6 -> 6, of which waited for: 4 -> 4; matrix products, arithmetic and copies ran while one was open for 0% -> 0% of each run, Pallas kernels for 2% -> 0%
where the time goes in v6:
time: 165 us
  waiting for transfers between devices  103 us (62%)
  blocking collectives  25 us (15%)
  starting transfers between devices  22.3 us (14%)
  Pallas kernels  12.9 us (8%)
    all_to_all x1, waiting for transfers between devices, body(): got = lax.all_to_all(packed, 'lon', split_axis=0, concat_axis=0, tiled=True)  95.1 us
    all_to_all x1, blocking collectives, body(): lax.all_to_all(spread, ('lon', 'lat'), split_axis=0, concat_axis=0, tiled...  25 us
    all_to_all x1, starting transfers between devices, body(): got = lax.all_to_all(packed, 'lon', split_axis=0, concat_axis=0, tiled=True)  13.1 us
    ppermute x4, starting transfers between devices, swapped(): return lax.ppermute(block, axis, pairs + [(b, a) for a, b in pairs])  7.9 us
    pallas_call x1, Pallas kernels, sums(): pl.pallas_call(sums_kernel, out_shape=[jax.ShapeDtypeStruct(s, F32) for s...  4.41 us
    ppermute x4, waiting for transfers between devices, swapped(): return lax.ppermute(block, axis, pairs + [(b, a) for a, b in pairs])  4.18 us
    ppermute x1, waiting for transfers between devices, passed_along(): return lax.ppermute(block, axis, route)  3.63 us
    pallas_call x1, Pallas kernels, pack(): pl.pallas_call(pack_kernel, out_shape=jax.ShapeDtypeStruct((tiles, CAPACI...  3.46 us
  transfers between devices with their start and end apart: 6, of which 4 were waited for; matrix products, arithmetic and copies ran while one was open for 0% of the time, Pallas kernels for 0%

profile of v6, /device:TPU:1, one launch (start us, length us, event | category | flops | bytes accessed | tf_op | source)
XLA Modules:
  0.0 164.8 jit_solution(12289650409186525147)
XLA Ops:
  0.6 3.5 %pack.1 = f32[64,129,1,128]{3,2,1,0:T(1,128)} custom-call(s32[64]{0:T(128)} %column_ref.1, s32[64]{0:T(128)} %width_ref.1, f32[64,32,1,128]{3,2,1,0:T(1,128)} %bitcast.21, f32[64,32,1,128]{3,2,1,0:T(1,128)} %bitcast.22), custom_call_target="tpu_custom_call" | custom-call | tf_op jit(solution)/shard_map/pack/pallas_call | solution.py:86
  4.1 13.1 %all-to-all-start = ((f32[64,129,1,128]{3,2,1,0:T(1,128)}), f32[64,129,1,128]{3,2,1,0:T(1,128)}, u32[]{:S(2)}, u32[]{:S(2)}) async-start(f32[64,129,1,128]{3,2,1,0:T(1,128)} %pack.1), calls=%async_computation | async-start | bytes 8454144 | tf_op jit(solution)/shard_map/all_to_all | solution.py:458
  17.3 95.1 %all-to-all-done.got_ref = f32[64,129,1,128]{3,2,1,0:T(1,128)} async-done(((f32[64,129,1,128]{3,2,1,0:T(1,128)}), f32[64,129,1,128]{3,2,1,0:T(1,128)}, u32[]{:S(2)}, u32[]{:S(2)}) %all-to-all-start) | async-done | bytes 4227104 | tf_op jit(solution)/shard_map/all_to_all | solution.py:458
  112.3 0.9 slice.9
  113.2 1.3 collective-permute-start
  114.5 0.1 pad_add_fusion.place_ref
  114.6 3.6 %collective-permute-done.above_ref = f32[64,2,1,128]{3,2,1,0:T(1,128)S(1)} collective-permute-done((f32[64,2,1,128]{3,2,1,0:T(1,128)S(1)}, f32[64,2,1,128]{3,2,1,0:T(1,128)S(1)}, u32[]{:S(2)}, u32[]{:S(2)}) %collective-permute-start) | collective-permute-done | bytes 65568 | tf_op jit(solution)/shard_map/ppermute | solution.py:27
  118.2 4.4 %sums.1 = (f32[32,32,128]{2,1,0:T(8,128)S(1)}, f32[32,32,128]{2,1,0:T(8,128)S(1)}, f32[32,8,128]{2,1,0:T(8,128)S(1)}, f32[32,8,128]{2,1,0:T(8,128)S(1)}, f32[2,72,128]{2,1,0:T(8,128)S(1)}) custom-call(s32[3]{0:T(128)S(1)} %pad_add_fusion.place_ref, f32[64,129,1,128]{3,2,1,0:T(1,128)} %all-to-all-done.got_ref, f32[8256,128]{1,0:T(8,128)} %bitcast.4.rows_ref, ...), custom_call_target="tpu_custom_call" | custom-call | tf_op jit(solution)/shard_map/sums/pallas_call | solution.py:190
  122.6 1.4 collective-permute-start.1
  124.0 0.7 collective-permute-start.2
  124.7 0.0 collective-permute-done.2.two_ref
  124.7 1.8 %collective-permute-done.1.one_ref = f32[32,8,128]{2,1,0:T(8,128)S(1)} collective-permute-done((f32[32,8,128]{2,1,0:T(8,128)S(1)}, f32[32,8,128]{2,1,0:T(8,128)S(1)}, u32[]{:S(2)}, u32[]{:S(2)}) %collective-permute-start.1) | collective-permute-done | bytes 131104 | tf_op jit(solution)/shard_map/ppermute | solution.py:34
  126.5 4.8 %collective-permute-start.3 = (f32[88,128]{1,0:T(8,128)S(1)}, f32[88,128]{1,0:T(8,128)S(1)}, u32[]{:S(2)}, u32[]{:S(2)}) collective-permute-start(f32[88,128]{1,0:T(8,128)S(1)} %pad_maximum_fusion), channel_id=1, source_target_pairs={{0,4},{8,12},{16,20},{24,28},{32,36},{40,44},{48,52},{56,60},{64,6... | collective-permute-start | bytes 135176 | tf_op jit(solution)/shard_map/ppermute | solution.py:34
  131.3 1.1 collective-permute-start.4
  132.4 0.0 collective-permute-done.3.lon_one_ref
  132.4 2.4 %collective-permute-done.4.lon_two_ref = f32[88,128]{1,0:T(8,128)S(1)} collective-permute-done((f32[88,128]{1,0:T(8,128)S(1)}, f32[88,128]{1,0:T(8,128)S(1)}, u32[]{:S(2)}, u32[]{:S(2)}) %collective-permute-start.4) | collective-permute-done | bytes 45088 | tf_op jit(solution)/shard_map/ppermute | solution.py:34
  134.8 3.4 %basis.1 = (f32[5,32,32,128]{3,2,1,0:T(8,128)S(1)}, f32[1,128]{1,0:T(1,128)S(1)}) custom-call(s32[3]{0:T(128)S(1)} %pad_add_fusion.place_ref, f32[32,32,128]{2,1,0:T(8,128)S(1)} %get-tuple-element.9.rhs_ref, f32[32,32,128]{2,1,0:T(8,128)S(1)} %get-tuple-element.10.diag_ref, f32[32,8,128]{2,1,0:T(8,128)S(1)} %get-tuple-element.11.own_one_ref, ...), custom_call_target="tpu_custom_call" | custom-call | tf_op jit(solution)/shard_map/basis/pallas_call | solution.py:333
  138.2 0.1 broadcast_in_dim.9
  138.3 25.0 %all_to_all.10 = f32[256,1,128]{2,1,0:T(1,128)S(1)} all-to-all(f32[256,1,128]{2,1,0:T(1,128)S(1)} %broadcast_in_dim.9), channel_id=1, replica_groups=mesh['lon'=64,'lat'=4] {'lon','lat'}, dimensions={0} | all-to-all | bytes 262144 | tf_op jit(solution)/shard_map/all_to_all | solution.py:473
  163.2 1.6 combine.1
  (5 shorter events, 0.0 us)
Async XLA Ops:
  4.1 108.2 %all-to-all-start = ((f32[64,129,1,128]{3,2,1,0:T(1,128)}), f32[64,129,1,128]{3,2,1,0:T(1,128)}, u32[]{:S(2)}, u32[]{:S(2)}) async-start(f32[64,129,1,128]{3,2,1,0:T(1,128)} %pack.1), calls=%async_computation | async-start | bytes 8454144 | tf_op jit(solution)/shard_map/all_to_all | solution.py:458
  113.2 5.0 %collective-permute-start = (f32[64,2,1,128]{3,2,1,0:T(1,128)S(1)}, f32[64,2,1,128]{3,2,1,0:T(1,128)S(1)}, u32[]{:S(2)}, u32[]{:S(2)}) collective-permute-start(f32[64,2,1,128]{3,2,1,0:T(1,128)S(1)} %slice.9), channel_id=1, source_target_pairs={{1,0},{2,1},{3,2},{5,4},{6,5},{7,6},{9,8},{10,9},{11,10},{13,12},{... | collective-permute-start | bytes 196616 | tf_op jit(solution)/shard_map/ppermute | solution.py:27
  122.6 3.9 %collective-permute-start.1 = (f32[32,8,128]{2,1,0:T(8,128)S(1)}, f32[32,8,128]{2,1,0:T(8,128)S(1)}, u32[]{:S(2)}, u32[]{:S(2)}) collective-permute-start(f32[32,8,128]{2,1,0:T(8,128)S(1)} %get-tuple-element.11.own_one_ref), channel_id=1, source_target_pairs={{0,1},{2,3},{1,0},{3,2},{4,5},{6,7},{5,4},{7,6},{8,9},{10,11},{9,8... | collective-permute-start | bytes 393224 | tf_op jit(solution)/shard_map/ppermute | solution.py:34
  124.0 0.7 collective-permute-start.2
  126.5 5.9 %collective-permute-start.3 = (f32[88,128]{1,0:T(8,128)S(1)}, f32[88,128]{1,0:T(8,128)S(1)}, u32[]{:S(2)}, u32[]{:S(2)}) collective-permute-start(f32[88,128]{1,0:T(8,128)S(1)} %pad_maximum_fusion), channel_id=1, source_target_pairs={{0,4},{8,12},{16,20},{24,28},{32,36},{40,44},{48,52},{56,60},{64,6... | collective-permute-start | bytes 135176 | tf_op jit(solution)/shard_map/ppermute | solution.py:34
  131.3 3.5 %collective-permute-start.4 = (f32[88,128]{1,0:T(8,128)S(1)}, f32[88,128]{1,0:T(8,128)S(1)}, u32[]{:S(2)}, u32[]{:S(2)}) collective-permute-start(f32[88,128]{1,0:T(8,128)S(1)} %pad_maximum_fusion.1), channel_id=1, source_target_pairs={{4,8},{12,16},{20,24},{28,32},{36,40},{44,48},{52,56},{60,64},{68,... | collective-permute-start | bytes 135176 | tf_op jit(solution)/shard_map/ppermute | solution.py:34

commit v7 on v6

--- a/solution.py
+++ b/solution.py
@@ -106,14 +106,14 @@
     )(piece_column, piece_width, tall(piece_height), tall(piece_weight))
 
 
-def sums_kernel(place_ref, got_ref, rows_ref, above_ref, rhs_ref, diag_ref, one_ref, two_ref, edge_ref,
-                held_ref, facts_ref, total_ref, facts_sem, sem):
+def gather_kernel(place_ref, got_ref, rows_ref, rhs_ref, diag_ref, one_ref, two_ref, last_ref,
+                  inverse_ref, blocks_ref, total_ref, held_ref, facts_ref, facts_sem, sem):
     rows = rhs_ref.shape[1]
+    lat, lat_count = place_ref[0], place_ref[1]
     part = 2 * rows
     message = CAPACITY * part + 1
     chunks, height, _ = held_ref.shape
     sources = height // message
-    lat, lat_count, lon = place_ref[0], place_ref[1], place_ref[2]
     lane = lax.broadcasted_iota(jnp.int32, (rows, BW), 1)
     row = lax.broadcasted_iota(jnp.int32, (rows, BW), 0)
 
@@ -140,14 +140,15 @@
             start = base + slot * part
             height = held_ref[n, start:start + rows]
             weight = held_ref[n, start + rows:start + part]
-            above = above_ref[n * sources + source, slot]
             cell = jnp.where(lane < width, weight, 0.0)
             east = jnp.where(lane < width - 1, weight, 0.0)
             east_step = pltpu.roll(height, BW - 1, 1) - height
-            raised = jnp.where(row == rows - 1, above, pltpu.roll(height, rows - 1, 0))
+            raised = jnp.where(row == rows - 1, 0.0, pltpu.roll(height, rows - 1, 0))
             terms = (cell, cell * height, east, east * east_step, cell * (raised - height))
             for k, term in enumerate(terms):
                 total_ref[block, k] += term
+            last_ref[n * sources + source, slot] = cell[rows - 8:]
+            blocks_ref[(n * sources + source) * CAPACITY + slot] = block
 
     last = (row == rows - 1) & (lat == lat_count - 1)
     first = (row == 0) & (lat == 0)
@@ -171,42 +172,85 @@
         down = jnp.where(row8 >= 4, pltpu.roll(diag[:8], 4, 0), rhs[:8])
         one_ref[i] = jnp.where(lat_even, up, down)
         two_ref[i] = jnp.where(lat_even, down, up)
-
-    first_edge = (BLOCKS - 1) * (1 - lon % 2)
-    for side, block in ((0, first_edge), (1, BLOCKS - 1 - first_edge)):
-        edge_ref[side, 0:rows] = rhs_ref[block]
-        edge_ref[side, rows:2 * rows] = diag_ref[block]
-        up = jnp.where(lat_even, one_ref[block], two_ref[block])
-        edge_ref[side, 2 * rows:2 * rows + 8] = up
-
-
-def sums(place, got, above, rows, chunks=2):
+        inverse_ref[i] = 1.0 / (cell[rows - 8:] + DAMPING)
+
+
+def gather(place, got, rows, chunks=2):
     tiles, message, _, _ = got.shape
     height = tiles * message // chunks
     field = (BLOCKS, rows, BW)
     strip = (BLOCKS, 8, BW)
-    edge = (2, 2 * rows + 8, BW)
     vmem = pl.BlockSpec(memory_space=pltpu.VMEM)
+    shapes = (field, field, strip, strip, (tiles, CAPACITY, 8, BW), strip)
     return pl.pallas_call(
-        sums_kernel,
-        out_shape=[jax.ShapeDtypeStruct(s, F32) for s in (field, field, strip, strip, edge)],
-        in_specs=[
-            pl.BlockSpec(memory_space=pltpu.SMEM),
-            pl.BlockSpec(memory_space=pl.ANY),
-            pl.BlockSpec(memory_space=pl.ANY),
-            vmem,
-        ],
-        out_specs=[vmem] * 5,
+        gather_kernel,
+        out_shape=[jax.ShapeDtypeStruct(s, F32) for s in shapes]
+        + [jax.ShapeDtypeStruct((tiles * CAPACITY,), jnp.int32)],
+        in_specs=[pl.BlockSpec(memory_space=pltpu.SMEM)] + [pl.BlockSpec(memory_space=pl.ANY)] * 2,
+        out_specs=[vmem] * len(shapes) + [pl.BlockSpec(memory_space=pltpu.SMEM)],
         scratch_shapes=[
+            pltpu.VMEM((BLOCKS + 1, 5, rows, BW), F32),
             pltpu.VMEM((chunks, height, BW), F32),
             pltpu.SMEM((tiles, 1, BW), F32),
-            pltpu.VMEM((BLOCKS + 1, 5, rows, BW), F32),
             pltpu.SemaphoreType.DMA,
             pltpu.SemaphoreType.DMA((chunks,)),
         ],
         compiler_params=pltpu.CompilerParams(vmem_limit_bytes=VMEM_BYTES),
-        name="sums",
-    )(place, got, got.reshape(chunks * height, BW), above)
+        name="gather",
+    )(place, got, got.reshape(chunks * height, BW))
+
+
+def finish_kernel(place_ref, blocks_ref, rhs_ref, diag_ref, part_one_ref, part_two_ref, last_ref,
+                  inverse_ref, above_ref, gain_ref, one_ref, two_ref, edge_ref, *fix_refs):
+    rows = rhs_ref.shape[1]
+    tiles = last_ref.shape[0]
+    lat, lon = place_ref[0], place_ref[2]
+    lat_even = lat % 2 == 0
+    row8 = lax.broadcasted_iota(jnp.int32, (8, BW), 0)
+    for ref in fix_refs:
+        ref[...] = jnp.zeros_like(ref)
+
+    @pl.loop(0, tiles // 2, unroll=8)
+    def _(n):
+        for k, ref in enumerate(fix_refs):
+            source, slot = 2 * n + k // CAPACITY, k % CAPACITY
+            block = blocks_ref[source * CAPACITY + slot]
+            ref[block] += last_ref[source, slot] * above_ref[source, slot]
+
+    @pl.loop(0, BLOCKS, unroll=8)
+    def _(i):
+        gain = sum(ref[i] for ref in fix_refs) * inverse_ref[i]
+        gain = jnp.where(row8 == 7, gain, 0.0)
+        gain_ref[i] = gain
+        up = pltpu.roll(gain, 1, 0) - gain
+        one_ref[i] = part_one_ref[i] + jnp.where(lat_even, up, 0.0)
+        two_ref[i] = part_two_ref[i] + jnp.where(lat_even, 0.0, up)
+
+    first_edge = (BLOCKS - 1) * (1 - lon % 2)
+    for side, block in ((0, first_edge), (1, BLOCKS - 1 - first_edge)):
+        edge_ref[side, 0:rows - 8] = rhs_ref[block, 0:rows - 8]
+        edge_ref[side, rows - 8:rows] = rhs_ref[block, rows - 8:rows] - gain_ref[block]
+        edge_ref[side, rows:2 * rows] = diag_ref[block]
+        edge_ref[side, 2 * rows:2 * rows + 8] = jnp.where(lat_even, one_ref[block], two_ref[block])
+
+
+def finish(place, blocks, rhs, diag, *strips):
+    rows = rhs.shape[1]
+    strip = (BLOCKS, 8, BW)
+    edge = (2, 2 * rows + 8, BW)
+    vmem = pl.BlockSpec(memory_space=pltpu.VMEM)
+    return pl.pallas_call(
+        finish_kernel,
+        out_shape=[jax.ShapeDtypeStruct(s, F32) for s in (strip, strip, strip, edge)],
+        in_specs=[
+            pl.BlockSpec(memory_space=pltpu.SMEM),
+            pl.BlockSpec(memory_space=pltpu.SMEM),
+        ] + [vmem] * 7,
+        out_specs=[vmem] * 4,
+        scratch_shapes=[pltpu.VMEM((BLOCKS + 1, 8, BW), F32)] * 4,
+        compiler_params=pltpu.CompilerParams(vmem_limit_bytes=VMEM_BYTES),
+        name="finish",
+    )(place, blocks, rhs, diag, *strips)
 
 
 def two_sum(a, b):
@@ -241,7 +285,7 @@
 LOW = 16
 
 
-def basis_kernel(place_ref, rhs_ref, diag_ref, own_one_ref, own_two_ref, one_ref, two_ref,
+def basis_kernel(place_ref, rhs_ref, diag_ref, gain_ref, own_one_ref, own_two_ref, one_ref, two_ref,
                  lon_one_ref, lon_two_ref, q_ref, gram_ref, scale_ref, *v_refs):
     rows = rhs_ref.shape[1]
     tall = rows + 16
@@ -270,7 +314,9 @@
     @pl.loop(0, BLOCKS, unroll=4)
     def _(i):
         up = jnp.where(lat_even, own_one_ref[i], own_two_ref[i])
-        assemble(i + 1, rhs_ref[i], diag_ref[i], up, one_ref[i], two_ref[i])
+        tail = rhs_ref[i, rows - 8:rows] - gain_ref[i]
+        rhs = jnp.concatenate([rhs_ref[i, 0:rows - 8], tail], axis=0)
+        assemble(i + 1, rhs, diag_ref[i], up, one_ref[i], two_ref[i])
 
     def applied(k, i):
         body = slice(8, 8 + tall)
@@ -336,7 +382,7 @@
             jax.ShapeDtypeStruct((5, BLOCKS, rows, BW), F32),
             jax.ShapeDtypeStruct((1, BW), F32),
         ],
-        in_specs=[pl.BlockSpec(memory_space=pltpu.SMEM)] + [vmem] * 8,
+        in_specs=[pl.BlockSpec(memory_space=pltpu.SMEM)] + [vmem] * 9,
         out_specs=[vmem, vmem],
         scratch_shapes=[
             pltpu.VMEM((BLOCKS + 2, rows + 16, BW), F32),
@@ -458,7 +504,8 @@
     got = lax.all_to_all(packed, "lon", split_axis=0, concat_axis=0, tiled=True)
     part = 2 * rows
     above = passed_along(got[:, :CAPACITY * part:part], "lat", -1)
-    rhs, diag, own_one, own_two, edge = sums(place, got, above, rows)
+    rhs, diag, *strips, blocks = gather(place, got, rows)
+    gain, own_one, own_two, edge = finish(place, blocks, rhs, diag, *strips, above)
 
     one = swapped(own_one, "lat", 0, False)
     two = swapped(own_two, "lat", 1, False)
@@ -468,7 +515,7 @@
         pick = lambda strip: lax.dynamic_index_in_dim(strip, block, 0, keepdims=False)
         message = jnp.concatenate([edge[start], pick(one), pick(two)], axis=0)
         strips.append(swapped(message, "lon", start, True))
-    q, gram = basis(place, rhs, diag, own_one, own_two, one, two, *strips)
+    q, gram = basis(place, rhs, diag, gain, own_one, own_two, one, two, *strips)
     spread = jnp.broadcast_to(gram[None], (lon_count * lat_count, 1, BW))
     grams = lax.all_to_all(spread, ("lon", "lat"), split_axis=0, concat_axis=0, tiled=True)
     return tuple(combine(grams.reshape(lon_count * lat_count, BW), q))

time: 165 us -> 163 us (0.988)
  waiting for transfers between devices: 103 us -> 98.5 us
    ppermute x1, waiting for transfers between devices: 3.63 us -> 0.01 us  [passed_along(): return lax.ppermute(block, axis, route)]
    pallas_call x1 -> x2, Pallas kernels: 4.41 us -> 5.88 us  [the longest x1 4.99 us: gather(): pl.pallas_call(gather_kernel, out_shape=[jax.ShapeDtypeStruct(s, F32) for...]
  transfers between devices with their start and end apart: 6 -> 6, of which waited for: 4 -> 3; matrix products, arithmetic and copies ran while one was open for 0% -> 0% of each run, Pallas kernels for 0% -> 3%
where the time goes in v7:
time: 163 us
  waiting for transfers between devices  98.5 us (60%)
  blocking collectives  26.1 us (16%)
  starting transfers between devices  21.9 us (13%)
  Pallas kernels  14.4 us (9%)
    all_to_all x1, waiting for transfers between devices, body(): got = lax.all_to_all(packed, 'lon', split_axis=0, concat_axis=0, tiled=True)  95.1 us
    all_to_all x1, blocking collectives, body(): lax.all_to_all(spread, ('lon', 'lat'), split_axis=0, concat_axis=0, tiled...  26.1 us
    all_to_all x1, starting transfers between devices, body(): got = lax.all_to_all(packed, 'lon', split_axis=0, concat_axis=0, tiled=True)  13.1 us
    ppermute x4, starting transfers between devices, swapped(): return lax.ppermute(block, axis, pairs + [(b, a) for a, b in pairs])  7.45 us
    pallas_call x1, Pallas kernels, gather(): pl.pallas_call(gather_kernel, out_shape=[jax.ShapeDtypeStruct(s, F32) for...  4.99 us
    pallas_call x1, Pallas kernels, pack(): pl.pallas_call(pack_kernel, out_shape=jax.ShapeDtypeStruct((tiles, CAPACI...  3.46 us
    pallas_call x1, Pallas kernels, basis(): pl.pallas_call(basis_kernel, out_shape=[jax.ShapeDtypeStruct((5, BLOCKS,...  3.41 us
    ppermute x4, waiting for transfers between devices, swapped(): return lax.ppermute(block, axis, pairs + [(b, a) for a, b in pairs])  3.41 us
  transfers between devices with their start and end apart: 6, of which 3 were waited for; matrix products, arithmetic and copies ran while one was open for 0% of the time, Pallas kernels for 3%

profile of v7, /device:TPU:1, one launch (start us, length us, event | category | flops | bytes accessed | tf_op | source)
XLA Modules:
  0.0 162.6 jit_solution(15248600670452657037)
XLA Ops:
  0.6 3.5 %pack.1 = f32[64,129,1,128]{3,2,1,0:T(1,128)} custom-call(s32[64]{0:T(128)} %column_ref.1, s32[64]{0:T(128)} %width_ref.1, f32[64,32,1,128]{3,2,1,0:T(1,128)} %bitcast.21, f32[64,32,1,128]{3,2,1,0:T(1,128)} %bitcast.22), custom_call_target="tpu_custom_call" | custom-call | tf_op jit(solution)/shard_map/pack/pallas_call | solution.py:86
  4.1 13.1 %all-to-all-start = ((f32[64,129,1,128]{3,2,1,0:T(1,128)}), f32[64,129,1,128]{3,2,1,0:T(1,128)}, u32[]{:S(2)}, u32[]{:S(2)}) async-start(f32[64,129,1,128]{3,2,1,0:T(1,128)} %pack.1), calls=%async_computation | async-start | bytes 8454144 | tf_op jit(solution)/shard_map/all_to_all | solution.py:504
  17.3 95.1 %all-to-all-done.got_ref = f32[64,129,1,128]{3,2,1,0:T(1,128)} async-done(((f32[64,129,1,128]{3,2,1,0:T(1,128)}), f32[64,129,1,128]{3,2,1,0:T(1,128)}, u32[]{:S(2)}, u32[]{:S(2)}) %all-to-all-start) | async-done | bytes 4227104 | tf_op jit(solution)/shard_map/all_to_all | solution.py:504
  112.4 0.9 slice.9
  113.2 1.3 collective-permute-start
  114.5 0.1 pad_add_fusion.place_ref
  114.6 5.0 %gather.1 = (f32[32,32,128]{2,1,0:T(8,128)S(1)}, f32[32,32,128]{2,1,0:T(8,128)S(1)}, f32[32,8,128]{2,1,0:T(8,128)S(1)}, f32[32,8,128]{2,1,0:T(8,128)S(1)}, f32[6...) custom-call(s32[3]{0:T(128)S(1)} %pad_add_fusion.place_ref, ...), custom_call_target="tpu_custom_call" | custom-call | tf_op jit(solution)/shard_map/gather/pallas_call | solution.py:185
  119.6 0.0 collective-permute-done.above_ref
  119.6 0.9 finish.1
  120.5 2.2 %collective-permute-start.1 = (f32[32,8,128]{2,1,0:T(8,128)S(1)}, f32[32,8,128]{2,1,0:T(8,128)S(1)}, u32[]{:S(2)}, u32[]{:S(2)}) collective-permute-start(f32[32,8,128]{2,1,0:T(8,128)S(1)} %get-tuple-element.23.own_one_ref), channel_id=1, source_target_pairs={{0,1},{2,3},{1,0},{3,2},{4,5},{6,7},{5,4},{7,6},{8,9},{10,11},{9,8... | collective-permute-start | bytes 393224 | tf_op jit(solution)/shard_map/ppermute | solution.py:34
  122.7 0.7 collective-permute-start.2
  123.4 1.7 %collective-permute-done.1.one_ref = f32[32,8,128]{2,1,0:T(8,128)S(1)} collective-permute-done((f32[32,8,128]{2,1,0:T(8,128)S(1)}, f32[32,8,128]{2,1,0:T(8,128)S(1)}, u32[]{:S(2)}, u32[]{:S(2)}) %collective-permute-start.1) | collective-permute-done | bytes 131104 | tf_op jit(solution)/shard_map/ppermute | solution.py:34
  125.0 0.0 collective-permute-done.2.two_ref
  125.1 4.6 %collective-permute-start.4 = (f32[88,128]{1,0:T(8,128)S(1)}, f32[88,128]{1,0:T(8,128)S(1)}, u32[]{:S(2)}, u32[]{:S(2)}) collective-permute-start(f32[88,128]{1,0:T(8,128)S(1)} %pad_maximum_fusion.1), channel_id=1, source_target_pairs={{4,8},{12,16},{20,24},{28,32},{36,40},{44,48},{52,56},{60,64},{68,... | collective-permute-start | bytes 135176 | tf_op jit(solution)/shard_map/ppermute | solution.py:34
  129.7 0.0 collective-permute-start.3
  129.7 1.7 %collective-permute-done.4.lon_two_ref = f32[88,128]{1,0:T(8,128)S(1)} collective-permute-done((f32[88,128]{1,0:T(8,128)S(1)}, f32[88,128]{1,0:T(8,128)S(1)}, u32[]{:S(2)}, u32[]{:S(2)}) %collective-permute-start.4) | collective-permute-done | bytes 45088 | tf_op jit(solution)/shard_map/ppermute | solution.py:34
  131.4 0.0 collective-permute-done.3.lon_one_ref
  131.4 3.4 %basis.1 = (f32[5,32,32,128]{3,2,1,0:T(8,128)S(1)}, f32[1,128]{1,0:T(1,128)S(1)}) custom-call(s32[3]{0:T(128)S(1)} %pad_add_fusion.place_ref, f32[32,32,128]{2,1,0:T(8,128)S(1)} %get-tuple-element.15.rhs_ref, f32[32,32,128]{2,1,0:T(8,128)S(1)} %get-tuple-element.16.diag_ref, f32[32,8,128]{2,1,0:T(8,128)S(1)} %get-tuple-element.22.gain_ref, ...), custom_call_target="tpu_custom_call" | custom-call | tf_op jit(solution)/shard_map/basis/pallas_call | solution.py:379
  134.8 0.1 broadcast_in_dim.9
  134.9 26.1 %all_to_all.10 = f32[256,1,128]{2,1,0:T(1,128)S(1)} all-to-all(f32[256,1,128]{2,1,0:T(1,128)S(1)} %broadcast_in_dim.9), channel_id=1, replica_groups=mesh['lon'=64,'lat'=4] {'lon','lat'}, dimensions={0} | all-to-all | bytes 262144 | tf_op jit(solution)/shard_map/all_to_all | solution.py:520
  161.0 1.6 %combine.1 = (f32[32,4096]{1,0:T(8,128)}, f32[32,4096]{1,0:T(8,128)}) custom-call(f32[256,128]{1,0:T(8,128)S(1)} %bitcast.19, f32[5,32,32,128]{3,2,1,0:T(8,128)S(1)} %get-tuple-element.27.q_ref), custom_call_target="tpu_custom_call" | custom-call | tf_op jit(solution)/shard_map/combine/pallas_call | solution.py:487
  (5 shorter events, 0.0 us)
Async XLA Ops:
  4.1 108.3 %all-to-all-start = ((f32[64,129,1,128]{3,2,1,0:T(1,128)}), f32[64,129,1,128]{3,2,1,0:T(1,128)}, u32[]{:S(2)}, u32[]{:S(2)}) async-start(f32[64,129,1,128]{3,2,1,0:T(1,128)} %pack.1), calls=%async_computation | async-start | bytes 8454144 | tf_op jit(solution)/shard_map/all_to_all | solution.py:504
  113.2 6.4 %collective-permute-start = (f32[64,2,1,128]{3,2,1,0:T(1,128)S(1)}, f32[64,2,1,128]{3,2,1,0:T(1,128)S(1)}, u32[]{:S(2)}, u32[]{:S(2)}) collective-permute-start(f32[64,2,1,128]{3,2,1,0:T(1,128)S(1)} %slice.9), channel_id=1, source_target_pairs={{1,0},{2,1},{3,2},{5,4},{6,5},{7,6},{9,8},{10,9},{11,10},{13,12},{... | collective-permute-start | bytes 196616 | tf_op jit(solution)/shard_map/ppermute | solution.py:27
  120.5 4.5 %collective-permute-start.1 = (f32[32,8,128]{2,1,0:T(8,128)S(1)}, f32[32,8,128]{2,1,0:T(8,128)S(1)}, u32[]{:S(2)}, u32[]{:S(2)}) collective-permute-start(f32[32,8,128]{2,1,0:T(8,128)S(1)} %get-tuple-element.23.own_one_ref), channel_id=1, source_target_pairs={{0,1},{2,3},{1,0},{3,2},{4,5},{6,7},{5,4},{7,6},{8,9},{10,11},{9,8... | collective-permute-start | bytes 393224 | tf_op jit(solution)/shard_map/ppermute | solution.py:34
  122.7 2.4 %collective-permute-start.2 = (f32[32,8,128]{2,1,0:T(8,128)S(1)}, f32[32,8,128]{2,1,0:T(8,128)S(1)}, u32[]{:S(2)}, u32[]{:S(2)}) collective-permute-start(f32[32,8,128]{2,1,0:T(8,128)S(1)} %get-tuple-element.24.own_two_ref), channel_id=1, source_target_pairs={{1,2},{2,1},{5,6},{6,5},{9,10},{10,9},{13,14},{14,13},{17,18},{18,... | collective-permute-start | bytes 393224 | tf_op jit(solution)/shard_map/ppermute | solution.py:34
  125.1 6.4 %collective-permute-start.4 = (f32[88,128]{1,0:T(8,128)S(1)}, f32[88,128]{1,0:T(8,128)S(1)}, u32[]{:S(2)}, u32[]{:S(2)}) collective-permute-start(f32[88,128]{1,0:T(8,128)S(1)} %pad_maximum_fusion.1), channel_id=1, source_target_pairs={{4,8},{12,16},{20,24},{28,32},{36,40},{44,48},{52,56},{60,64},{68,... | collective-permute-start | bytes 135176 | tf_op jit(solution)/shard_map/ppermute | solution.py:34
  129.7 1.7 %collective-permute-start.3 = (f32[88,128]{1,0:T(8,128)S(1)}, f32[88,128]{1,0:T(8,128)S(1)}, u32[]{:S(2)}, u32[]{:S(2)}) collective-permute-start(f32[88,128]{1,0:T(8,128)S(1)} %pad_maximum_fusion), channel_id=1, source_target_pairs={{0,4},{8,12},{16,20},{24,28},{32,36},{40,44},{48,52},{56,60},{64,6... | collective-permute-start | bytes 135176 | tf_op jit(solution)/shard_map/ppermute | solution.py:34

commit v8 on v7

--- a/solution.py
+++ b/solution.py
@@ -285,75 +285,144 @@
 LOW = 16
 
 
-def basis_kernel(place_ref, rhs_ref, diag_ref, gain_ref, own_one_ref, own_two_ref, one_ref, two_ref,
-                 lon_one_ref, lon_two_ref, q_ref, gram_ref, scale_ref, *v_refs):
-    rows = rhs_ref.shape[1]
-    tall = rows + 16
-    lat, lat_count, lon = place_ref[0], place_ref[1], place_ref[2]
-    lat_even = lat % 2 == 0
-    row = lax.broadcasted_iota(jnp.int32, (rows, BW), 0)
-    row8 = row[:8]
-    lane = lax.broadcasted_iota(jnp.int32, (tall, BW), 1)
-
-    def assemble(i, rhs, diag, up, one, two):
-        south = jnp.where(lat_even, two, one)
-        north = jnp.where(lat_even, one, two)
-        first = jnp.where(row == 0, south[0:1], 0.0) + rhs
+class Field:
+    def __init__(self, place_ref, rows, scale_ref, v_refs):
+        self.rows, self.tall = rows, rows + 16
+        self.scale_ref, self.v_refs = scale_ref, v_refs
+        lat, lat_count = place_ref[0], place_ref[1]
+        self.lat_even = lat % 2 == 0
+        self.has_south, self.has_north = lat > 0, lat < lat_count - 1
+        self.row = lax.broadcasted_iota(jnp.int32, (rows, BW), 0)
+        self.lane = lax.broadcasted_iota(jnp.int32, (self.tall, BW), 1)
+
+    def assemble(self, i, rhs, diag, up, one, two):
+        row8 = self.row[:8]
+        south = jnp.where(self.lat_even, two, one)
+        north = jnp.where(self.lat_even, one, two)
+        first = jnp.where(self.row == 0, south[0:1], 0.0) + rhs
         below = jnp.where(row8 >= 4, south, 0.0)
         above = jnp.where(row8 == 0, north + up, jnp.where(row8 < 4, north, 0.0))
-        v_refs[0][i, 8:8 + tall] = jnp.concatenate([below, first, above], axis=0)
+        self.v_refs[0][i, 8:8 + self.tall] = jnp.concatenate([below, first, above], axis=0)
         diag = jnp.concatenate([pltpu.roll(south, 4, 0), diag, pltpu.roll(north, 4, 0)], axis=0)
-        scale_ref[i] = (diag - MID) * 0.125
-
-    side = (BLOCKS + 1) * (1 - lon % 2)
-    for i, ref in ((side, lon_one_ref), (BLOCKS + 1 - side, lon_two_ref)):
-        two = 2 * rows
-        assemble(i, ref[0:rows], ref[rows:two], ref[two:two + 8], ref[two + 8:two + 16],
-                 ref[two + 16:two + 24])
-
-    @pl.loop(0, BLOCKS, unroll=4)
-    def _(i):
-        up = jnp.where(lat_even, own_one_ref[i], own_two_ref[i])
-        tail = rhs_ref[i, rows - 8:rows] - gain_ref[i]
-        rhs = jnp.concatenate([rhs_ref[i, 0:rows - 8], tail], axis=0)
-        assemble(i + 1, rhs, diag_ref[i], up, one_ref[i], two_ref[i])
-
-    def applied(k, i):
+        self.scale_ref[i] = (diag - MID) * 0.125
+
+    def applied(self, k, i, left, right):
+        ref, rows, tall = self.v_refs[k], self.rows, self.tall
         body = slice(8, 8 + tall)
-        v = v_refs[k][i, body]
-        left = v_refs[k][jnp.maximum(i - 1, 0), body]
-        right = v_refs[k][jnp.minimum(i + 1, BLOCKS + 1), body]
-        west = pltpu.roll(jnp.where(lane == BW - 1, left, v), 1, 1)
-        east = pltpu.roll(jnp.where(lane == 0, right, v), BW - 1, 1)
-        south = v_refs[k][i, 7:7 + tall]
-        north = v_refs[k][i, 9:9 + tall]
-        image = scale_ref[i] * v - 0.125 * ((west + east) + (south + north))
+        v = ref[i, body]
+        west = pltpu.roll(jnp.where(self.lane == BW - 1, ref[left, body], v), 1, 1)
+        east = pltpu.roll(jnp.where(self.lane == 0, ref[right, body], v), BW - 1, 1)
+        south = ref[i, 7:7 + tall]
+        north = ref[i, 9:9 + tall]
+        image = self.scale_ref[i] * v - 0.125 * ((west + east) + (south + north))
         if k == 0:
             image = 0.5 * image
         else:
-            image = image - 0.0625 * v_refs[k - 1][i, body]
-        ends = (jnp.where(lat > 0, image[:8], 0.0), image[8:rows + 8],
-                jnp.where(lat < lat_count - 1, image[rows + 8:], 0.0))
+            image = image - 0.0625 * self.v_refs[k - 1][i, body]
+        ends = (jnp.where(self.has_south, image[:8], 0.0), image[8:rows + 8],
+                jnp.where(self.has_north, image[rows + 8:], 0.0))
         return jnp.concatenate(ends, axis=0)
 
-    for k in range(3):
-        @pl.loop(0, BLOCKS + 2, unroll=34)
-        def _(i, k=k):
-            v_refs[k + 1][i, 8:8 + tall] = applied(k, i)
-
-    def products(i, carry):
-        last = applied(3, i + 1)[8:8 + rows]
-        q = [v_refs[k][i + 1, 16:16 + rows] for k in range(4)] + [last]
+    def step(self, k, i, left, right):
+        self.v_refs[k + 1][i, 8:8 + self.tall] = self.applied(k, i, left, right)
+
+    def products(self, i, left, right, q_ref, at, totals):
+        rows = self.rows
+        last = self.applied(3, i, left, right)[8:8 + rows]
+        q = [self.v_refs[k][i, 16:16 + rows] for k in range(4)] + [last]
         for k in range(5):
-            q_ref[k, i] = q[k]
+            q_ref[k, at] = q[k]
         out = []
-        for total, (a, b) in zip(carry, PAIRS):
+        for total, (a, b) in zip(totals, PAIRS):
             term = q[a] * q[b]
             out.append(total + sum(term[8 * n:8 * n + 8] for n in range(rows // 8)))
         return tuple(out)
 
+
+NEAR = 6
+
+
+def inner_kernel(place_ref, rhs_ref, diag_ref, gain_ref, own_one_ref, own_two_ref, one_ref,
+                 two_ref, q_ref, totals_ref, sides_ref, scale_ref, *v_refs):
+    rows = rhs_ref.shape[1]
+    field = Field(place_ref, rows, scale_ref, v_refs)
+
+    @pl.loop(0, BLOCKS, unroll=4)
+    def _(i):
+        up = jnp.where(field.lat_even, own_one_ref[i], own_two_ref[i])
+        tail = rhs_ref[i, rows - 8:rows] - gain_ref[i]
+        rhs = jnp.concatenate([rhs_ref[i, 0:rows - 8], tail], axis=0)
+        field.assemble(i + 1, rhs, diag_ref[i], up, one_ref[i], two_ref[i])
+
+    for k in range(3):
+        @pl.loop(k + 2, BLOCKS - k, unroll=BLOCKS - 2 * k - 2)
+        def _(i, k=k):
+            field.step(k, i, i - 1, i + 1)
+
+    def products(i, totals):
+        return field.products(i, i - 1, i + 1, q_ref, i - 1, totals)
+
     zero = tuple(jnp.zeros((8, BW), F32) for _ in PAIRS)
-    totals = lax.fori_loop(0, BLOCKS, products, zero, unroll=8)
+    totals = lax.fori_loop(5, BLOCKS - 3, products, zero, unroll=8)
+    for n, total in enumerate(totals):
+        totals_ref[n] = total
+    for k, ref in enumerate((scale_ref,) + v_refs):
+        body = slice(8, 24 + rows) if k else slice(0, 16 + rows)
+        for n in range(NEAR):
+            sides_ref[0, k, n] = ref[n + 1, body]
+            sides_ref[1, k, n] = ref[BLOCKS - n, body]
+
+
+def inner(place, rhs, diag, *strips):
+    rows = rhs.shape[1]
+    vmem = pl.BlockSpec(memory_space=pltpu.VMEM)
+    shapes = ((5, BLOCKS, rows, BW), (len(PAIRS), 8, BW), (2, 5, NEAR, rows + 16, BW))
+    return pl.pallas_call(
+        inner_kernel,
+        out_shape=[jax.ShapeDtypeStruct(s, F32) for s in shapes],
+        in_specs=[pl.BlockSpec(memory_space=pltpu.SMEM)] + [vmem] * 7,
+        out_specs=[vmem] * 3,
+        scratch_shapes=[pltpu.VMEM((BLOCKS + 2, rows + 16, BW), F32)]
+        + [pltpu.VMEM((BLOCKS + 2, rows + 32, BW), F32)] * 4,
+        compiler_params=pltpu.CompilerParams(vmem_limit_bytes=VMEM_BYTES),
+        name="inner",
+    )(place, rhs, diag, *strips)
+
+
+def outer_kernel(place_ref, totals_ref, sides_ref, lon_one_ref, lon_two_ref, q_ref, gram_ref,
+                 scale_ref, *v_refs):
+    tall = sides_ref.shape[3]
+    rows = tall - 16
+    field = Field(place_ref, rows, scale_ref, v_refs)
+    size = NEAR + 1
+    for side in range(2):
+        for n in range(NEAR):
+            scale_ref[side * size + n + 1] = sides_ref[side, 0, n]
+            for k in range(4):
+                if n >= k:
+                    v_refs[k][side * size + n + 1, 8:8 + tall] = sides_ref[side, k + 1, n]
+    one_east = place_ref[2] % 2 == 0
+    two = 2 * rows
+    for side in range(2):
+        first = lon_two_ref[...] if side == 0 else lon_one_ref[...]
+        other = lon_one_ref[...] if side == 0 else lon_two_ref[...]
+        strip = jnp.where(one_east, first, other)
+        field.assemble(side * size, strip[0:rows], strip[rows:two], strip[two:two + 8],
+                       strip[two + 8:two + 16], strip[two + 16:two + 24])
+
+    def beside(side, n):
+        inward, outward = side * size + n + 1, side * size + max(n - 1, 0)
+        return (side * size + n,) + ((outward, inward) if side == 0 else (inward, outward))
+
+    for k in range(3):
+        for n in range(k + 2):
+            for side in range(2):
+                field.step(k, *beside(side, n))
+    totals = tuple(totals_ref[n] for n in range(len(PAIRS)))
+    for n in range(1, 5):
+        for side in range(2):
+            totals = field.products(*beside(side, n), q_ref, side * 4 + n - 1, totals)
+
     row_of = lax.broadcasted_iota(jnp.int32, (8, BW), 0)
     lane_of = lax.broadcasted_iota(jnp.int32, (8, BW), 1)
     gram = jnp.zeros((8, BW), F32)
@@ -373,23 +442,23 @@
     gram_ref[...] = jnp.sum(gram, axis=0, keepdims=True)
 
 
-def basis(place, rhs, diag, *strips):
-    rows = rhs.shape[1]
+def outer(place, totals, sides, one, two):
+    tall = sides.shape[3]
+    rows = tall - 16
     vmem = pl.BlockSpec(memory_space=pltpu.VMEM)
     return pl.pallas_call(
-        basis_kernel,
+        outer_kernel,
         out_shape=[
-            jax.ShapeDtypeStruct((5, BLOCKS, rows, BW), F32),
+            jax.ShapeDtypeStruct((5, 8, rows, BW), F32),
             jax.ShapeDtypeStruct((1, BW), F32),
         ],
-        in_specs=[pl.BlockSpec(memory_space=pltpu.SMEM)] + [vmem] * 9,
+        in_specs=[pl.BlockSpec(memory_space=pltpu.SMEM)] + [vmem] * 4,
         out_specs=[vmem, vmem],
-        scratch_shapes=[
-            pltpu.VMEM((BLOCKS + 2, rows + 16, BW), F32),
-        ] + [pltpu.VMEM((BLOCKS + 2, rows + 32, BW), F32)] * 4,
+        scratch_shapes=[pltpu.VMEM((2 * (NEAR + 1), tall, BW), F32)]
+        + [pltpu.VMEM((2 * (NEAR + 1), tall + 16, BW), F32)] * 4,
         compiler_params=pltpu.CompilerParams(vmem_limit_bytes=VMEM_BYTES),
-        name="basis",
-    )(place, rhs, diag, *strips)
+        name="outer",
+    )(place, totals, sides, one, two)
 
 
 def solved(high, low):
@@ -454,7 +523,7 @@
     return c, r
 
 
-def combine_kernel(gram_ref, q_ref, x_ref, r_ref):
+def combine_kernel(gram_ref, q_ref, sides_ref, x_ref, r_ref):
     rows = q_ref.shape[2]
     terms = [(gram_ref[n:n + 8], jnp.zeros((8, BW), F32)) for n in range(0, gram_ref.shape[0], 8)]
     while len(terms) > 1:
@@ -474,24 +543,29 @@
     c = [jnp.broadcast_to(value, (rows, BW)) for value in c]
     r = [jnp.broadcast_to(value, (rows, BW)) for value in r]
     for i in range(q_ref.shape[1]):
-        q = [q_ref[k, i] for k in range(5)]
+        if i < 4:
+            q = [sides_ref[k, i] for k in range(5)]
+        elif i >= BLOCKS - 4:
+            q = [sides_ref[k, 4 + BLOCKS - 1 - i] for k in range(5)]
+        else:
+            q = [q_ref[k, i] for k in range(5)]
         columns = slice(i * BW, (i + 1) * BW)
         x_ref[:, columns] = sum(c[k] * q[k] for k in range(4))
         r_ref[:, columns] = sum(r[k] * q[k] for k in range(5))
 
 
-def combine(gram, q):
+def combine(gram, q, sides):
     _, blocks, rows, _ = q.shape
     out = jax.ShapeDtypeStruct((rows, blocks * BW), F32)
     vmem = pl.BlockSpec(memory_space=pltpu.VMEM)
     return pl.pallas_call(
         combine_kernel,
         out_shape=[out, out],
-        in_specs=[vmem, vmem],
+        in_specs=[vmem] * 3,
         out_specs=[vmem, vmem],
         compiler_params=pltpu.CompilerParams(vmem_limit_bytes=VMEM_BYTES),
         name="combine",
-    )(gram, q)
+    )(gram, q, sides)
 
 
 def body(piece_height, piece_weight, piece_column, piece_width):
@@ -515,10 +589,11 @@
         pick = lambda strip: lax.dynamic_index_in_dim(strip, block, 0, keepdims=False)
         message = jnp.concatenate([edge[start], pick(one), pick(two)], axis=0)
         strips.append(swapped(message, "lon", start, True))
-    q, gram = basis(place, rhs, diag, gain, own_one, own_two, one, two, *strips)
+    q, totals, near = inner(place, rhs, diag, gain, own_one, own_two, one, two)
+    sides, gram = outer(place, totals, near, *strips)
     spread = jnp.broadcast_to(gram[None], (lon_count * lat_count, 1, BW))
     grams = lax.all_to_all(spread, ("lon", "lat"), split_axis=0, concat_axis=0, tiled=True)
-    return tuple(combine(grams.reshape(lon_count * lat_count, BW), q))
+    return tuple(combine(grams.reshape(lon_count * lat_count, BW), q, sides))
 
 
 def solution(mesh):

time: 163 us -> 162 us (level)
  waiting for transfers between devices: 98.5 us -> 96.8 us
    ppermute x4, waiting for transfers between devices: 3.41 us -> 1.69 us  [swapped(): return lax.ppermute(block, axis, pairs + [(b, a) for a, b in pairs])]
    pallas_call x2 -> x3, Pallas kernels: 5.05 us -> 5.76 us  [the longest x1 2.52 us: inner(): pl.pallas_call(inner_kernel, out_shape=[jax.ShapeDtypeStruct(s, F32) for...]
  transfers between devices with their start and end apart: 6 -> 6, of which waited for: 3 -> 2; matrix products, arithmetic and copies ran while one was open for 0% -> 0% of each run, Pallas kernels for 3% -> 5%
where the time goes in v8:
time: 162 us; the launch traced here: 161 us
  waiting for transfers between devices  96.8 us (60%)
  blocking collectives  25.9 us (16%)
  starting transfers between devices  21.9 us (14%)
  Pallas kernels  15.1 us (9%)
    all_to_all x1, waiting for transfers between devices, body(): got = lax.all_to_all(packed, 'lon', split_axis=0, concat_axis=0, tiled=True)  95.1 us
    all_to_all x1, blocking collectives, body(): lax.all_to_all(spread, ('lon', 'lat'), split_axis=0, concat_axis=0, tiled...  25.9 us
    all_to_all x1, starting transfers between devices, body(): got = lax.all_to_all(packed, 'lon', split_axis=0, concat_axis=0, tiled=True)  13.2 us
    ppermute x4, starting transfers between devices, swapped(): return lax.ppermute(block, axis, pairs + [(b, a) for a, b in pairs])  7.43 us
    pallas_call x1, Pallas kernels, gather(): pl.pallas_call(gather_kernel, out_shape=[jax.ShapeDtypeStruct(s, F32) for...  4.99 us
    pallas_call x1, Pallas kernels, pack(): pl.pallas_call(pack_kernel, out_shape=jax.ShapeDtypeStruct((tiles, CAPACI...  3.43 us
  transfers between devices with their start and end apart: 6, of which 2 were waited for; matrix products, arithmetic and copies ran while one was open for 0% of the time, Pallas kernels for 5%

profile of v8, /device:TPU:1, one launch (start us, length us, event | category | flops | bytes accessed | tf_op | source)
XLA Modules:
  0.0 161.5 jit_solution(12498775351719410779)
XLA Ops:
  0.6 3.4 %pack.1 = f32[64,129,1,128]{3,2,1,0:T(1,128)} custom-call(s32[64]{0:T(128)} %column_ref.1, s32[64]{0:T(128)} %width_ref.1, f32[64,32,1,128]{3,2,1,0:T(1,128)} %bitcast.21, f32[64,32,1,128]{3,2,1,0:T(1,128)} %bitcast.22), custom_call_target="tpu_custom_call" | custom-call | tf_op jit(solution)/shard_map/pack/pallas_call | solution.py:86
  4.1 13.2 %all-to-all-start = ((f32[64,129,1,128]{3,2,1,0:T(1,128)}), f32[64,129,1,128]{3,2,1,0:T(1,128)}, u32[]{:S(2)}, u32[]{:S(2)}) async-start(f32[64,129,1,128]{3,2,1,0:T(1,128)} %pack.1), calls=%async_computation | async-start | bytes 8454144 | tf_op jit(solution)/shard_map/all_to_all | solution.py:578
  17.3 95.1 %all-to-all-done.got_ref = f32[64,129,1,128]{3,2,1,0:T(1,128)} async-done(((f32[64,129,1,128]{3,2,1,0:T(1,128)}), f32[64,129,1,128]{3,2,1,0:T(1,128)}, u32[]{:S(2)}, u32[]{:S(2)}) %all-to-all-start) | async-done | bytes 4227104 | tf_op jit(solution)/shard_map/all_to_all | solution.py:578
  112.4 0.9 slice.9
  113.2 1.3 collective-permute-start
  114.5 0.1 pad_add_fusion.place_ref
  114.6 5.0 %gather.1 = (f32[32,32,128]{2,1,0:T(8,128)S(1)}, f32[32,32,128]{2,1,0:T(8,128)S(1)}, f32[32,8,128]{2,1,0:T(8,128)S(1)}, f32[32,8,128]{2,1,0:T(8,128)S(1)}, f32[6...) custom-call(s32[3]{0:T(128)S(1)} %pad_add_fusion.place_ref, ...), custom_call_target="tpu_custom_call" | custom-call | tf_op jit(solution)/shard_map/gather/pallas_call | solution.py:185
  119.6 0.0 collective-permute-done.above_ref
  119.6 0.9 finish.1
  120.5 2.2 %collective-permute-start.1 = (f32[32,8,128]{2,1,0:T(8,128)S(1)}, f32[32,8,128]{2,1,0:T(8,128)S(1)}, u32[]{:S(2)}, u32[]{:S(2)}) collective-permute-start(f32[32,8,128]{2,1,0:T(8,128)S(1)} %get-tuple-element.26.own_one_ref), channel_id=1, source_target_pairs={{0,1},{2,3},{1,0},{3,2},{4,5},{6,7},{5,4},{7,6},{8,9},{10,11},{9,8... | collective-permute-start | bytes 393224 | tf_op jit(solution)/shard_map/ppermute | solution.py:34
  122.7 0.7 collective-permute-start.2
  123.4 1.7 %collective-permute-done.1.one_ref = f32[32,8,128]{2,1,0:T(8,128)S(1)} collective-permute-done((f32[32,8,128]{2,1,0:T(8,128)S(1)}, f32[32,8,128]{2,1,0:T(8,128)S(1)}, u32[]{:S(2)}, u32[]{:S(2)}) %collective-permute-start.1) | collective-permute-done | bytes 131104 | tf_op jit(solution)/shard_map/ppermute | solution.py:34
  125.1 0.0 collective-permute-done.2.two_ref
  125.1 4.6 %collective-permute-start.4 = (f32[88,128]{1,0:T(8,128)S(1)}, f32[88,128]{1,0:T(8,128)S(1)}, u32[]{:S(2)}, u32[]{:S(2)}) collective-permute-start(f32[88,128]{1,0:T(8,128)S(1)} %pad_maximum_fusion.1), channel_id=1, source_target_pairs={{4,8},{12,16},{20,24},{28,32},{36,40},{44,48},{52,56},{60,64},{68,... | collective-permute-start | bytes 135176 | tf_op jit(solution)/shard_map/ppermute | solution.py:34
  129.7 0.0 collective-permute-start.3
  129.7 2.5 %inner.1 = (f32[5,32,32,128]{3,2,1,0:T(8,128)S(1)}, f32[14,8,128]{2,1,0:T(8,128)S(1)}, f32[2,5,6,48,128]{4,3,2,1,0:T(8,128)S(1)}) custom-call(s32[3]{0:T(128)S(1)} %pad_add_fusion.place_ref, f32[32,32,128]{2,1,0:T(8,128)S(1)} %get-tuple-element.18.rhs_ref, f32[32,32,128]{2,1,0:T(8,128)S(1)} %get-tuple-element.19.diag_ref, ...), custom_call_target="tpu_custom_call" | custom-call | tf_op jit(solution)/shard_map/inner/pallas_call | solution.py:380
  132.2 0.0 collective-permute-done.4.lon_two_ref
  132.2 0.0 collective-permute-done.3.lon_one_ref
  132.2 1.6 outer.1
  133.8 0.1 broadcast_in_dim.9
  133.9 25.9 %all_to_all.10 = f32[256,1,128]{2,1,0:T(1,128)S(1)} all-to-all(f32[256,1,128]{2,1,0:T(1,128)S(1)} %broadcast_in_dim.9), channel_id=1, replica_groups=mesh['lon'=64,'lat'=4] {'lon','lat'}, dimensions={0} | all-to-all | bytes 262144 | tf_op jit(solution)/shard_map/all_to_all | solution.py:595
  159.8 1.6 %combine.1 = (f32[32,4096]{1,0:T(8,128)}, f32[32,4096]{1,0:T(8,128)}) custom-call(f32[256,128]{1,0:T(8,128)S(1)} %bitcast.19, f32[5,32,32,128]{3,2,1,0:T(8,128)S(1)} %get-tuple-element.32.q_ref, f32[5,8,32,128]{3,2,1,0:T(8,128)S(1)} %get-tuple-element.33.sides_ref), custom_call_target="tpu_custom_call" | custom-call | tf_op jit(solution)/shard_map/combine/pallas_call | solution.py:561
  (5 shorter events, 0.0 us)
Async XLA Ops:
  4.1 108.3 %all-to-all-start = ((f32[64,129,1,128]{3,2,1,0:T(1,128)}), f32[64,129,1,128]{3,2,1,0:T(1,128)}, u32[]{:S(2)}, u32[]{:S(2)}) async-start(f32[64,129,1,128]{3,2,1,0:T(1,128)} %pack.1), calls=%async_computation | async-start | bytes 8454144 | tf_op jit(solution)/shard_map/all_to_all | solution.py:578
  113.2 6.4 %collective-permute-start = (f32[64,2,1,128]{3,2,1,0:T(1,128)S(1)}, f32[64,2,1,128]{3,2,1,0:T(1,128)S(1)}, u32[]{:S(2)}, u32[]{:S(2)}) collective-permute-start(f32[64,2,1,128]{3,2,1,0:T(1,128)S(1)} %slice.9), channel_id=1, source_target_pairs={{1,0},{2,1},{3,2},{5,4},{6,5},{7,6},{9,8},{10,9},{11,10},{13,12},{... | collective-permute-start | bytes 196616 | tf_op jit(solution)/shard_map/ppermute | solution.py:27
  120.5 4.5 %collective-permute-start.1 = (f32[32,8,128]{2,1,0:T(8,128)S(1)}, f32[32,8,128]{2,1,0:T(8,128)S(1)}, u32[]{:S(2)}, u32[]{:S(2)}) collective-permute-start(f32[32,8,128]{2,1,0:T(8,128)S(1)} %get-tuple-element.26.own_one_ref), channel_id=1, source_target_pairs={{0,1},{2,3},{1,0},{3,2},{4,5},{6,7},{5,4},{7,6},{8,9},{10,11},{9,8... | collective-permute-start | bytes 393224 | tf_op jit(solution)/shard_map/ppermute | solution.py:34
  122.7 2.4 %collective-permute-start.2 = (f32[32,8,128]{2,1,0:T(8,128)S(1)}, f32[32,8,128]{2,1,0:T(8,128)S(1)}, u32[]{:S(2)}, u32[]{:S(2)}) collective-permute-start(f32[32,8,128]{2,1,0:T(8,128)S(1)} %get-tuple-element.27.own_two_ref), channel_id=1, source_target_pairs={{1,2},{2,1},{5,6},{6,5},{9,10},{10,9},{13,14},{14,13},{17,18},{18,... | collective-permute-start | bytes 393224 | tf_op jit(solution)/shard_map/ppermute | solution.py:34
  125.1 7.1 %collective-permute-start.4 = (f32[88,128]{1,0:T(8,128)S(1)}, f32[88,128]{1,0:T(8,128)S(1)}, u32[]{:S(2)}, u32[]{:S(2)}) collective-permute-start(f32[88,128]{1,0:T(8,128)S(1)} %pad_maximum_fusion.1), channel_id=1, source_target_pairs={{4,8},{12,16},{20,24},{28,32},{36,40},{44,48},{52,56},{60,64},{68,... | collective-permute-start | bytes 135176 | tf_op jit(solution)/shard_map/ppermute | solution.py:34
  129.7 2.5 %collective-permute-start.3 = (f32[88,128]{1,0:T(8,128)S(1)}, f32[88,128]{1,0:T(8,128)S(1)}, u32[]{:S(2)}, u32[]{:S(2)}) collective-permute-start(f32[88,128]{1,0:T(8,128)S(1)} %pad_maximum_fusion), channel_id=1, source_target_pairs={{0,4},{8,12},{16,20},{24,28},{32,36},{40,44},{48,52},{56,60},{64,6... | collective-permute-start | bytes 135176 | tf_op jit(solution)/shard_map/ppermute | solution.py:34

commit v9 on v8

--- a/solution.py
+++ b/solution.py
@@ -35,7 +35,7 @@
 
 
 def pack_kernel(column_ref, width_ref, height_ref, weight_ref, out_ref, held_ref, facts_ref,
-                count_ref, in_sem, out_sem, facts_sem):
+                count_ref, slot_ref, in_sem, out_sem, facts_sem):
     tiles, pieces = out_ref.shape[0], height_ref.shape[0]
     rows = height_ref.shape[1]
     part = 2 * rows
@@ -58,29 +58,33 @@
     def _(t):
         count_ref[t] = 0
 
+    @pl.loop(0, pieces, unroll=8)
+    def _(p):
+        tile = column_ref[p] // COLS_DEV
+        block = column_ref[p] % COLS_DEV // BW
+        slot = count_ref[tile]
+        count_ref[tile] = slot + 1
+        slot_ref[p] = slot
+        at = 2 * slot
+        facts = jnp.where(lane == at, block + 1, jnp.where(lane == at + 1, width_ref[p], 0))
+        facts_ref[tile] += facts.astype(F32)
+
+    facts = pltpu.make_async_copy(facts_ref, out_ref.at[:, CAPACITY * part], facts_sem)
+    facts.start()
     for g in range(in_sem.shape[0]):
         for load in loads(g):
             load.wait()
 
-        @pl.loop(g * batch, (g + 1) * batch, unroll=4)
+        @pl.loop(g * batch, (g + 1) * batch, unroll=8)
         def _(p):
-            tile = column_ref[p] // COLS_DEV
-            block = column_ref[p] % COLS_DEV // BW
-            slot = count_ref[tile]
-            count_ref[tile] = slot + 1
-            at = 2 * slot
-            facts = jnp.where(lane == at, block + 1, jnp.where(lane == at + 1, width_ref[p], 0))
-            facts_ref[tile] += facts.astype(F32)
-            pltpu.make_async_copy(held_ref.at[p], out_ref.at[tile, pl.ds(slot * part, part)],
-                                  out_sem).start()
-
-    facts = pltpu.make_async_copy(facts_ref, out_ref.at[:, CAPACITY * part], facts_sem)
-    facts.start()
+            target = out_ref.at[column_ref[p] // COLS_DEV, pl.ds(slot_ref[p] * part, part)]
+            pltpu.make_async_copy(held_ref.at[p], target, out_sem).start()
+
     pltpu.make_async_copy(held_ref, out_ref.at[pl.ds(0, pieces), pl.ds(0, part)], out_sem).wait()
     facts.wait()
 
 
-def pack(piece_column, piece_width, piece_height, piece_weight, tiles, batches=8):
+def pack(piece_column, piece_width, piece_height, piece_weight, tiles, batches=4):
     pieces, rows, _ = piece_height.shape
     tall = lambda array: array.reshape(pieces, rows, 1, BW)
     return pl.pallas_call(
@@ -97,6 +101,7 @@
             pltpu.VMEM((pieces, 2 * rows, 1, BW), F32),
             pltpu.VMEM((tiles, 1, BW), F32),
             pltpu.SMEM((tiles,), jnp.int32),
+            pltpu.SMEM((pieces,), jnp.int32),
             pltpu.SemaphoreType.DMA((batches, 2)),
             pltpu.SemaphoreType.DMA,
             pltpu.SemaphoreType.DMA,
@@ -156,7 +161,7 @@
     row8 = row[:8]
     lat_even = lat % 2 == 0
 
-    @pl.loop(0, BLOCKS, unroll=4)
+    @pl.loop(0, BLOCKS, unroll=32)
     def _(i):
         cell, height = total_ref[i, 0], total_ref[i, 1]
         east = total_ref[i, 3] / (total_ref[i, 2] + DAMPING)
@@ -523,7 +528,7 @@
     return c, r
 
 
-def combine_kernel(gram_ref, q_ref, sides_ref, x_ref, r_ref):
+def combine_kernel(gram_ref, q_ref, sides_ref, x_out_ref, r_out_ref, x_ref, r_ref, sem):
     rows = q_ref.shape[2]
     terms = [(gram_ref[n:n + 8], jnp.zeros((8, BW), F32)) for n in range(0, gram_ref.shape[0], 8)]
     while len(terms) > 1:
@@ -542,7 +547,9 @@
     c, r = solved([pick(high, n) for n in count], [pick(low, n) for n in count])
     c = [jnp.broadcast_to(value, (rows, BW)) for value in c]
     r = [jnp.broadcast_to(value, (rows, BW)) for value in r]
-    for i in range(q_ref.shape[1]):
+    copies = []
+    batch = BLOCKS // sem.shape[0]
+    for i in range(BLOCKS):
         if i < 4:
             q = [sides_ref[k, i] for k in range(5)]
         elif i >= BLOCKS - 4:
@@ -552,6 +559,14 @@
         columns = slice(i * BW, (i + 1) * BW)
         x_ref[:, columns] = sum(c[k] * q[k] for k in range(4))
         r_ref[:, columns] = sum(r[k] * q[k] for k in range(5))
+        if i % batch == batch - 1:
+            done = pl.ds((i + 1 - batch) * BW, batch * BW)
+            for n, (held, out) in enumerate(((x_ref, x_out_ref), (r_ref, r_out_ref))):
+                copies.append(pltpu.make_async_copy(held.at[:, done], out.at[:, done],
+                                                    sem.at[i // batch, n]))
+                copies[-1].start()
+    for copy in copies:
+        copy.wait()
 
 
 def combine(gram, q, sides):
@@ -562,7 +577,8 @@
         combine_kernel,
         out_shape=[out, out],
         in_specs=[vmem] * 3,
-        out_specs=[vmem, vmem],
+        out_specs=[pl.BlockSpec(memory_space=pl.ANY)] * 2,
+        scratch_shapes=[pltpu.VMEM(out.shape, F32)] * 2 + [pltpu.SemaphoreType.DMA((4, 2))],
         compiler_params=pltpu.CompilerParams(vmem_limit_bytes=VMEM_BYTES),
         name="combine",
     )(gram, q, sides)

time: 162 us -> 161 us (level)
  transfers between devices with their start and end apart: 6 -> 6, of which waited for: 2 -> 2; matrix products, arithmetic and copies ran while one was open for 0% -> 0% of each run, Pallas kernels for 5% -> 4%
where the time goes in v9:
time: 161 us; the launch traced here: 160 us
  waiting for transfers between devices  96.8 us (60%)
  blocking collectives  25.9 us (16%)
  starting transfers between devices  21.9 us (14%)
  Pallas kernels  13.9 us (9%)
    all_to_all x1, waiting for transfers between devices, body(): got = lax.all_to_all(packed, 'lon', split_axis=0, concat_axis=0, tiled=True)  95.1 us
    all_to_all x1, blocking collectives, body(): lax.all_to_all(spread, ('lon', 'lat'), split_axis=0, concat_axis=0, tiled...  25.9 us
    all_to_all x1, starting transfers between devices, body(): got = lax.all_to_all(packed, 'lon', split_axis=0, concat_axis=0, tiled=True)  13.2 us
    ppermute x4, starting transfers between devices, swapped(): return lax.ppermute(block, axis, pairs + [(b, a) for a, b in pairs])  7.44 us
    pallas_call x1, Pallas kernels, gather(): pl.pallas_call(gather_kernel, out_shape=[jax.ShapeDtypeStruct(s, F32) for...  4.22 us
  transfers between devices with their start and end apart: 6, of which 2 were waited for; matrix products, arithmetic and copies ran while one was open for 0% of the time, Pallas kernels for 4%

profile of v9, /device:TPU:1, one launch (start us, length us, event | category | flops | bytes accessed | tf_op | source)
XLA Modules:
  0.0 160.3 jit_solution(18321110634035423850)
XLA Ops:
  0.6 3.2 %pack.1 = f32[64,129,1,128]{3,2,1,0:T(1,128)} custom-call(s32[64]{0:T(128)} %column_ref.1, s32[64]{0:T(128)} %width_ref.1, f32[64,32,1,128]{3,2,1,0:T(1,128)} %bitcast.21, f32[64,32,1,128]{3,2,1,0:T(1,128)} %bitcast.22), custom_call_target="tpu_custom_call" | custom-call | tf_op jit(solution)/shard_map/pack/pallas_call | solution.py:90
  3.8 13.2 %all-to-all-start = ((f32[64,129,1,128]{3,2,1,0:T(1,128)}), f32[64,129,1,128]{3,2,1,0:T(1,128)}, u32[]{:S(2)}, u32[]{:S(2)}) async-start(f32[64,129,1,128]{3,2,1,0:T(1,128)} %pack.1), calls=%async_computation | async-start | bytes 8454144 | tf_op jit(solution)/shard_map/all_to_all | solution.py:594
  17.0 95.1 %all-to-all-done.got_ref = f32[64,129,1,128]{3,2,1,0:T(1,128)} async-done(((f32[64,129,1,128]{3,2,1,0:T(1,128)}), f32[64,129,1,128]{3,2,1,0:T(1,128)}, u32[]{:S(2)}, u32[]{:S(2)}) %all-to-all-start) | async-done | bytes 4227104 | tf_op jit(solution)/shard_map/all_to_all | solution.py:594
  112.1 0.9 slice.9
  113.0 1.3 collective-permute-start
  114.3 0.1 pad_add_fusion.place_ref
  114.3 4.2 %gather.1 = (f32[32,32,128]{2,1,0:T(8,128)S(1)}, f32[32,32,128]{2,1,0:T(8,128)S(1)}, f32[32,8,128]{2,1,0:T(8,128)S(1)}, f32[32,8,128]{2,1,0:T(8,128)S(1)}, f32[6...) custom-call(s32[3]{0:T(128)S(1)} %pad_add_fusion.place_ref, ...), custom_call_target="tpu_custom_call" | custom-call | tf_op jit(solution)/shard_map/gather/pallas_call | solution.py:190
  118.6 0.0 collective-permute-done.above_ref
  118.6 0.9 finish.1
  119.5 2.2 %collective-permute-start.1 = (f32[32,8,128]{2,1,0:T(8,128)S(1)}, f32[32,8,128]{2,1,0:T(8,128)S(1)}, u32[]{:S(2)}, u32[]{:S(2)}) collective-permute-start(f32[32,8,128]{2,1,0:T(8,128)S(1)} %get-tuple-element.26.own_one_ref), channel_id=1, source_target_pairs={{0,1},{2,3},{1,0},{3,2},{4,5},{6,7},{5,4},{7,6},{8,9},{10,11},{9,8... | collective-permute-start | bytes 393224 | tf_op jit(solution)/shard_map/ppermute | solution.py:34
  121.7 0.7 collective-permute-start.2
  122.4 1.7 %collective-permute-done.1.one_ref = f32[32,8,128]{2,1,0:T(8,128)S(1)} collective-permute-done((f32[32,8,128]{2,1,0:T(8,128)S(1)}, f32[32,8,128]{2,1,0:T(8,128)S(1)}, u32[]{:S(2)}, u32[]{:S(2)}) %collective-permute-start.1) | collective-permute-done | bytes 131104 | tf_op jit(solution)/shard_map/ppermute | solution.py:34
  124.0 0.0 collective-permute-done.2.two_ref
  124.1 4.6 %collective-permute-start.4 = (f32[88,128]{1,0:T(8,128)S(1)}, f32[88,128]{1,0:T(8,128)S(1)}, u32[]{:S(2)}, u32[]{:S(2)}) collective-permute-start(f32[88,128]{1,0:T(8,128)S(1)} %pad_maximum_fusion.1), channel_id=1, source_target_pairs={{4,8},{12,16},{20,24},{28,32},{36,40},{44,48},{52,56},{60,64},{68,... | collective-permute-start | bytes 135176 | tf_op jit(solution)/shard_map/ppermute | solution.py:34
  128.7 0.0 collective-permute-start.3
  128.7 2.5 %inner.1 = (f32[5,32,32,128]{3,2,1,0:T(8,128)S(1)}, f32[14,8,128]{2,1,0:T(8,128)S(1)}, f32[2,5,6,48,128]{4,3,2,1,0:T(8,128)S(1)}) custom-call(s32[3]{0:T(128)S(1)} %pad_add_fusion.place_ref, f32[32,32,128]{2,1,0:T(8,128)S(1)} %get-tuple-element.18.rhs_ref, f32[32,32,128]{2,1,0:T(8,128)S(1)} %get-tuple-element.19.diag_ref, ...), custom_call_target="tpu_custom_call" | custom-call | tf_op jit(solution)/shard_map/inner/pallas_call | solution.py:385
  131.2 0.0 collective-permute-done.4.lon_two_ref
  131.2 0.0 collective-permute-done.3.lon_one_ref
  131.2 1.6 %outer.1 = (f32[5,8,32,128]{3,2,1,0:T(8,128)S(1)}, f32[1,128]{1,0:T(1,128)S(1)}) custom-call(s32[3]{0:T(128)S(1)} %pad_add_fusion.place_ref, f32[14,8,128]{2,1,0:T(8,128)S(1)} %get-tuple-element.28.totals_ref, f32[2,5,6,48,128]{4,3,2,1,0:T(8,128)S(1)} %get-tuple-element.29.sides_ref, f32[88,128]{1,0:T(8,128)S(1)} %collective-permute-done.3.lon_one_ref, ...), custom_call_target="tpu_custom_call" | custom-call | tf_op jit(solution)/shard_map/outer/pallas_call | solution.py:454
  132.8 0.1 broadcast_in_dim.9
  132.9 25.9 %all_to_all.10 = f32[256,1,128]{2,1,0:T(1,128)S(1)} all-to-all(f32[256,1,128]{2,1,0:T(1,128)S(1)} %broadcast_in_dim.9), channel_id=1, replica_groups=mesh['lon'=64,'lat'=4] {'lon','lat'}, dimensions={0} | all-to-all | bytes 262144 | tf_op jit(solution)/shard_map/all_to_all | solution.py:611
  158.8 1.5 combine.1
  (5 shorter events, 0.0 us)
Async XLA Ops:
  3.8 108.3 %all-to-all-start = ((f32[64,129,1,128]{3,2,1,0:T(1,128)}), f32[64,129,1,128]{3,2,1,0:T(1,128)}, u32[]{:S(2)}, u32[]{:S(2)}) async-start(f32[64,129,1,128]{3,2,1,0:T(1,128)} %pack.1), calls=%async_computation | async-start | bytes 8454144 | tf_op jit(solution)/shard_map/all_to_all | solution.py:594
  113.0 5.6 %collective-permute-start = (f32[64,2,1,128]{3,2,1,0:T(1,128)S(1)}, f32[64,2,1,128]{3,2,1,0:T(1,128)S(1)}, u32[]{:S(2)}, u32[]{:S(2)}) collective-permute-start(f32[64,2,1,128]{3,2,1,0:T(1,128)S(1)} %slice.9), channel_id=1, source_target_pairs={{1,0},{2,1},{3,2},{5,4},{6,5},{7,6},{9,8},{10,9},{11,10},{13,12},{... | collective-permute-start | bytes 196616 | tf_op jit(solution)/shard_map/ppermute | solution.py:27
  119.5 4.5 %collective-permute-start.1 = (f32[32,8,128]{2,1,0:T(8,128)S(1)}, f32[32,8,128]{2,1,0:T(8,128)S(1)}, u32[]{:S(2)}, u32[]{:S(2)}) collective-permute-start(f32[32,8,128]{2,1,0:T(8,128)S(1)} %get-tuple-element.26.own_one_ref), channel_id=1, source_target_pairs={{0,1},{2,3},{1,0},{3,2},{4,5},{6,7},{5,4},{7,6},{8,9},{10,11},{9,8... | collective-permute-start | bytes 393224 | tf_op jit(solution)/shard_map/ppermute | solution.py:34
  121.7 2.4 %collective-permute-start.2 = (f32[32,8,128]{2,1,0:T(8,128)S(1)}, f32[32,8,128]{2,1,0:T(8,128)S(1)}, u32[]{:S(2)}, u32[]{:S(2)}) collective-permute-start(f32[32,8,128]{2,1,0:T(8,128)S(1)} %get-tuple-element.27.own_two_ref), channel_id=1, source_target_pairs={{1,2},{2,1},{5,6},{6,5},{9,10},{10,9},{13,14},{14,13},{17,18},{18,... | collective-permute-start | bytes 393224 | tf_op jit(solution)/shard_map/ppermute | solution.py:34
  124.1 7.1 %collective-permute-start.4 = (f32[88,128]{1,0:T(8,128)S(1)}, f32[88,128]{1,0:T(8,128)S(1)}, u32[]{:S(2)}, u32[]{:S(2)}) collective-permute-start(f32[88,128]{1,0:T(8,128)S(1)} %pad_maximum_fusion.1), channel_id=1, source_target_pairs={{4,8},{12,16},{20,24},{28,32},{36,40},{44,48},{52,56},{60,64},{68,... | collective-permute-start | bytes 135176 | tf_op jit(solution)/shard_map/ppermute | solution.py:34
  128.7 2.5 %collective-permute-start.3 = (f32[88,128]{1,0:T(8,128)S(1)}, f32[88,128]{1,0:T(8,128)S(1)}, u32[]{:S(2)}, u32[]{:S(2)}) collective-permute-start(f32[88,128]{1,0:T(8,128)S(1)} %pad_maximum_fusion), channel_id=1, source_target_pairs={{0,4},{8,12},{16,20},{24,28},{32,36},{40,44},{48,52},{56,60},{64,6... | collective-permute-start | bytes 135176 | tf_op jit(solution)/shard_map/ppermute | solution.py:34

commit v10 on v9

--- a/solution.py
+++ b/solution.py
@@ -180,7 +180,7 @@
         inverse_ref[i] = 1.0 / (cell[rows - 8:] + DAMPING)
 
 
-def gather(place, got, rows, chunks=2):
+def gather(place, got, rows, chunks=4):
     tiles, message, _, _ = got.shape
     height = tiles * message // chunks
     field = (BLOCKS, rows, BW)
@@ -608,7 +608,7 @@
     q, totals, near = inner(place, rhs, diag, gain, own_one, own_two, one, two)
     sides, gram = outer(place, totals, near, *strips)
     spread = jnp.broadcast_to(gram[None], (lon_count * lat_count, 1, BW))
-    grams = lax.all_to_all(spread, ("lon", "lat"), split_axis=0, concat_axis=0, tiled=True)
+    grams = lax.all_to_all(spread, ("lat", "lon"), split_axis=0, concat_axis=0, tiled=True)
     return tuple(combine(grams.reshape(lon_count * lat_count, BW), q, sides))
 
 

time: 161 us -> 161 us (level)
  no operation moved by 1% of the time
where the time goes in v10:
time: 161 us; the launch traced here: 160 us
  waiting for transfers between devices  96.8 us (60%)
  blocking collectives  26 us (16%)
  starting transfers between devices  21.8 us (14%)
  Pallas kernels  13.9 us (9%)
    all_to_all x1, waiting for transfers between devices, body(): got = lax.all_to_all(packed, 'lon', split_axis=0, concat_axis=0, tiled=True)  95.1 us
    all_to_all x1, blocking collectives, body(): lax.all_to_all(spread, ('lat', 'lon'), split_axis=0, concat_axis=0, tiled...  26 us
    all_to_all x1, starting transfers between devices, body(): got = lax.all_to_all(packed, 'lon', split_axis=0, concat_axis=0, tiled=True)  13.1 us
    ppermute x4, starting transfers between devices, swapped(): return lax.ppermute(block, axis, pairs + [(b, a) for a, b in pairs])  7.43 us
    pallas_call x1, Pallas kernels, gather(): pl.pallas_call(gather_kernel, out_shape=[jax.ShapeDtypeStruct(s, F32) for...  4.14 us
  transfers between devices with their start and end apart: 6, of which 2 were waited for; matrix products, arithmetic and copies ran while one was open for 0% of the time, Pallas kernels for 4%

profile of v10, /device:TPU:1, one launch (start us, length us, event | category | flops | bytes accessed | tf_op | source)
XLA Modules:
  0.0 160.2 jit_solution(8726387690728890631)
XLA Ops:
  0.6 3.2 %pack.1 = f32[64,129,1,128]{3,2,1,0:T(1,128)} custom-call(s32[64]{0:T(128)} %column_ref.1, s32[64]{0:T(128)} %width_ref.1, f32[64,32,1,128]{3,2,1,0:T(1,128)} %bitcast.21, f32[64,32,1,128]{3,2,1,0:T(1,128)} %bitcast.22), custom_call_target="tpu_custom_call" | custom-call | tf_op jit(solution)/shard_map/pack/pallas_call | solution.py:90
  3.8 13.1 %all-to-all-start = ((f32[64,129,1,128]{3,2,1,0:T(1,128)}), f32[64,129,1,128]{3,2,1,0:T(1,128)}, u32[]{:S(2)}, u32[]{:S(2)}) async-start(f32[64,129,1,128]{3,2,1,0:T(1,128)} %pack.1), calls=%async_computation | async-start | bytes 8454144 | tf_op jit(solution)/shard_map/all_to_all | solution.py:594
  17.0 95.1 %all-to-all-done.got_ref = f32[64,129,1,128]{3,2,1,0:T(1,128)} async-done(((f32[64,129,1,128]{3,2,1,0:T(1,128)}), f32[64,129,1,128]{3,2,1,0:T(1,128)}, u32[]{:S(2)}, u32[]{:S(2)}) %all-to-all-start) | async-done | bytes 4227104 | tf_op jit(solution)/shard_map/all_to_all | solution.py:594
  112.1 0.9 slice.9
  112.9 1.3 collective-permute-start
  114.2 0.1 pad_add_fusion.place_ref
  114.3 4.1 %gather.1 = (f32[32,32,128]{2,1,0:T(8,128)S(1)}, f32[32,32,128]{2,1,0:T(8,128)S(1)}, f32[32,8,128]{2,1,0:T(8,128)S(1)}, f32[32,8,128]{2,1,0:T(8,128)S(1)}, f32[6...) custom-call(s32[3]{0:T(128)S(1)} %pad_add_fusion.place_ref, ...), custom_call_target="tpu_custom_call" | custom-call | tf_op jit(solution)/shard_map/gather/pallas_call | solution.py:190
  118.5 0.0 collective-permute-done.above_ref
  118.5 0.9 finish.1
  119.4 2.2 %collective-permute-start.1 = (f32[32,8,128]{2,1,0:T(8,128)S(1)}, f32[32,8,128]{2,1,0:T(8,128)S(1)}, u32[]{:S(2)}, u32[]{:S(2)}) collective-permute-start(f32[32,8,128]{2,1,0:T(8,128)S(1)} %get-tuple-element.26.own_one_ref), channel_id=1, source_target_pairs={{0,1},{2,3},{1,0},{3,2},{4,5},{6,7},{5,4},{7,6},{8,9},{10,11},{9,8... | collective-permute-start | bytes 393224 | tf_op jit(solution)/shard_map/ppermute | solution.py:34
  121.6 0.7 collective-permute-start.2
  122.2 1.7 %collective-permute-done.1.one_ref = f32[32,8,128]{2,1,0:T(8,128)S(1)} collective-permute-done((f32[32,8,128]{2,1,0:T(8,128)S(1)}, f32[32,8,128]{2,1,0:T(8,128)S(1)}, u32[]{:S(2)}, u32[]{:S(2)}) %collective-permute-start.1) | collective-permute-done | bytes 131104 | tf_op jit(solution)/shard_map/ppermute | solution.py:34
  123.9 0.0 collective-permute-done.2.two_ref
  123.9 4.6 %collective-permute-start.4 = (f32[88,128]{1,0:T(8,128)S(1)}, f32[88,128]{1,0:T(8,128)S(1)}, u32[]{:S(2)}, u32[]{:S(2)}) collective-permute-start(f32[88,128]{1,0:T(8,128)S(1)} %pad_maximum_fusion.1), channel_id=1, source_target_pairs={{4,8},{12,16},{20,24},{28,32},{36,40},{44,48},{52,56},{60,64},{68,... | collective-permute-start | bytes 135176 | tf_op jit(solution)/shard_map/ppermute | solution.py:34
  128.5 0.0 collective-permute-start.3
  128.5 2.5 %inner.1 = (f32[5,32,32,128]{3,2,1,0:T(8,128)S(1)}, f32[14,8,128]{2,1,0:T(8,128)S(1)}, f32[2,5,6,48,128]{4,3,2,1,0:T(8,128)S(1)}) custom-call(s32[3]{0:T(128)S(1)} %pad_add_fusion.place_ref, f32[32,32,128]{2,1,0:T(8,128)S(1)} %get-tuple-element.18.rhs_ref, f32[32,32,128]{2,1,0:T(8,128)S(1)} %get-tuple-element.19.diag_ref, ...), custom_call_target="tpu_custom_call" | custom-call | tf_op jit(solution)/shard_map/inner/pallas_call | solution.py:385
  131.1 0.0 collective-permute-done.4.lon_two_ref
  131.1 0.0 collective-permute-done.3.lon_one_ref
  131.1 1.6 %outer.1 = (f32[5,8,32,128]{3,2,1,0:T(8,128)S(1)}, f32[1,128]{1,0:T(1,128)S(1)}) custom-call(s32[3]{0:T(128)S(1)} %pad_add_fusion.place_ref, f32[14,8,128]{2,1,0:T(8,128)S(1)} %get-tuple-element.28.totals_ref, f32[2,5,6,48,128]{4,3,2,1,0:T(8,128)S(1)} %get-tuple-element.29.sides_ref, f32[88,128]{1,0:T(8,128)S(1)} %collective-permute-done.3.lon_one_ref, ...), custom_call_target="tpu_custom_call" | custom-call | tf_op jit(solution)/shard_map/outer/pallas_call | solution.py:454
  132.7 0.1 broadcast_in_dim.9
  132.8 26.0 %all_to_all.10 = f32[256,1,128]{2,1,0:T(1,128)S(1)} all-to-all(f32[256,1,128]{2,1,0:T(1,128)S(1)} %broadcast_in_dim.9), channel_id=1, replica_groups=mesh['lon'=64,'lat'=4] {'lat','lon'}, dimensions={0} | all-to-all | bytes 262144 | tf_op jit(solution)/shard_map/all_to_all | solution.py:611
  158.8 1.5 combine.1
  (5 shorter events, 0.0 us)
Async XLA Ops:
  3.8 108.2 %all-to-all-start = ((f32[64,129,1,128]{3,2,1,0:T(1,128)}), f32[64,129,1,128]{3,2,1,0:T(1,128)}, u32[]{:S(2)}, u32[]{:S(2)}) async-start(f32[64,129,1,128]{3,2,1,0:T(1,128)} %pack.1), calls=%async_computation | async-start | bytes 8454144 | tf_op jit(solution)/shard_map/all_to_all | solution.py:594
  112.9 5.5 %collective-permute-start = (f32[64,2,1,128]{3,2,1,0:T(1,128)S(1)}, f32[64,2,1,128]{3,2,1,0:T(1,128)S(1)}, u32[]{:S(2)}, u32[]{:S(2)}) collective-permute-start(f32[64,2,1,128]{3,2,1,0:T(1,128)S(1)} %slice.9), channel_id=1, source_target_pairs={{1,0},{2,1},{3,2},{5,4},{6,5},{7,6},{9,8},{10,9},{11,10},{13,12},{... | collective-permute-start | bytes 196616 | tf_op jit(solution)/shard_map/ppermute | solution.py:27
  119.4 4.5 %collective-permute-start.1 = (f32[32,8,128]{2,1,0:T(8,128)S(1)}, f32[32,8,128]{2,1,0:T(8,128)S(1)}, u32[]{:S(2)}, u32[]{:S(2)}) collective-permute-start(f32[32,8,128]{2,1,0:T(8,128)S(1)} %get-tuple-element.26.own_one_ref), channel_id=1, source_target_pairs={{0,1},{2,3},{1,0},{3,2},{4,5},{6,7},{5,4},{7,6},{8,9},{10,11},{9,8... | collective-permute-start | bytes 393224 | tf_op jit(solution)/shard_map/ppermute | solution.py:34
  121.6 2.4 %collective-permute-start.2 = (f32[32,8,128]{2,1,0:T(8,128)S(1)}, f32[32,8,128]{2,1,0:T(8,128)S(1)}, u32[]{:S(2)}, u32[]{:S(2)}) collective-permute-start(f32[32,8,128]{2,1,0:T(8,128)S(1)} %get-tuple-element.27.own_two_ref), channel_id=1, source_target_pairs={{1,2},{2,1},{5,6},{6,5},{9,10},{10,9},{13,14},{14,13},{17,18},{18,... | collective-permute-start | bytes 393224 | tf_op jit(solution)/shard_map/ppermute | solution.py:34
  123.9 7.1 %collective-permute-start.4 = (f32[88,128]{1,0:T(8,128)S(1)}, f32[88,128]{1,0:T(8,128)S(1)}, u32[]{:S(2)}, u32[]{:S(2)}) collective-permute-start(f32[88,128]{1,0:T(8,128)S(1)} %pad_maximum_fusion.1), channel_id=1, source_target_pairs={{4,8},{12,16},{20,24},{28,32},{36,40},{44,48},{52,56},{60,64},{68,... | collective-permute-start | bytes 135176 | tf_op jit(solution)/shard_map/ppermute | solution.py:34
  128.5 2.5 %collective-permute-start.3 = (f32[88,128]{1,0:T(8,128)S(1)}, f32[88,128]{1,0:T(8,128)S(1)}, u32[]{:S(2)}, u32[]{:S(2)}) collective-permute-start(f32[88,128]{1,0:T(8,128)S(1)} %pad_maximum_fusion), channel_id=1, source_target_pairs={{0,4},{8,12},{16,20},{24,28},{32,36},{40,44},{48,52},{56,60},{64,6... | collective-permute-start | bytes 135176 | tf_op jit(solution)/shard_map/ppermute | solution.py:34

commit v11 on v9

--- a/solution.py
+++ b/solution.py
@@ -444,10 +444,11 @@
             shift //= 2
         gram = jnp.where(lane_of == row_of + start, high, gram)
         gram = jnp.where(lane_of == row_of + start + LOW, low, gram)
-    gram_ref[...] = jnp.sum(gram, axis=0, keepdims=True)
-
-
-def outer(place, totals, sides, one, two):
+    row = jnp.sum(gram, axis=0, keepdims=True)
+    gram_ref[...] = jnp.broadcast_to(row[None], gram_ref.shape)
+
+
+def outer(place, totals, sides, one, two, devices):
     tall = sides.shape[3]
     rows = tall - 16
     vmem = pl.BlockSpec(memory_space=pltpu.VMEM)
@@ -455,7 +456,7 @@
         outer_kernel,
         out_shape=[
             jax.ShapeDtypeStruct((5, 8, rows, BW), F32),
-            jax.ShapeDtypeStruct((1, BW), F32),
+            jax.ShapeDtypeStruct((devices, 1, BW), F32),
         ],
         in_specs=[pl.BlockSpec(memory_space=pltpu.SMEM)] + [vmem] * 4,
         out_specs=[vmem, vmem],
@@ -606,8 +607,7 @@
         message = jnp.concatenate([edge[start], pick(one), pick(two)], axis=0)
         strips.append(swapped(message, "lon", start, True))
     q, totals, near = inner(place, rhs, diag, gain, own_one, own_two, one, two)
-    sides, gram = outer(place, totals, near, *strips)
-    spread = jnp.broadcast_to(gram[None], (lon_count * lat_count, 1, BW))
+    sides, spread = outer(place, totals, near, *strips, lon_count * lat_count)
     grams = lax.all_to_all(spread, ("lon", "lat"), split_axis=0, concat_axis=0, tiled=True)
     return tuple(combine(grams.reshape(lon_count * lat_count, BW), q, sides))
 

time: 161 us -> 161 us (level)
  no operation moved by 1% of the time
where the time goes in v11:
time: 161 us; the launch traced here: 160 us
  waiting for transfers between devices  96.8 us (60%)
  blocking collectives  25.9 us (16%)
  starting transfers between devices  21.9 us (14%)
  Pallas kernels  14 us (9%)
    all_to_all x1, waiting for transfers between devices, body(): got = lax.all_to_all(packed, 'lon', split_axis=0, concat_axis=0, tiled=True)  95.1 us
    all_to_all x1, blocking collectives, body(): lax.all_to_all(spread, ('lon', 'lat'), split_axis=0, concat_axis=0, tiled...  25.9 us
    all_to_all x1, starting transfers between devices, body(): got = lax.all_to_all(packed, 'lon', split_axis=0, concat_axis=0, tiled=True)  13.2 us
    ppermute x4, starting transfers between devices, swapped(): return lax.ppermute(block, axis, pairs + [(b, a) for a, b in pairs])  7.44 us
    pallas_call x1, Pallas kernels, gather(): pl.pallas_call(gather_kernel, out_shape=[jax.ShapeDtypeStruct(s, F32) for...  4.22 us
    pallas_call x1, Pallas kernels, pack(): pl.pallas_call(pack_kernel, out_shape=jax.ShapeDtypeStruct((tiles, CAPACI...  3.23 us
  transfers between devices with their start and end apart: 6, of which 2 were waited for; matrix products, arithmetic and copies ran while one was open for 0% of the time, Pallas kernels for 4%

profile of v11, /device:TPU:1, one launch (start us, length us, event | category | flops | bytes accessed | tf_op | source)
XLA Modules:
  0.0 160.3 jit_solution(11183851092003118585)
XLA Ops:
  0.6 3.2 %pack.1 = f32[64,129,1,128]{3,2,1,0:T(1,128)} custom-call(s32[64]{0:T(128)} %column_ref.1, s32[64]{0:T(128)} %width_ref.1, f32[64,32,1,128]{3,2,1,0:T(1,128)} %bitcast.19, f32[64,32,1,128]{3,2,1,0:T(1,128)} %bitcast.20), custom_call_target="tpu_custom_call" | custom-call | tf_op jit(solution)/shard_map/pack/pallas_call | solution.py:90
  3.9 13.2 %all-to-all-start = ((f32[64,129,1,128]{3,2,1,0:T(1,128)}), f32[64,129,1,128]{3,2,1,0:T(1,128)}, u32[]{:S(2)}, u32[]{:S(2)}) async-start(f32[64,129,1,128]{3,2,1,0:T(1,128)} %pack.1), calls=%async_computation | async-start | bytes 8454144 | tf_op jit(solution)/shard_map/all_to_all | solution.py:595
  17.1 95.1 %all-to-all-done.got_ref = f32[64,129,1,128]{3,2,1,0:T(1,128)} async-done(((f32[64,129,1,128]{3,2,1,0:T(1,128)}), f32[64,129,1,128]{3,2,1,0:T(1,128)}, u32[]{:S(2)}, u32[]{:S(2)}) %all-to-all-start) | async-done | bytes 4227104 | tf_op jit(solution)/shard_map/all_to_all | solution.py:595
  112.2 0.9 slice.9
  113.0 1.3 collective-permute-start
  114.3 0.1 pad_add_fusion.place_ref
  114.4 4.2 %gather.1 = (f32[32,32,128]{2,1,0:T(8,128)S(1)}, f32[32,32,128]{2,1,0:T(8,128)S(1)}, f32[32,8,128]{2,1,0:T(8,128)S(1)}, f32[32,8,128]{2,1,0:T(8,128)S(1)}, f32[6...) custom-call(s32[3]{0:T(128)S(1)} %pad_add_fusion.place_ref, ...), custom_call_target="tpu_custom_call" | custom-call | tf_op jit(solution)/shard_map/gather/pallas_call | solution.py:190
  118.6 0.0 collective-permute-done.above_ref
  118.7 0.9 finish.1
  119.6 2.2 %collective-permute-start.1 = (f32[32,8,128]{2,1,0:T(8,128)S(1)}, f32[32,8,128]{2,1,0:T(8,128)S(1)}, u32[]{:S(2)}, u32[]{:S(2)}) collective-permute-start(f32[32,8,128]{2,1,0:T(8,128)S(1)} %get-tuple-element.26.own_one_ref), channel_id=1, source_target_pairs={{0,1},{2,3},{1,0},{3,2},{4,5},{6,7},{5,4},{7,6},{8,9},{10,11},{9,8... | collective-permute-start | bytes 393224 | tf_op jit(solution)/shard_map/ppermute | solution.py:34
  121.7 0.7 collective-permute-start.2
  122.4 1.7 %collective-permute-done.1.one_ref = f32[32,8,128]{2,1,0:T(8,128)S(1)} collective-permute-done((f32[32,8,128]{2,1,0:T(8,128)S(1)}, f32[32,8,128]{2,1,0:T(8,128)S(1)}, u32[]{:S(2)}, u32[]{:S(2)}) %collective-permute-start.1) | collective-permute-done | bytes 131104 | tf_op jit(solution)/shard_map/ppermute | solution.py:34
  124.1 0.0 collective-permute-done.2.two_ref
  124.1 4.6 %collective-permute-start.4 = (f32[88,128]{1,0:T(8,128)S(1)}, f32[88,128]{1,0:T(8,128)S(1)}, u32[]{:S(2)}, u32[]{:S(2)}) collective-permute-start(f32[88,128]{1,0:T(8,128)S(1)} %pad_maximum_fusion.1), channel_id=1, source_target_pairs={{4,8},{12,16},{20,24},{28,32},{36,40},{44,48},{52,56},{60,64},{68,... | collective-permute-start | bytes 135176 | tf_op jit(solution)/shard_map/ppermute | solution.py:34
  128.7 0.0 collective-permute-start.3
  128.7 2.5 %inner.1 = (f32[5,32,32,128]{3,2,1,0:T(8,128)S(1)}, f32[14,8,128]{2,1,0:T(8,128)S(1)}, f32[2,5,6,48,128]{4,3,2,1,0:T(8,128)S(1)}) custom-call(s32[3]{0:T(128)S(1)} %pad_add_fusion.place_ref, f32[32,32,128]{2,1,0:T(8,128)S(1)} %get-tuple-element.18.rhs_ref, f32[32,32,128]{2,1,0:T(8,128)S(1)} %get-tuple-element.19.diag_ref, ...), custom_call_target="tpu_custom_call" | custom-call | tf_op jit(solution)/shard_map/inner/pallas_call | solution.py:385
  131.3 0.0 collective-permute-done.4.lon_two_ref
  131.3 0.0 collective-permute-done.3.lon_one_ref
  131.3 1.7 %outer.1 = (f32[5,8,32,128]{3,2,1,0:T(8,128)S(1)}, f32[256,1,128]{2,1,0:T(1,128)S(1)}) custom-call(s32[3]{0:T(128)S(1)} %pad_add_fusion.place_ref, f32[14,8,128]{2,1,0:T(8,128)S(1)} %get-tuple-element.28.totals_ref, f32[2,5,6,48,128]{4,3,2,1,0:T(8,128)S(1)} %get-tuple-element.29.sides_ref, f32[88,128]{1,0:T(8,128)S(1)} %collective-permute-done.3.lon_one_ref, ...), custom_call_target="tpu_custom_call" | custom-call | tf_op jit(solution)/shard_map/outer/pallas_call | solution.py:455
  133.0 25.9 %all_to_all.10 = f32[256,1,128]{2,1,0:T(1,128)S(1)} all-to-all(f32[256,1,128]{2,1,0:T(1,128)S(1)} %get-tuple-element.31), channel_id=1, replica_groups=mesh['lon'=64,'lat'=4] {'lon','lat'}, dimensions={0} | all-to-all | bytes 262144 | tf_op jit(solution)/shard_map/all_to_all | solution.py:611
  158.9 1.5 combine.1
  (5 shorter events, 0.0 us)
Async XLA Ops:
  3.9 108.3 %all-to-all-start = ((f32[64,129,1,128]{3,2,1,0:T(1,128)}), f32[64,129,1,128]{3,2,1,0:T(1,128)}, u32[]{:S(2)}, u32[]{:S(2)}) async-start(f32[64,129,1,128]{3,2,1,0:T(1,128)} %pack.1), calls=%async_computation | async-start | bytes 8454144 | tf_op jit(solution)/shard_map/all_to_all | solution.py:595
  113.0 5.6 %collective-permute-start = (f32[64,2,1,128]{3,2,1,0:T(1,128)S(1)}, f32[64,2,1,128]{3,2,1,0:T(1,128)S(1)}, u32[]{:S(2)}, u32[]{:S(2)}) collective-permute-start(f32[64,2,1,128]{3,2,1,0:T(1,128)S(1)} %slice.9), channel_id=1, source_target_pairs={{1,0},{2,1},{3,2},{5,4},{6,5},{7,6},{9,8},{10,9},{11,10},{13,12},{... | collective-permute-start | bytes 196616 | tf_op jit(solution)/shard_map/ppermute | solution.py:27
  119.6 4.5 %collective-permute-start.1 = (f32[32,8,128]{2,1,0:T(8,128)S(1)}, f32[32,8,128]{2,1,0:T(8,128)S(1)}, u32[]{:S(2)}, u32[]{:S(2)}) collective-permute-start(f32[32,8,128]{2,1,0:T(8,128)S(1)} %get-tuple-element.26.own_one_ref), channel_id=1, source_target_pairs={{0,1},{2,3},{1,0},{3,2},{4,5},{6,7},{5,4},{7,6},{8,9},{10,11},{9,8... | collective-permute-start | bytes 393224 | tf_op jit(solution)/shard_map/ppermute | solution.py:34
  121.7 2.4 %collective-permute-start.2 = (f32[32,8,128]{2,1,0:T(8,128)S(1)}, f32[32,8,128]{2,1,0:T(8,128)S(1)}, u32[]{:S(2)}, u32[]{:S(2)}) collective-permute-start(f32[32,8,128]{2,1,0:T(8,128)S(1)} %get-tuple-element.27.own_two_ref), channel_id=1, source_target_pairs={{1,2},{2,1},{5,6},{6,5},{9,10},{10,9},{13,14},{14,13},{17,18},{18,... | collective-permute-start | bytes 393224 | tf_op jit(solution)/shard_map/ppermute | solution.py:34
  124.1 7.1 %collective-permute-start.4 = (f32[88,128]{1,0:T(8,128)S(1)}, f32[88,128]{1,0:T(8,128)S(1)}, u32[]{:S(2)}, u32[]{:S(2)}) collective-permute-start(f32[88,128]{1,0:T(8,128)S(1)} %pad_maximum_fusion.1), channel_id=1, source_target_pairs={{4,8},{12,16},{20,24},{28,32},{36,40},{44,48},{52,56},{60,64},{68,... | collective-permute-start | bytes 135176 | tf_op jit(solution)/shard_map/ppermute | solution.py:34
  128.7 2.5 %collective-permute-start.3 = (f32[88,128]{1,0:T(8,128)S(1)}, f32[88,128]{1,0:T(8,128)S(1)}, u32[]{:S(2)}, u32[]{:S(2)}) collective-permute-start(f32[88,128]{1,0:T(8,128)S(1)} %pad_maximum_fusion), channel_id=1, source_target_pairs={{0,4},{8,12},{16,20},{24,28},{32,36},{40,44},{48,52},{56,60},{64,6... | collective-permute-start | bytes 135176 | tf_op jit(solution)/shard_map/ppermute | solution.py:34

commit v12 on v11

--- a/solution.py
+++ b/solution.py
@@ -58,7 +58,7 @@
     def _(t):
         count_ref[t] = 0
 
-    @pl.loop(0, pieces, unroll=8)
+    @pl.loop(0, pieces, unroll=32)
     def _(p):
         tile = column_ref[p] // COLS_DEV
         block = column_ref[p] % COLS_DEV // BW

time: 161 us -> 161 us (level)
  no operation moved by 1% of the time
where the time goes in v12:
time: 161 us; the launch traced here: 160 us
  waiting for transfers between devices  96.8 us (60%)
  blocking collectives  25.9 us (16%)
  starting transfers between devices  21.9 us (14%)
  Pallas kernels  13.9 us (9%)
    all_to_all x1, waiting for transfers between devices, body(): got = lax.all_to_all(packed, 'lon', split_axis=0, concat_axis=0, tiled=True)  95.1 us
    all_to_all x1, blocking collectives, body(): lax.all_to_all(spread, ('lon', 'lat'), split_axis=0, concat_axis=0, tiled...  25.9 us
    all_to_all x1, starting transfers between devices, body(): got = lax.all_to_all(packed, 'lon', split_axis=0, concat_axis=0, tiled=True)  13.2 us
    ppermute x4, starting transfers between devices, swapped(): return lax.ppermute(block, axis, pairs + [(b, a) for a, b in pairs])  7.44 us
    pallas_call x1, Pallas kernels, gather(): pl.pallas_call(gather_kernel, out_shape=[jax.ShapeDtypeStruct(s, F32) for...  4.22 us
  transfers between devices with their start and end apart: 6, of which 2 were waited for; matrix products, arithmetic and copies ran while one was open for 0% of the time, Pallas kernels for 4%

profile of v12, /device:TPU:1, one launch (start us, length us, event | category | flops | bytes accessed | tf_op | source)
XLA Modules:
  0.0 160.2 jit_solution(10839832859901403407)
XLA Ops:
  0.6 3.1 %pack.1 = f32[64,129,1,128]{3,2,1,0:T(1,128)} custom-call(s32[64]{0:T(128)} %column_ref.1, s32[64]{0:T(128)} %width_ref.1, f32[64,32,1,128]{3,2,1,0:T(1,128)} %bitcast.19, f32[64,32,1,128]{3,2,1,0:T(1,128)} %bitcast.20), custom_call_target="tpu_custom_call" | custom-call | tf_op jit(solution)/shard_map/pack/pallas_call | solution.py:90
  3.8 13.2 %all-to-all-start = ((f32[64,129,1,128]{3,2,1,0:T(1,128)}), f32[64,129,1,128]{3,2,1,0:T(1,128)}, u32[]{:S(2)}, u32[]{:S(2)}) async-start(f32[64,129,1,128]{3,2,1,0:T(1,128)} %pack.1), calls=%async_computation | async-start | bytes 8454144 | tf_op jit(solution)/shard_map/all_to_all | solution.py:595
  17.0 95.1 %all-to-all-done.got_ref = f32[64,129,1,128]{3,2,1,0:T(1,128)} async-done(((f32[64,129,1,128]{3,2,1,0:T(1,128)}), f32[64,129,1,128]{3,2,1,0:T(1,128)}, u32[]{:S(2)}, u32[]{:S(2)}) %all-to-all-start) | async-done | bytes 4227104 | tf_op jit(solution)/shard_map/all_to_all | solution.py:595
  112.1 0.9 slice.9
  112.9 1.3 collective-permute-start
  114.2 0.1 pad_add_fusion.place_ref
  114.3 4.2 %gather.1 = (f32[32,32,128]{2,1,0:T(8,128)S(1)}, f32[32,32,128]{2,1,0:T(8,128)S(1)}, f32[32,8,128]{2,1,0:T(8,128)S(1)}, f32[32,8,128]{2,1,0:T(8,128)S(1)}, f32[6...) custom-call(s32[3]{0:T(128)S(1)} %pad_add_fusion.place_ref, ...), custom_call_target="tpu_custom_call" | custom-call | tf_op jit(solution)/shard_map/gather/pallas_call | solution.py:190
  118.5 0.0 collective-permute-done.above_ref
  118.5 0.9 finish.1
  119.4 2.2 %collective-permute-start.1 = (f32[32,8,128]{2,1,0:T(8,128)S(1)}, f32[32,8,128]{2,1,0:T(8,128)S(1)}, u32[]{:S(2)}, u32[]{:S(2)}) collective-permute-start(f32[32,8,128]{2,1,0:T(8,128)S(1)} %get-tuple-element.26.own_one_ref), channel_id=1, source_target_pairs={{0,1},{2,3},{1,0},{3,2},{4,5},{6,7},{5,4},{7,6},{8,9},{10,11},{9,8... | collective-permute-start | bytes 393224 | tf_op jit(solution)/shard_map/ppermute | solution.py:34
  121.6 0.7 collective-permute-start.2
  122.3 1.7 %collective-permute-done.1.one_ref = f32[32,8,128]{2,1,0:T(8,128)S(1)} collective-permute-done((f32[32,8,128]{2,1,0:T(8,128)S(1)}, f32[32,8,128]{2,1,0:T(8,128)S(1)}, u32[]{:S(2)}, u32[]{:S(2)}) %collective-permute-start.1) | collective-permute-done | bytes 131104 | tf_op jit(solution)/shard_map/ppermute | solution.py:34
  124.0 0.0 collective-permute-done.2.two_ref
  124.0 4.6 %collective-permute-start.4 = (f32[88,128]{1,0:T(8,128)S(1)}, f32[88,128]{1,0:T(8,128)S(1)}, u32[]{:S(2)}, u32[]{:S(2)}) collective-permute-start(f32[88,128]{1,0:T(8,128)S(1)} %pad_maximum_fusion.1), channel_id=1, source_target_pairs={{4,8},{12,16},{20,24},{28,32},{36,40},{44,48},{52,56},{60,64},{68,... | collective-permute-start | bytes 135176 | tf_op jit(solution)/shard_map/ppermute | solution.py:34
  128.6 0.0 collective-permute-start.3
  128.6 2.5 %inner.1 = (f32[5,32,32,128]{3,2,1,0:T(8,128)S(1)}, f32[14,8,128]{2,1,0:T(8,128)S(1)}, f32[2,5,6,48,128]{4,3,2,1,0:T(8,128)S(1)}) custom-call(s32[3]{0:T(128)S(1)} %pad_add_fusion.place_ref, f32[32,32,128]{2,1,0:T(8,128)S(1)} %get-tuple-element.18.rhs_ref, f32[32,32,128]{2,1,0:T(8,128)S(1)} %get-tuple-element.19.diag_ref, ...), custom_call_target="tpu_custom_call" | custom-call | tf_op jit(solution)/shard_map/inner/pallas_call | solution.py:385
  131.1 0.0 collective-permute-done.4.lon_two_ref
  131.1 0.0 collective-permute-done.3.lon_one_ref
  131.2 1.7 %outer.1 = (f32[5,8,32,128]{3,2,1,0:T(8,128)S(1)}, f32[256,1,128]{2,1,0:T(1,128)S(1)}) custom-call(s32[3]{0:T(128)S(1)} %pad_add_fusion.place_ref, f32[14,8,128]{2,1,0:T(8,128)S(1)} %get-tuple-element.28.totals_ref, f32[2,5,6,48,128]{4,3,2,1,0:T(8,128)S(1)} %get-tuple-element.29.sides_ref, f32[88,128]{1,0:T(8,128)S(1)} %collective-permute-done.3.lon_one_ref, ...), custom_call_target="tpu_custom_call" | custom-call | tf_op jit(solution)/shard_map/outer/pallas_call | solution.py:455
  132.9 25.9 %all_to_all.10 = f32[256,1,128]{2,1,0:T(1,128)S(1)} all-to-all(f32[256,1,128]{2,1,0:T(1,128)S(1)} %get-tuple-element.31), channel_id=1, replica_groups=mesh['lon'=64,'lat'=4] {'lon','lat'}, dimensions={0} | all-to-all | bytes 262144 | tf_op jit(solution)/shard_map/all_to_all | solution.py:611
  158.7 1.5 combine.1
  (5 shorter events, 0.0 us)
Async XLA Ops:
  3.8 108.3 %all-to-all-start = ((f32[64,129,1,128]{3,2,1,0:T(1,128)}), f32[64,129,1,128]{3,2,1,0:T(1,128)}, u32[]{:S(2)}, u32[]{:S(2)}) async-start(f32[64,129,1,128]{3,2,1,0:T(1,128)} %pack.1), calls=%async_computation | async-start | bytes 8454144 | tf_op jit(solution)/shard_map/all_to_all | solution.py:595
  112.9 5.6 %collective-permute-start = (f32[64,2,1,128]{3,2,1,0:T(1,128)S(1)}, f32[64,2,1,128]{3,2,1,0:T(1,128)S(1)}, u32[]{:S(2)}, u32[]{:S(2)}) collective-permute-start(f32[64,2,1,128]{3,2,1,0:T(1,128)S(1)} %slice.9), channel_id=1, source_target_pairs={{1,0},{2,1},{3,2},{5,4},{6,5},{7,6},{9,8},{10,9},{11,10},{13,12},{... | collective-permute-start | bytes 196616 | tf_op jit(solution)/shard_map/ppermute | solution.py:27
  119.4 4.5 %collective-permute-start.1 = (f32[32,8,128]{2,1,0:T(8,128)S(1)}, f32[32,8,128]{2,1,0:T(8,128)S(1)}, u32[]{:S(2)}, u32[]{:S(2)}) collective-permute-start(f32[32,8,128]{2,1,0:T(8,128)S(1)} %get-tuple-element.26.own_one_ref), channel_id=1, source_target_pairs={{0,1},{2,3},{1,0},{3,2},{4,5},{6,7},{5,4},{7,6},{8,9},{10,11},{9,8... | collective-permute-start | bytes 393224 | tf_op jit(solution)/shard_map/ppermute | solution.py:34
  121.6 2.4 %collective-permute-start.2 = (f32[32,8,128]{2,1,0:T(8,128)S(1)}, f32[32,8,128]{2,1,0:T(8,128)S(1)}, u32[]{:S(2)}, u32[]{:S(2)}) collective-permute-start(f32[32,8,128]{2,1,0:T(8,128)S(1)} %get-tuple-element.27.own_two_ref), channel_id=1, source_target_pairs={{1,2},{2,1},{5,6},{6,5},{9,10},{10,9},{13,14},{14,13},{17,18},{18,... | collective-permute-start | bytes 393224 | tf_op jit(solution)/shard_map/ppermute | solution.py:34
  124.0 7.1 %collective-permute-start.4 = (f32[88,128]{1,0:T(8,128)S(1)}, f32[88,128]{1,0:T(8,128)S(1)}, u32[]{:S(2)}, u32[]{:S(2)}) collective-permute-start(f32[88,128]{1,0:T(8,128)S(1)} %pad_maximum_fusion.1), channel_id=1, source_target_pairs={{4,8},{12,16},{20,24},{28,32},{36,40},{44,48},{52,56},{60,64},{68,... | collective-permute-start | bytes 135176 | tf_op jit(solution)/shard_map/ppermute | solution.py:34
  128.6 2.5 %collective-permute-start.3 = (f32[88,128]{1,0:T(8,128)S(1)}, f32[88,128]{1,0:T(8,128)S(1)}, u32[]{:S(2)}, u32[]{:S(2)}) collective-permute-start(f32[88,128]{1,0:T(8,128)S(1)} %pad_maximum_fusion), channel_id=1, source_target_pairs={{0,4},{8,12},{16,20},{24,28},{32,36},{40,44},{48,52},{56,60},{64,6... | collective-permute-start | bytes 135176 | tf_op jit(solution)/shard_map/ppermute | solution.py:34
